TPU v7x, 256 devices: a whole 4x4x8 slice. The times are simulated.
256 devices in a mesh: seq: 32 (over y, z_hi, core), head: 8 (over z_lo, x).
Axes of the slice: x: 4, y: 4, z: 8 (z_hi: 4, z_lo: 2; z = z_hi * 2 + z_lo), core: 2. Of those that a mesh axis runs over, the one named last changes fastest.
Arguments:
- q_img: bfloat16 [2, 6144, 3072], P(None, ('seq', 'head')), may hold values from -140 to 140
- k_img: bfloat16 [2, 6144, 3072], P(None, ('seq', 'head')), may hold values from -6 to 6
- v_img: bfloat16 [2, 6144, 3072], P(None, ('seq', 'head')), may hold values from -6 to 6
- k_txt: bfloat16 [2, 512, 3072], P(None, 'seq', 'head'), may hold values from -8 to 8
- v_txt: bfloat16 [2, 512, 3072], P(None, 'seq', 'head'), may hold values from -6 to 6
- replace_cols: int32 [8], replicated, may hold values from 0 to 511
- shared_flags: int32 [512], replicated, may hold values 0 or 1
Outputs:
- attended: bfloat16 [2, 6144, 3072], P(None, ('seq', 'head'))
All inputs are finite; a program needn't handle non-finite values.
Results may differ from a plain program's by a relative error of at most 0.0095.
Values may be sent and summed in bfloat16 or wider, within the bound.
No kernel may reach another device: no remote copies, remote signals or barrier semaphores. Data moves between devices by JAX's collectives and lax.ppermute only.
A program may use at most 128 MiB of HBM per device.

v0:
```python
import math

import jax
import jax.numpy as jnp
from jax import lax
from jax.sharding import PartitionSpec as P

H = 24
HD = 128


def absorb(state_carry, pieces, query_heads, heads_dev, score_scale):
    row_top, totals, partial_value = state_carry
    piece_keys, piece_values = pieces
    piece_rows = piece_keys.shape[1]
    key_heads = piece_keys.reshape(2, piece_rows, heads_dev, HD)
    value_heads = piece_values.reshape(2, piece_rows, heads_dev, HD)
    logit_scores = (
        jnp.einsum("bqhd,bkhd->bhqk", query_heads, key_heads, preferred_element_type=jnp.float32)
        * score_scale
    )
    new_top = jnp.max(logit_scores, axis=-1)
    factor = jnp.exp(row_top - new_top)
    weights = jnp.exp(logit_scores - new_top[..., None])
    totals = totals * factor + jnp.sum(weights, axis=-1)
    partial_value = partial_value * factor[..., None] + jnp.einsum(
        "bhqk,bkhd->bhqd",
        weights.astype(jnp.bfloat16),
        value_heads,
        preferred_element_type=jnp.float32,
    )
    return (new_top, totals, partial_value)


def finish(
    row_top,
    totals,
    partial_value,
    query_heads,
    txt_key_heads,
    txt_value_heads,
    edit_mask,
    score_scale,
):
    logit_scores = (
        jnp.einsum(
            "bqhd,bkhd->bhqk", query_heads, txt_key_heads, preferred_element_type=jnp.float32
        )
        * score_scale
    )
    overall = jnp.maximum(row_top, jnp.max(logit_scores, axis=-1))
    factor = jnp.exp(row_top - overall)
    weights = jnp.exp(logit_scores - overall[..., None])
    whole_totals = totals * factor + jnp.sum(weights, axis=-1)
    keep_rows = jnp.stack([jnp.ones_like(edit_mask), 1.0 - edit_mask])
    kept_weights = (weights * keep_rows[:, None, None, :]).astype(jnp.bfloat16)
    weighted_numerator = partial_value * factor[..., None] + jnp.einsum(
        "bhqk,bkhd->bhqd", kept_weights, txt_value_heads, preferred_element_type=jnp.float32
    )
    result = weighted_numerator / whole_totals[..., None]
    source_probs = weights[0] / whole_totals[0][..., None]
    borrowed = (source_probs * edit_mask).astype(jnp.bfloat16)
    borrowed_sum = jnp.einsum(
        "hqk,khd->hqd", borrowed, txt_value_heads[1], preferred_element_type=jnp.float32
    )
    return result.at[1].add(borrowed_sum)


def body(q_img, k_img, v_img, k_txt, v_txt, replace_cols, shared_flags):
    heads_dev = H // lax.axis_size("head")
    score_scale = 1.0 / math.sqrt(HD)
    queries, keys_img, values_img = (
        lax.all_to_all(q_img, "head", split_axis=2, concat_axis=1, tiled=True),
        lax.all_to_all(k_img, "head", split_axis=2, concat_axis=1, tiled=True),
        lax.all_to_all(v_img, "head", split_axis=2, concat_axis=1, tiled=True),
    )
    keys_txt, values_txt = (
        lax.all_gather(k_txt, "seq", axis=1, tiled=True),
        lax.all_gather(v_txt, "seq", axis=1, tiled=True),
    )
    group_rows = queries.shape[1]
    txt_cols = keys_txt.shape[1]
    query_heads = queries.reshape(2, group_rows, heads_dev, HD)
    txt_key_heads = keys_txt.reshape(2, txt_cols, heads_dev, HD)
    txt_value_heads = values_txt.reshape(2, txt_cols, heads_dev, HD)
    columns = jnp.arange(txt_cols, dtype=jnp.int32)
    listed = jnp.any(replace_cols[:, None] == columns[None, :], axis=0)
    edit_mask = jnp.logical_or(listed, shared_flags == 1).astype(jnp.float32)
    initial = (
        jnp.full((2, heads_dev, group_rows), -jnp.inf, jnp.float32),
        jnp.zeros((2, heads_dev, group_rows), jnp.float32),
        jnp.zeros((2, heads_dev, group_rows, HD), jnp.float32),
    )
    row_top, totals, partial_value = absorb(
        initial,
        (
            lax.all_gather(keys_img, "seq", axis=1, tiled=True),
            lax.all_gather(values_img, "seq", axis=1, tiled=True),
        ),
        query_heads,
        heads_dev,
        score_scale,
    )
    result = finish(
        row_top,
        totals,
        partial_value,
        query_heads,
        txt_key_heads,
        txt_value_heads,
        edit_mask,
        score_scale,
    )
    merged = (
        jnp.transpose(result, (0, 2, 1, 3))
        .reshape(2, group_rows, heads_dev * HD)
        .astype(jnp.bfloat16)
    )
    return lax.all_to_all(merged, "head", split_axis=1, concat_axis=2, tiled=True)


def solution(mesh):
    placed = (
        P(None, ("seq", "head"), None),
        P(None, ("seq", "head"), None),
        P(None, ("seq", "head"), None),
        P(None, "seq", "head"),
        P(None, "seq", "head"),
        P(),
        P(),
    )
    return jax.shard_map(
        body, mesh=mesh, in_specs=placed, out_specs=P(None, ("seq", "head"), None), check_vma=False
    )
```

profile of v0, /device:TPU:1, one launch (start us, length us, event | category | flops | bytes accessed | tf_op | source)
XLA Modules:
  0.0 270.4 jit_solution(5251059994385734174)
XLA Ops:
  6.5 3.4 %copy.65 = bf16[2,24,3072]{1,0,2:T(2,128)(2,1)S(1)} copy(bf16[2,24,3072]{2,1,0:T(8,128)(2,1)} %param.10) | data formatting | bytes 589824 | tf_op args[1]
  10.0 2.1 reshape.98
  12.0 12.8 %all_to_all.69 = bf16[8,2,9216]{2,1,0:T(2,128)(2,1)S(1)} all-to-all(bf16[8,2,9216]{2,1,0:T(2,128)(2,1)S(1)} %reshape.98), channel_id=1, replica_groups=mesh['seq'=32,'head'=8] {'head'}, dimensions={0} | all-to-all | bytes 589824 | tf_op jit(solution)/shard_map/all_to_all | solution.py:74
  24.8 2.2 reshape.99
  27.0 2.6 copy.95
  29.7 1.9 copy.71
  31.6 2.1 reshape.96
  33.7 9.7 %all_to_all.70 = bf16[8,2,9216]{2,1,0:T(2,128)(2,1)S(1)} all-to-all(bf16[8,2,9216]{2,1,0:T(2,128)(2,1)S(1)} %reshape.96), channel_id=1, replica_groups=mesh['seq'=32,'head'=8] {'head'}, dimensions={0} | all-to-all | bytes 589824 | tf_op jit(solution)/shard_map/all_to_all | solution.py:75
  43.4 2.2 reshape.97
  45.6 2.5 copy.97
  48.2 1.9 copy.63
  50.1 2.8 %reshape.100 = bf16[8,2,9216]{2,1,0:T(2,128)(2,1)} reshape(bf16[3072,2,24]{2,1,0:T(2,128)(2,1)S(1)} %bitcast.64) | data formatting | bytes 589824
  52.9 3.4 %all-to-all-start = ((bf16[8,2,9216]{2,1,0:T(2,128)(2,1)}), bf16[8,2,9216]{2,1,0:T(2,128)(2,1)S(1)}, u32[]{:S(2)}, u32[]{:S(2)}) async-start(bf16[8,2,9216]{2,1,0:T(2,128)(2,1)} %reshape.100), calls=%async_computation | async-start | bytes 589824 | tf_op jit(solution)/shard_map/all_to_all | solution.py:73
  56.4 60.8 %all_gather.14 = bf16[2,512,384]{2,0,1:T(2,128)(2,1)S(1)} all-gather(bf16[2,16,384]{2,0,1:T(2,128)(2,1)S(1)} %copy.76), channel_id=1, replica_groups=mesh['seq'=32,'head'=8] {'seq'}, dimensions={1}, use_global_device_ids=true | all-gather | bytes 811008 | tf_op jit(solution)/shard_map/all_gather | solution.py:78
  117.2 44.0 %all_gather.15 = bf16[2,512,384]{2,0,1:T(2,128)(2,1)S(1)} all-gather(bf16[2,16,384]{2,0,1:T(2,128)(2,1)S(1)} %copy.80), channel_id=1, replica_groups=mesh['seq'=32,'head'=8] {'seq'}, dimensions={1}, use_global_device_ids=true | all-gather | bytes 811008 | tf_op jit(solution)/shard_map/all_gather | solution.py:79
  161.2 1.1 copy.77
  162.3 1.1 copy.81
  163.4 0.8 slice.44
  164.4 2.2 reshape.101
  166.6 1.1 copy.64
  167.8 1.8 multiply_reduce_fusion.1
  169.6 12.7 %copy.68 = bf16[2,6144,384]{1,2,0:T(8,128)(2,1)} copy(bf16[2,6144,384]{2,1,0:T(8,128)(2,1)} %all-gather.3.cloned.1.call-done) | data formatting | bytes 18874368 | tf_op jit(solution)/shard_map/all_gather | solution.py:97
  182.4 14.5 %multiply_reduce_fusion = (f32[2,3,192]{2,1,0:T(4,128)S(1)}, f32[2,3,192,6144]{3,2,1,0:T(8,128)}) fusion(bf16[2,6144,3,128]{1,3,2,0:T(8,128)(2,1)} %bitcast.58, bf16[2,192,3,128]{3,2,1,0:T(4,128)(2,1)S(1)} %reshape.89), kind=kOutput, calls=%fused_computation.1 | convolution fusion | flops 1826093952 | bytes 38048256 | tf_op jit(solution)/shard_map/bqhd,bkhd->bhqk/dot_general | solution.py:19
  196.9 0.7 fusion.27
  197.5 12.8 %fusion = f32[2,3,192]{2,1,0:T(4,128)S(1)} fusion(f32[2,3,192,6144]{3,2,1,0:T(8,128)} %get-tuple-element.25, f32[2,3,192]{2,1,0:T(4,128)S(1)} %get-tuple-element.24), kind=kLoop, calls=%fused_computation.2 | loop fusion | flops 21232512 | bytes 28320768 | tf_op jit(solution)/shard_map/reduce_sum | solution.py:25
  210.4 12.6 %copy.74 = bf16[2,6144,384]{1,2,0:T(8,128)(2,1)} copy(bf16[2,6144,384]{2,1,0:T(8,128)(2,1)} %all-gather.5.cloned.1.call-done) | data formatting | bytes 18874368 | tf_op jit(solution)/shard_map/all_gather | solution.py:98
  223.1 15.3 %fusion.10 = f32[2,3,192,128]{3,2,1,0:T(8,128)} fusion(bf16[2,6144,3,128]{1,3,2,0:T(8,128)(2,1)} %bitcast.57, f32[2,3,192,6144]{3,2,1,0:T(8,128)} %get-tuple-element.25, f32[2,3,192]{2,1,0:T(4,128)S(1)} %get-tuple-element.24, f32[2,3,192]{2,1,0:T(4,128)S(1)} %get-tuple-element.18, f32[2,3,192]{2,1,0:T(4,128)S(1)} %get-tuple-element.23), kind=kOutput, calls=%fused_computation.13 | convolution fusion | flops 1833467904 | bytes 38352384 | tf_op jit(solution)/shard_map/bhqk,bkhd->bhqd/dot_general | solution.py:26
  238.3 1.6 fusion.6
  239.9 0.4 fusion.18
  240.4 0.3 copy.98
  240.9 21.9 %all_to_all.71 = bf16[2,192,384]{2,0,1:T(2,128)(2,1)S(1)} all-to-all(bf16[2,192,384]{2,0,1:T(2,128)(2,1)S(1)} %reshape.95), channel_id=1, replica_groups=mesh['seq'=32,'head'=8] {'head'}, dimensions={1} | all-to-all | bytes 589824 | tf_op jit(solution)/shard_map/all_to_all | solution.py:119
  262.8 0.7 copy.100
  (35 shorter events, 0.7 us)
Async XLA Ops:
  6.5 163.1 %all-gather.3.cloned.1.call-start = ((), (), s32[]{:S(2)}) async-start(), calls=%async_computation.4 | async-start | bytes 9732096 | tf_op jit(solution)/shard_map/all_gather | solution.py:97
  12.0 17.7 %copy-start.2 = (bf16[2,24,3072]{2,1,0:T(8,128)(2,1)S(1)}, bf16[2,24,3072]{2,1,0:T(8,128)(2,1)}, u32[]{:S(2)}) copy-start(bf16[2,24,3072]{2,1,0:T(8,128)(2,1)} %param.11) | copy-start | bytes 884740
  29.6 180.8 %all-gather.5.cloned.1.call-start = ((), (), s32[]{:S(2)}) async-start(), calls=%async_computation.5 | async-start | bytes 9732096 | tf_op jit(solution)/shard_map/all_gather | solution.py:98
  33.7 14.5 %copy-start.3 = (bf16[2,24,3072]{2,1,0:T(8,128)(2,1)S(1)}, bf16[2,24,3072]{2,1,0:T(8,128)(2,1)}, u32[]{:S(2)}) copy-start(bf16[2,24,3072]{2,1,0:T(8,128)(2,1)} %param.9) | copy-start | bytes 884740
  48.1 8.2 %copy-start.4 = (bf16[2,16,384]{2,1,0:T(8,128)(2,1)S(1)}, bf16[2,16,384]{2,1,0:T(8,128)(2,1)}, u32[]{:S(2)}) copy-start(bf16[2,16,384]{2,1,0:T(8,128)(2,1)} %param.12) | copy-start | bytes 73732
  48.1 8.2 %copy-start.5 = (bf16[2,16,384]{2,1,0:T(8,128)(2,1)S(1)}, bf16[2,16,384]{2,1,0:T(8,128)(2,1)}, u32[]{:S(2)}) copy-start(bf16[2,16,384]{2,1,0:T(8,128)(2,1)} %param.13) | copy-start | bytes 73732
  52.9 111.5 %all-to-all-start = ((bf16[8,2,9216]{2,1,0:T(2,128)(2,1)}), bf16[8,2,9216]{2,1,0:T(2,128)(2,1)S(1)}, u32[]{:S(2)}, u32[]{:S(2)}) async-start(bf16[8,2,9216]{2,1,0:T(2,128)(2,1)} %reshape.100), calls=%async_computation | async-start | bytes 589824 | tf_op jit(solution)/shard_map/all_to_all | solution.py:73
  117.2 47.0 %copy-start.7 = (s32[8]{0:T(128)S(1)}, s32[8]{0:T(128)}, u32[]{:S(2)}) copy-start(s32[8]{0:T(128)} %param.14) | copy-start | bytes 100
  117.2 47.1 %copy-start.6 = (s32[512]{0:T(512)S(1)}, s32[512]{0:T(512)}, u32[]{:S(2)}) copy-start(s32[512]{0:T(512)} %param.15) | copy-start | bytes 6148
  182.4 14.5 %copy-start = (f32[2,3,192,512]{3,2,1,0:T(8,128)S(1)}, f32[2,3,192,512]{3,2,1,0:T(8,128)}, u32[]{:S(2)}) copy-start(f32[2,3,192,512]{3,2,1,0:T(8,128)} %get-tuple-element.27) | copy-start | bytes 7077892
  238.3 1.6 copy-start.1
Sparse Core Ops, SparseCore 0:
  29.8 89.7 all-gather.2
  122.1 87.5 all-gather.4
where the time goes:
time: 275 us; the launch traced here: 270 us
  blocking collectives  149 us (54%)
  local copies, waits for them, and re-layouts  56.8 us (21%)
  matrix products  33.6 us (12%)
  other arithmetic  13.7 us (5%)
  between operations  13.7 us (5%)
  starting transfers between devices  3.47 us (1%)
    all_gather x1, blocking collectives, body(): lax.all_gather(k_txt, 'seq', axis=1, tiled=True)  60.8 us
    all_gather x1, blocking collectives, body(): lax.all_gather(v_txt, 'seq', axis=1, tiled=True)  44 us
    all_to_all x1, blocking collectives, body(): lax.all_to_all(merged, 'head', split_axis=1, concat_axis=2, tiled=True)  21.9 us
    unnamed x27, local copies, waits for them, and re-layouts  20.9 us
    dot_general x1, matrix products, absorb(): jnp.einsum('bhqk,bkhd->bhqd', weights.astype(jnp.bfloat16), value_heads,...  15.3 us
    dot_general x1, matrix products, absorb(): jnp.einsum('bqhd,bkhd->bhqk', query_heads, key_heads, preferred_element_t...  14.5 us
    reduce_sum x1, other arithmetic, absorb(): totals = totals * factor + jnp.sum(weights, axis=-1)  12.8 us
    all_to_all x1, blocking collectives, body(): lax.all_to_all(k_img, 'head', split_axis=2, concat_axis=1, tiled=True)  12.8 us
  transfers between devices with their start and end apart: 3, of which 0 were waited for; matrix products, arithmetic and copies ran while one was open for 23% of the time, Pallas kernels for 0%

commit v1 on v0

v1 whole, which is shorter than its diff:
```python
import functools
import math

import jax
import jax.numpy as jnp
import numpy as np
from jax import lax
from jax.experimental import pallas as pl
from jax.experimental.pallas import tpu as pltpu
from jax.sharding import Mesh
from jax.sharding import PartitionSpec as P

H = 24
HD = 128
LOG2E = 1.4426950408889634
SCALE2 = LOG2E / math.sqrt(HD)
VMEM_LIMIT = 56 * 1024 * 1024

VM = pl.BlockSpec(memory_space=pltpu.VMEM)
SM = pl.BlockSpec(memory_space=pltpu.SMEM)


def params():
    return pltpu.CompilerParams(vmem_limit_bytes=VMEM_LIMIT)


def pack_kernel(groups, q_ref, k_ref, v_ref, out_ref):
    width = q_ref.shape[2] // groups
    for group in range(groups):
        for branch in range(2):
            for at, ref in enumerate((q_ref, k_ref, v_ref)):
                out_ref[2 * group + branch, :, at * width : (at + 1) * width] = ref[
                    branch, :, group * width : (group + 1) * width
                ]


def pack(q, k, v, groups):
    rows, width = q.shape[1], q.shape[2] // groups
    return pl.pallas_call(
        functools.partial(pack_kernel, groups),
        out_shape=jax.ShapeDtypeStruct((2 * groups, rows, 3 * width), q.dtype),
        in_specs=[VM] * 3,
        out_specs=VM,
        compiler_params=params(),
    )(q, k, v)


def unpack_kernel(groups, in_ref, out_ref):
    width = in_ref.shape[2]
    for group in range(groups):
        for branch in range(2):
            out_ref[branch, :, group * width : (group + 1) * width] = in_ref[2 * group + branch]


def unpack(x, groups):
    return pl.pallas_call(
        functools.partial(unpack_kernel, groups),
        out_shape=jax.ShapeDtypeStruct((2, x.shape[1], groups * x.shape[2]), x.dtype),
        in_specs=[VM],
        out_specs=VM,
        compiler_params=params(),
    )(x)


def nt(a, b):
    return lax.dot_general(a, b, (((1,), (1,)), ((), ())), preferred_element_type=jnp.float32)


def nn(a, b):
    return lax.dot_general(a, b, (((1,), (0,)), ((), ())), preferred_element_type=jnp.float32)


def image_part(q, kv_refs, head, heads):
    cols = slice(head * HD, (head + 1) * HD)
    vcols = slice((heads + head) * HD, (heads + head + 1) * HD)
    scores = [nt(q, kv[:, cols]) for kv in kv_refs]
    top = scores[0].max(axis=-1, keepdims=True)
    for s in scores[1:]:
        top = jnp.maximum(top, s.max(axis=-1, keepdims=True))
    shift = top * SCALE2
    total = None
    acc = None
    for s, kv in zip(scores, kv_refs):
        w = jnp.exp2(s * SCALE2 - shift)
        t = w.sum(axis=-1, keepdims=True)
        a = nn(w.astype(jnp.bfloat16), kv[:, vcols])
        total = t if total is None else total + t
        acc = a if acc is None else acc + a
    return shift, total, acc


def block_kernel(heads, chunk, q_ref, kv0, kv1, kv2, kv3, out_ref, lse_ref):
    kvs = (kv0, kv1, kv2, kv3)
    rows = q_ref.shape[0]
    for head in range(heads):
        cols = slice(head * HD, (head + 1) * HD)
        for r in range(0, rows, chunk):
            shift, total, acc = image_part(q_ref[r : r + chunk, cols], kvs, head, heads)
            out_ref[r : r + chunk, cols] = (acc / total).astype(jnp.bfloat16)
            lse = jnp.broadcast_to(shift + jnp.log2(total), (chunk, HD))
            lse_ref[8 * head : 8 * head + 8, r : r + chunk] = lse.T[0:8]


def block_attention(q, kvs, heads, chunk=128):
    rows = q.shape[0]
    return pl.pallas_call(
        functools.partial(block_kernel, heads, chunk),
        out_shape=(
            jax.ShapeDtypeStruct((rows, heads * HD), jnp.bfloat16),
            jax.ShapeDtypeStruct((8 * heads, rows), jnp.float32),
        ),
        in_specs=[VM] * 5,
        out_specs=(VM, VM),
        compiler_params=params(),
        cost_estimate=pl.CostEstimate(
            flops=4 * heads * rows * HD * 4 * kvs[0].shape[0],
            bytes_accessed=4 * kvs[0].size * 2 + q.size * 4,
            transcendentals=heads * rows * 4 * kvs[0].shape[0],
        ),
    )(q, *kvs)


def own_kernel(
    heads, chunk, branch_ref, cols_ref, q_ref, kv0, kv1, kv2, kv3, text_ref, flags_ref,
    acc_ref, stat_ref, borrow_ref, kt, vt, vb,
):
    kvs = (kv0, kv1, kv2, kv3)
    rows = q_ref.shape[0]
    parts, _, per, _ = text_ref.shape
    txt = parts * per
    branch = branch_ref[0]
    for i in range(parts):
        kt[i * per : (i + 1) * per] = text_ref[i, branch]
        vt[i * per : (i + 1) * per] = text_ref[i, 2 + branch]
        vb[i * per : (i + 1) * per] = text_ref[i, 3]
    columns = lax.broadcasted_iota(jnp.int32, (1, txt), 1)
    listed = flags_ref[...] == 1
    for i in range(cols_ref.shape[0]):
        listed = jnp.logical_or(listed, columns == cols_ref[i])
    mask = listed.astype(jnp.float32)
    keep = 1.0 - mask * branch.astype(jnp.float32)
    for head in range(heads):
        cols = slice(head * HD, (head + 1) * HD)
        for r in range(0, rows, chunk):
            q = q_ref[r : r + chunk, cols]
            shift, total, acc = image_part(q, kvs, head, heads)
            s = nt(q, kt[:, cols])
            txt_shift = s.max(axis=-1, keepdims=True) * SCALE2
            overall = jnp.maximum(shift, txt_shift)
            factor = jnp.exp2(shift - overall)
            w = jnp.exp2(s * SCALE2 - overall)
            total = total * factor + w.sum(axis=-1, keepdims=True)
            acc = acc * factor + nn((w * keep).astype(jnp.bfloat16), vt[:, cols])
            borrow = nn((w * mask).astype(jnp.bfloat16), vb[:, cols])
            acc_ref[r : r + chunk, cols] = acc / total
            borrow_ref[r : r + chunk, cols] = borrow / total
            stat = jnp.broadcast_to(overall + jnp.log2(total), (chunk, HD))
            stat_ref[r : r + chunk, cols] = stat


def own_attention(branch, replace_cols, q, kvs, text, flags, heads, chunk=128):
    rows = q.shape[0]
    txt = text.shape[0] * text.shape[2]
    wide = jax.ShapeDtypeStruct((rows, heads * HD), jnp.float32)
    return pl.pallas_call(
        functools.partial(own_kernel, heads, chunk),
        out_shape=(wide, wide, wide),
        in_specs=[SM, SM] + [VM] * 7,
        out_specs=(VM, VM, VM),
        scratch_shapes=[pltpu.VMEM((txt, heads * HD), jnp.bfloat16)] * 3,
        compiler_params=params(),
        cost_estimate=pl.CostEstimate(
            flops=4 * heads * rows * HD * (4 * kvs[0].shape[0] + 2 * txt),
            bytes_accessed=4 * kvs[0].size * 2 + q.size * 4,
            transcendentals=heads * rows * (4 * kvs[0].shape[0] + txt),
        ),
    )(branch, replace_cols, q, *kvs, text, flags)


def merge_kernel(heads, chunk, acc_ref, stat_ref, borrow_ref, p1, p2, p3, l1, l2, l3, out_ref, lent_ref):
    rows = acc_ref.shape[0]
    for head in range(heads):
        cols = slice(head * HD, (head + 1) * HD)
        for r in range(0, rows, chunk):
            here = slice(r, r + chunk)
            own = stat_ref[here, cols]
            others = [
                jnp.broadcast_to(l[8 * head : 8 * head + 1, here], (HD, chunk)).T for l in (l1, l2, l3)
            ]
            top = own
            for o in others:
                top = jnp.maximum(top, o)
            own_w = jnp.exp2(own - top)
            weights = [jnp.exp2(o - top) for o in others]
            inverse = 1.0 / (own_w + weights[0] + weights[1] + weights[2])
            result = acc_ref[here, cols] * own_w
            for p, w in zip((p1, p2, p3), weights):
                result += p[here, cols].astype(jnp.float32) * w
            out_ref[here, cols] = result * inverse
            lent_ref[here, cols] = (borrow_ref[here, cols] * (own_w * inverse)).astype(jnp.bfloat16)


def merge(own, parts, stats, heads, chunk=128):
    rows = own[0].shape[0]
    return pl.pallas_call(
        functools.partial(merge_kernel, heads, chunk),
        out_shape=(
            jax.ShapeDtypeStruct((rows, heads * HD), jnp.float32),
            jax.ShapeDtypeStruct((rows, heads * HD), jnp.bfloat16),
        ),
        in_specs=[VM] * 9,
        out_specs=(VM, VM),
        compiler_params=params(),
    )(*own, *parts, *stats)


def ring(n, step):
    return [(i, (i + step) % n) for i in range(n)]


def body(q_img, k_img, v_img, k_txt, v_txt, replace_cols, shared_flags):
    groups = lax.axis_size("z_lo") * lax.axis_size("x")
    n_y, n_z = lax.axis_size("y"), lax.axis_size("z_hi")
    heads = H // groups
    width = heads * HD
    text = lax.all_gather(jnp.concatenate([k_txt, v_txt], axis=0), ("y", "z_hi", "core"), axis=0, tiled=False)
    packed = pack(q_img, k_img, v_img, groups)
    held = lax.all_to_all(packed, ("z_lo", "x", "core"), split_axis=0, concat_axis=0, tiled=True)
    rows = held.shape[0] * held.shape[1]
    held = held.reshape(rows, 3 * width)
    q, kv = held[:, :width], held[:, width:]
    kvs = [kv] + [lax.ppermute(kv, "y", ring(n_y, s)) for s in range(1, n_y)]
    parts, stats = [], []
    for s in (2, 1, 3):
        far_q = lax.ppermute(q, "z_hi", ring(n_z, s))
        part, stat = block_attention(far_q, kvs, heads)
        parts.append(lax.ppermute(part, "z_hi", ring(n_z, n_z - s)))
        stats.append(lax.ppermute(stat, "z_hi", ring(n_z, n_z - s)))
    branch = lax.axis_index("core").astype(jnp.int32)
    own = own_attention(branch.reshape(1), replace_cols, q, kvs, text, shared_flags.reshape(1, -1), heads)
    result, lent = merge(own, parts, stats, heads)
    borrowed = lax.ppermute(lent, "core", [(0, 1)])
    result = (result + borrowed.astype(jnp.float32)).astype(jnp.bfloat16)
    result = result.reshape(2 * groups, rows // (2 * groups), width)
    back = lax.all_to_all(result, ("z_lo", "x", "core"), split_axis=0, concat_axis=0, tiled=True)
    return unpack(back, groups)


def solution(mesh):
    fine = Mesh(mesh.devices.reshape(4, 4, 2, 2, 4), ("y", "z_hi", "core", "z_lo", "x"))
    seq, head = ("y", "z_hi", "core"), ("z_lo", "x")
    tokens = P(None, seq + head, None)
    text = P(None, seq, head)
    return jax.shard_map(
        body,
        mesh=fine,
        in_specs=(tokens, tokens, tokens, text, text, P(), P()),
        out_specs=tokens,
        check_vma=False,
    )
```

time: 275 us -> 156 us (0.57); the launches traced: 270 us -> 156 us
  blocking collectives: 149 us -> 36.7 us
  local copies, waits for them, and re-layouts: 56.8 us -> 4.02 us
  Pallas kernels: 0 us -> 39 us
  matrix products: 33.6 us -> 0 us
  starting transfers between devices: 3.47 us -> 33.5 us
  waiting for transfers between devices: 0.06 us -> 26.5 us
  other arithmetic: 13.7 us -> 2.52 us
    all_gather x2 -> x0, blocking collectives: 105 us -> none  [the longest x1 60.8 us: body(): lax.all_gather(k_txt, 'seq', axis=1, tiled=True)]
    pallas_call x0 -> x7, Pallas kernels: none -> 39 us  [the longest x3 21.2 us: block_attention(): pl.pallas_call(functools.partial(block_kernel, heads, chunk), out_shape=(...]
    dot_general x5 -> x0, matrix products: 33.6 us -> none  [the longest x1 15.3 us: absorb(): jnp.einsum('bhqk,bkhd->bhqd', weights.astype(jnp.bfloat16), value_heads,...]
    ppermute x0 -> x13, starting transfers between devices: none -> 33.5 us  [the longest x3 10.2 us: body(): far_q = lax.ppermute(q, 'z_hi', ring(n_z, s))]
    all_gather x4 -> x0, local copies, waits for them, and re-layouts: 27.5 us -> none  [the longest x1 12.7 us: body(): lax.all_gather(keys_img, 'seq', axis=1, tiled=True)]
    ppermute x0 -> x13, waiting for transfers between devices: none -> 26.4 us  [the longest x3 11.8 us: body(): far_q = lax.ppermute(q, 'z_hi', ring(n_z, s))]
    unnamed x27 -> x32, local copies, waits for them, and re-layouts: 20.9 us -> 3.95 us
    reduce_sum x2 -> x0, other arithmetic: 13.5 us -> none  [the longest x1 12.8 us: absorb(): totals = totals * factor + jnp.sum(weights, axis=-1)]
  transfers between devices with their start and end apart: 3 -> 14, of which waited for: 0 -> 4; matrix products, arithmetic and copies ran while one was open for 23% -> 0% of each run, Pallas kernels for 0% -> 22%
where the time goes in v1:
time: 156 us
  Pallas kernels  39 us (25%)
  blocking collectives  36.7 us (24%)
  starting transfers between devices  33.5 us (21%)
  waiting for transfers between devices  26.5 us (17%)
  between operations  13.5 us (9%)
  local copies, waits for them, and re-layouts  4.02 us (3%)
  other arithmetic  2.52 us (2%)
    pallas_call x3, Pallas kernels, block_attention(): pl.pallas_call(functools.partial(block_kernel, heads, chunk), out_shape=(...  21.2 us
    all_to_all x1, blocking collectives, body(): lax.all_to_all(packed, ('z_lo', 'x', 'core'), split_axis=0, concat_axis=0...  20.8 us
    all_to_all x1, blocking collectives, body(): lax.all_to_all(result, ('z_lo', 'x', 'core'), split_axis=0, concat_axis=0...  15.9 us
    ppermute x3, waiting for transfers between devices, body(): far_q = lax.ppermute(q, 'z_hi', ring(n_z, s))  11.8 us
    pallas_call x1, Pallas kernels, own_attention(): pl.pallas_call(functools.partial(own_kernel, heads, chunk), out_shape=(wi...  10.8 us
    ppermute x3, starting transfers between devices, body(): far_q = lax.ppermute(q, 'z_hi', ring(n_z, s))  10.2 us
    ppermute x3, starting transfers between devices, body(): parts.append(lax.ppermute(part, 'z_hi', ring(n_z, n_z - s)))  9.73 us
    ppermute x3, waiting for transfers between devices, body(): stats.append(lax.ppermute(stat, 'z_hi', ring(n_z, n_z - s)))  7.81 us
  transfers between devices with their start and end apart: 14, of which 4 were waited for; matrix products, arithmetic and copies ran while one was open for 0% of the time, Pallas kernels for 22%

profile of v1, /device:TPU:1, one launch (start us, length us, event | category | flops | bytes accessed | tf_op | source)
XLA Modules:
  0.0 155.8 jit_solution(17556251199475601530)
XLA Ops:
  6.5 1.4 pad_maximum_fusion
  7.9 2.1 %shard_map.73 = bf16[16,24,1152]{2,1,0:T(8,128)(2,1)} custom-call(bf16[2,24,3072]{2,1,0:T(8,128)(2,1)} %q_ref.1, bf16[2,24,3072]{2,1,0:T(8,128)(2,1)} %k_ref.1, bf16[2,24,3072]{2,1,0:T(8,128)(2,1)} %v_ref.1), custom_call_target="tpu_custom_call" | custom-call | tf_op jit(solution)/shard_map/pallas_call | solution.py:39
  10.1 20.8 %all_to_all.10 = bf16[16,24,1152]{2,1,0:T(8,128)(2,1)S(1)} all-to-all(bf16[16,24,1152]{2,1,0:T(8,128)(2,1)} %shard_map.73), channel_id=1, replica_groups=mesh['y'=4,'z_hi'=4,'core'=2,'z_lo'=2,'x'=4] {'z_lo','x','core'}, dimensions={0} | all-to-all | bytes 1769472 | tf_op jit(solution)/shard_map/all_to_all | solution.py:228
  30.9 1.4 collective-permute-start
  32.3 2.6 %collective-permute-start.1 = (bf16[384,768]{1,0:T(8,128)(2,1)S(1)}, bf16[384,768]{1,0:T(8,128)(2,1)S(1)}, u32[]{:S(2)}, u32[]{:S(2)}) collective-permute-start(bf16[384,768]{1,0:T(8,128)(2,1)S(1)} %slice.9.kv0), channel_id=1, source_target_pairs={{0,128},{64,192},{128,0},{192,64},{1,129},{65,193},{129,1},{193,65... | collective-permute-start | bytes 1769480 | tf_op jit(solution)/shard_map/ppermute | solution.py:232
  35.0 1.1 collective-permute-start.2
  36.1 5.7 %collective-permute-start.7 = (bf16[384,384]{1,0:T(8,128)(2,1)S(1)}, bf16[384,384]{1,0:T(8,128)(2,1)S(1)}, u32[]{:S(2)}, u32[]{:S(2)}) collective-permute-start(bf16[384,384]{1,0:T(8,128)(2,1)S(1)} %slice.8.q_ref), channel_id=1, source_target_pairs={{0,48},{16,0},{32,16},{48,32},{1,49},{17,1},{33,17},{49,33},{2,50}... | collective-permute-start | bytes 884744 | tf_op jit(solution)/shard_map/ppermute | solution.py:235
  41.8 11.8 %collective-permute-done.7.q_ref = bf16[384,384]{1,0:T(8,128)(2,1)S(1)} collective-permute-done((bf16[384,384]{1,0:T(8,128)(2,1)S(1)}, bf16[384,384]{1,0:T(8,128)(2,1)S(1)}, u32[]{:S(2)}, u32[]{:S(2)}) %collective-permute-start.7) | collective-permute-done | bytes 294944 | tf_op jit(solution)/shard_map/ppermute | solution.py:235
  53.6 4.4 %collective-permute-start.3 = (bf16[384,384]{1,0:T(8,128)(2,1)S(1)}, bf16[384,384]{1,0:T(8,128)(2,1)S(1)}, u32[]{:S(2)}, u32[]{:S(2)}) collective-permute-start(bf16[384,384]{1,0:T(8,128)(2,1)S(1)} %slice.8.q_ref), channel_id=1, source_target_pairs={{0,32},{16,48},{32,0},{48,16},{1,33},{17,49},{33,1},{49,17},{2,34}... | collective-permute-start | bytes 884744 | tf_op jit(solution)/shard_map/ppermute | solution.py:235
  58.1 2.1 %collective-permute-done.1.kv2 = bf16[384,768]{1,0:T(8,128)(2,1)S(1)} collective-permute-done((bf16[384,768]{1,0:T(8,128)(2,1)S(1)}, bf16[384,768]{1,0:T(8,128)(2,1)S(1)}, u32[]{:S(2)}, u32[]{:S(2)}) %collective-permute-start.1) | collective-permute-done | bytes 589856 | tf_op jit(solution)/shard_map/ppermute | solution.py:232
  60.2 0.8 copy-done.9
  61.0 0.8 copy-done.10
  61.8 7.0 %shard_map.77 = (bf16[384,384]{1,0:T(8,128)(2,1)}, f32[24,384]{1,0:T(8,128)}) custom-call(bf16[384,384]{1,0:T(8,128)(2,1)} %copy-done.13, bf16[384,768]{1,0:T(8,128)(2,1)} %copy-done, bf16[384,768]{1,0:T(8,128)(2,1)} %copy-done.8, bf16[384,768]{1,0:T(8,128)(2,1)} %copy-done.9, bf16[384,768]{1,0:T(8,128)(2,1)} %copy-done.10), custom_call_target="tpu_custom_call" | custom-call | flops 905969664 | bytes 2949120 | tf_op jit(solution)/shard_map/pallas_call | solution.py:106
  68.9 3.4 %collective-permute-start.8 = (bf16[384,384]{1,0:T(8,128)(2,1)}, bf16[384,384]{1,0:T(8,128)(2,1)S(1)}, u32[]{:S(2)}, u32[]{:S(2)}) collective-permute-start(bf16[384,384]{1,0:T(8,128)(2,1)} %get-tuple-element.21), channel_id=1, source_target_pairs={{0,16},{16,32},{32,48},{48,0},{1,17},{17,33},{33,49},{49,1},{2,18}... | collective-permute-start | bytes 884744 | tf_op jit(solution)/shard_map/ppermute | solution.py:237
  72.3 0.7 copy-done.12
  73.0 7.1 %shard_map.76 = (bf16[384,384]{1,0:T(8,128)(2,1)}, f32[24,384]{1,0:T(8,128)}) custom-call(bf16[384,384]{1,0:T(8,128)(2,1)} %copy-done.12, bf16[384,768]{1,0:T(8,128)(2,1)} %copy-done, bf16[384,768]{1,0:T(8,128)(2,1)} %copy-done.8, bf16[384,768]{1,0:T(8,128)(2,1)} %copy-done.9, bf16[384,768]{1,0:T(8,128)(2,1)} %copy-done.10), custom_call_target="tpu_custom_call" | custom-call | flops 905969664 | bytes 2949120 | tf_op jit(solution)/shard_map/pallas_call | solution.py:106
  80.1 2.3 %collective-permute-start.6 = (bf16[384,384]{1,0:T(8,128)(2,1)}, bf16[384,384]{1,0:T(8,128)(2,1)S(1)}, u32[]{:S(2)}, u32[]{:S(2)}) collective-permute-start(bf16[384,384]{1,0:T(8,128)(2,1)} %get-tuple-element.20), channel_id=1, source_target_pairs={{0,48},{16,0},{32,16},{48,32},{1,49},{17,1},{33,17},{49,33},{2,50}... | collective-permute-start | bytes 884744 | tf_op jit(solution)/shard_map/ppermute | solution.py:237
  82.4 0.7 copy-done.11
  83.1 7.0 %shard_map.75 = (bf16[384,384]{1,0:T(8,128)(2,1)}, f32[24,384]{1,0:T(8,128)}) custom-call(bf16[384,384]{1,0:T(8,128)(2,1)} %copy-done.11, bf16[384,768]{1,0:T(8,128)(2,1)} %copy-done, bf16[384,768]{1,0:T(8,128)(2,1)} %copy-done.8, bf16[384,768]{1,0:T(8,128)(2,1)} %copy-done.9, bf16[384,768]{1,0:T(8,128)(2,1)} %copy-done.10), custom_call_target="tpu_custom_call" | custom-call | flops 905969664 | bytes 2949120 | tf_op jit(solution)/shard_map/pallas_call | solution.py:106
  90.1 4.0 %collective-permute-start.4 = (bf16[384,384]{1,0:T(8,128)(2,1)}, bf16[384,384]{1,0:T(8,128)(2,1)S(1)}, u32[]{:S(2)}, u32[]{:S(2)}) collective-permute-start(bf16[384,384]{1,0:T(8,128)(2,1)} %get-tuple-element.19), channel_id=1, source_target_pairs={{0,32},{16,48},{32,0},{48,16},{1,33},{17,49},{33,1},{49,17},{2,34}... | collective-permute-start | bytes 884744 | tf_op jit(solution)/shard_map/ppermute | solution.py:237
  94.2 0.4 collective-permute-start.11
  94.6 3.2 %collective-permute-start.10 = (f32[24,384]{1,0:T(8,128)S(1)}, f32[24,384]{1,0:T(8,128)S(1)}, u32[]{:S(2)}, u32[]{:S(2)}) collective-permute-start(f32[24,384]{1,0:T(8,128)S(1)} %copy-done.14), channel_id=1, source_target_pairs={{0,48},{16,0},{32,16},{48,32},{1,49},{17,1},{33,17},{49,33},{2,50}... | collective-permute-start | bytes 110600 | tf_op jit(solution)/shard_map/ppermute | solution.py:238
  97.8 7.8 %collective-permute-done.11.l3 = f32[24,384]{1,0:T(8,128)S(1)} collective-permute-done((f32[24,384]{1,0:T(8,128)S(1)}, f32[24,384]{1,0:T(8,128)S(1)}, u32[]{:S(2)}, u32[]{:S(2)}) %collective-permute-start.11) | collective-permute-done | bytes 36896 | tf_op jit(solution)/shard_map/ppermute | solution.py:238
  105.6 3.7 %collective-permute-start.9 = (f32[24,384]{1,0:T(8,128)}, f32[24,384]{1,0:T(8,128)S(1)}, u32[]{:S(2)}, u32[]{:S(2)}) collective-permute-start(f32[24,384]{1,0:T(8,128)} %get-tuple-element.22), channel_id=1, source_target_pairs={{0,32},{16,48},{32,0},{48,16},{1,33},{17,49},{33,1},{49,17},{2,34}... | collective-permute-start | bytes 110600 | tf_op jit(solution)/shard_map/ppermute | solution.py:238
  109.3 10.8 %shard_map.74 = (f32[384,384]{1,0:T(8,128)}, f32[384,384]{1,0:T(8,128)}, f32[384,384]{1,0:T(8,128)}) custom-call(s32[1]{0:T(128)} %bitcast.branch_ref, s32[8]{0:T(128)} %cols_ref.1, bf16[384,384]{1,0:T(8,128)(2,1)} %copy-done.1, bf16[384,768]{1,0:T(8,128)(2,1)} %copy-done, bf16[384,768]{1,0:T(8,128)(2,1)} %copy-done.8, bf16[384,768]{1,0:T(8,128)(2,1)} %copy-done.9, ...), custom_call_target="tpu_custom_call" | custom-call | flops 1509949440 | bytes 2949120 | tf_op jit(solution)/shard_map/pallas_call | solution.py:165
  120.1 0.5 copy-done.6
  121.0 3.3 %shard_map.78 = (f32[384,384]{1,0:T(8,128)}, bf16[384,384]{1,0:T(8,128)(2,1)}) custom-call(f32[384,384]{1,0:T(8,128)} %get-tuple-element.16.acc_ref, f32[384,384]{1,0:T(8,128)} %get-tuple-element.17.stat_ref, f32[384,384]{1,0:T(8,128)} %get-tuple-element.18.borrow_ref, bf16[384,384]{1,0:T(8,128)(2,1)} %copy-done.4, bf16[384,384]{1,0:T(8,128)(2,1)} %copy-done.3, ...), custom_call_target="tpu_custom_call" | custom-call | tf_op jit(solution)/shard_map/pallas_call | solution.py:205
  124.3 1.3 collective-permute-start.12
  125.6 4.7 %collective-permute-done.12 = bf16[384,384]{1,0:T(8,128)(2,1)S(1)} collective-permute-done((bf16[384,384]{1,0:T(8,128)(2,1)}, bf16[384,384]{1,0:T(8,128)(2,1)S(1)}, u32[]{:S(2)}, u32[]{:S(2)}) %collective-permute-start.12) | collective-permute-done | bytes 294944 | tf_op jit(solution)/shard_map/ppermute | solution.py:242
  130.2 1.1 add_convert_fusion
  131.4 15.9 %all_to_all.11.in_ref = bf16[16,24,384]{2,1,0:T(8,128)(2,1)} all-to-all(bf16[16,24,384]{2,1,0:T(8,128)(2,1)S(1)} %bitcast.7), channel_id=1, replica_groups=mesh['y'=4,'z_hi'=4,'core'=2,'z_lo'=2,'x'=4] {'z_lo','x','core'}, dimensions={0} | all-to-all | bytes 589824 | tf_op jit(solution)/shard_map/all_to_all | solution.py:245
  147.3 1.7 %shard_map.79 = bf16[2,24,3072]{2,1,0:T(8,128)(2,1)} custom-call(bf16[16,24,384]{2,1,0:T(8,128)(2,1)} %all_to_all.11.in_ref), custom_call_target="tpu_custom_call" | custom-call | tf_op jit(solution)/shard_map/pallas_call | solution.py:56
  (42 shorter events, 0.5 us)
Async XLA Ops:
  6.5 102.7 %all-gather.3.cloned.1.call-start = ((), (), s32[]{:S(2)}) async-start(), calls=%async_computation.2 | async-start | bytes 1622016 | tf_op jit(solution)/shard_map/all_gather | solution.py:226
  30.9 29.3 %copy-start = (bf16[384,768]{1,0:T(8,128)(2,1)}, bf16[384,768]{1,0:T(8,128)(2,1)S(1)}, u32[]{:S(2)}) copy-start(bf16[384,768]{1,0:T(8,128)(2,1)S(1)} %slice.9.kv0) | copy-start | bytes 1769476
  30.9 27.1 %collective-permute-start = (bf16[384,768]{1,0:T(8,128)(2,1)S(1)}, bf16[384,768]{1,0:T(8,128)(2,1)S(1)}, u32[]{:S(2)}, u32[]{:S(2)}) collective-permute-start(bf16[384,768]{1,0:T(8,128)(2,1)S(1)} %slice.9.kv0), channel_id=1, source_target_pairs={{0,64},{64,128},{128,192},{192,0},{1,65},{65,129},{129,193},{193,1... | collective-permute-start | bytes 1769480 | tf_op jit(solution)/shard_map/ppermute | solution.py:232
  32.3 27.9 %collective-permute-start.1 = (bf16[384,768]{1,0:T(8,128)(2,1)S(1)}, bf16[384,768]{1,0:T(8,128)(2,1)S(1)}, u32[]{:S(2)}, u32[]{:S(2)}) collective-permute-start(bf16[384,768]{1,0:T(8,128)(2,1)S(1)} %slice.9.kv0), channel_id=1, source_target_pairs={{0,128},{64,192},{128,0},{192,64},{1,129},{65,193},{129,1},{193,65... | collective-permute-start | bytes 1769480 | tf_op jit(solution)/shard_map/ppermute | solution.py:232
  35.0 25.2 %collective-permute-start.2 = (bf16[384,768]{1,0:T(8,128)(2,1)S(1)}, bf16[384,768]{1,0:T(8,128)(2,1)S(1)}, u32[]{:S(2)}, u32[]{:S(2)}) collective-permute-start(bf16[384,768]{1,0:T(8,128)(2,1)S(1)} %slice.9.kv0), channel_id=1, source_target_pairs={{0,192},{64,0},{128,64},{192,128},{1,193},{65,1},{129,65},{193,129... | collective-permute-start | bytes 1769480 | tf_op jit(solution)/shard_map/ppermute | solution.py:232
  36.0 32.8 %copy-start.1 = (bf16[384,384]{1,0:T(8,128)(2,1)}, bf16[384,384]{1,0:T(8,128)(2,1)S(1)}, u32[]{:S(2)}) copy-start(bf16[384,384]{1,0:T(8,128)(2,1)S(1)} %slice.8.q_ref) | copy-start | bytes 884740
  36.1 17.5 %collective-permute-start.7 = (bf16[384,384]{1,0:T(8,128)(2,1)S(1)}, bf16[384,384]{1,0:T(8,128)(2,1)S(1)}, u32[]{:S(2)}, u32[]{:S(2)}) collective-permute-start(bf16[384,384]{1,0:T(8,128)(2,1)S(1)} %slice.8.q_ref), channel_id=1, source_target_pairs={{0,48},{16,0},{32,16},{48,32},{1,49},{17,1},{33,17},{49,33},{2,50}... | collective-permute-start | bytes 884744 | tf_op jit(solution)/shard_map/ppermute | solution.py:235
  41.8 30.5 %collective-permute-start.5 = (bf16[384,384]{1,0:T(8,128)(2,1)S(1)}, bf16[384,384]{1,0:T(8,128)(2,1)S(1)}, u32[]{:S(2)}, u32[]{:S(2)}) collective-permute-start(bf16[384,384]{1,0:T(8,128)(2,1)S(1)} %slice.8.q_ref), channel_id=1, source_target_pairs={{0,16},{16,32},{32,48},{48,0},{1,17},{17,33},{33,49},{49,1},{2,18}... | collective-permute-start | bytes 884744 | tf_op jit(solution)/shard_map/ppermute | solution.py:235
  53.6 6.6 %copy-start.13 = (bf16[384,384]{1,0:T(8,128)(2,1)}, bf16[384,384]{1,0:T(8,128)(2,1)S(1)}, u32[]{:S(2)}) copy-start(bf16[384,384]{1,0:T(8,128)(2,1)S(1)} %collective-permute-done.7.q_ref) | copy-start | bytes 884740
  53.6 28.8 %collective-permute-start.3 = (bf16[384,384]{1,0:T(8,128)(2,1)S(1)}, bf16[384,384]{1,0:T(8,128)(2,1)S(1)}, u32[]{:S(2)}, u32[]{:S(2)}) collective-permute-start(bf16[384,384]{1,0:T(8,128)(2,1)S(1)} %slice.8.q_ref), channel_id=1, source_target_pairs={{0,32},{16,48},{32,0},{48,16},{1,33},{17,49},{33,1},{49,17},{2,34}... | collective-permute-start | bytes 884744 | tf_op jit(solution)/shard_map/ppermute | solution.py:235
  58.1 2.2 %copy-start.8 = (bf16[384,768]{1,0:T(8,128)(2,1)}, bf16[384,768]{1,0:T(8,128)(2,1)S(1)}, u32[]{:S(2)}) copy-start(bf16[384,768]{1,0:T(8,128)(2,1)S(1)} %collective-permute-done.kv1) | copy-start | bytes 1769476
  60.2 0.8 copy-start.9
  61.0 0.8 copy-start.10
  68.9 51.2 %collective-permute-start.8 = (bf16[384,384]{1,0:T(8,128)(2,1)}, bf16[384,384]{1,0:T(8,128)(2,1)S(1)}, u32[]{:S(2)}, u32[]{:S(2)}) collective-permute-start(bf16[384,384]{1,0:T(8,128)(2,1)} %get-tuple-element.21), channel_id=1, source_target_pairs={{0,16},{16,32},{32,48},{48,0},{1,17},{17,33},{33,49},{49,1},{2,18}... | collective-permute-start | bytes 884744 | tf_op jit(solution)/shard_map/ppermute | solution.py:237
  72.3 0.7 copy-start.12
  80.1 14.1 %copy-start.15 = (f32[24,384]{1,0:T(8,128)S(1)}, f32[24,384]{1,0:T(8,128)}, u32[]{:S(2)}) copy-start(f32[24,384]{1,0:T(8,128)} %get-tuple-element.24) | copy-start | bytes 110596
  80.1 14.5 %copy-start.14 = (f32[24,384]{1,0:T(8,128)S(1)}, f32[24,384]{1,0:T(8,128)}, u32[]{:S(2)}) copy-start(f32[24,384]{1,0:T(8,128)} %get-tuple-element.23) | copy-start | bytes 110596
  80.1 40.0 %collective-permute-start.6 = (bf16[384,384]{1,0:T(8,128)(2,1)}, bf16[384,384]{1,0:T(8,128)(2,1)S(1)}, u32[]{:S(2)}, u32[]{:S(2)}) collective-permute-start(bf16[384,384]{1,0:T(8,128)(2,1)} %get-tuple-element.20), channel_id=1, source_target_pairs={{0,48},{16,0},{32,16},{48,32},{1,49},{17,1},{33,17},{49,33},{2,50}... | collective-permute-start | bytes 884744 | tf_op jit(solution)/shard_map/ppermute | solution.py:237
  82.4 0.7 copy-start.11
  90.1 30.0 %collective-permute-start.4 = (bf16[384,384]{1,0:T(8,128)(2,1)}, bf16[384,384]{1,0:T(8,128)(2,1)S(1)}, u32[]{:S(2)}, u32[]{:S(2)}) collective-permute-start(bf16[384,384]{1,0:T(8,128)(2,1)} %get-tuple-element.19), channel_id=1, source_target_pairs={{0,32},{16,48},{32,0},{48,16},{1,33},{17,49},{33,1},{49,17},{2,34}... | collective-permute-start | bytes 884744 | tf_op jit(solution)/shard_map/ppermute | solution.py:237
  94.2 11.4 %collective-permute-start.11 = (f32[24,384]{1,0:T(8,128)S(1)}, f32[24,384]{1,0:T(8,128)S(1)}, u32[]{:S(2)}, u32[]{:S(2)}) collective-permute-start(f32[24,384]{1,0:T(8,128)S(1)} %copy-done.15), channel_id=1, source_target_pairs={{0,16},{16,32},{32,48},{48,0},{1,17},{17,33},{33,49},{49,1},{2,18}... | collective-permute-start | bytes 110600 | tf_op jit(solution)/shard_map/ppermute | solution.py:238
  94.6 25.4 %collective-permute-start.10 = (f32[24,384]{1,0:T(8,128)S(1)}, f32[24,384]{1,0:T(8,128)S(1)}, u32[]{:S(2)}, u32[]{:S(2)}) collective-permute-start(f32[24,384]{1,0:T(8,128)S(1)} %copy-done.14), channel_id=1, source_target_pairs={{0,48},{16,0},{32,16},{48,32},{1,49},{17,1},{33,17},{49,33},{2,50}... | collective-permute-start | bytes 110600 | tf_op jit(solution)/shard_map/ppermute | solution.py:238
  105.6 14.5 %copy-start.5 = (f32[24,384]{1,0:T(8,128)}, f32[24,384]{1,0:T(8,128)S(1)}, u32[]{:S(2)}) copy-start(f32[24,384]{1,0:T(8,128)S(1)} %collective-permute-done.11.l3) | copy-start | bytes 110596
  105.6 14.5 %collective-permute-start.9 = (f32[24,384]{1,0:T(8,128)}, f32[24,384]{1,0:T(8,128)S(1)}, u32[]{:S(2)}, u32[]{:S(2)}) collective-permute-start(f32[24,384]{1,0:T(8,128)} %get-tuple-element.22), channel_id=1, source_target_pairs={{0,32},{16,48},{32,0},{48,16},{1,33},{17,49},{33,1},{49,17},{2,34}... | collective-permute-start | bytes 110600 | tf_op jit(solution)/shard_map/ppermute | solution.py:238
  120.0 0.6 copy-start.6
  120.1 0.6 copy-start.7
  120.1 0.7 copy-start.2
  120.1 0.8 copy-start.3
  120.1 0.9 copy-start.4
  124.3 6.0 %collective-permute-start.12 = (bf16[384,384]{1,0:T(8,128)(2,1)}, bf16[384,384]{1,0:T(8,128)(2,1)S(1)}, u32[]{:S(2)}, u32[]{:S(2)}) collective-permute-start(bf16[384,384]{1,0:T(8,128)(2,1)} %get-tuple-element.26), channel_id=1, source_target_pairs={{0,8},{1,9},{2,10},{3,11},{4,12},{5,13},{6,14},{7,15},{16,24},{17,... | collective-permute-start | bytes 884744 | tf_op jit(solution)/shard_map/ppermute | solution.py:242
Sparse Core Ops, SparseCore 0:
  9.9 71.4 all-gather.2

commit v2 on v1

v2 whole, which is shorter than its diff:
```python
import functools
import math

import jax
import jax.numpy as jnp
from jax import lax
from jax.experimental import pallas as pl
from jax.experimental.pallas import tpu as pltpu
from jax.sharding import Mesh
from jax.sharding import PartitionSpec as P

H = 24
HD = 128
LOG2E = 1.4426950408889634
SCALE2 = LOG2E / math.sqrt(HD)
VMEM_LIMIT = 24 * 1024 * 1024

VM = pl.BlockSpec(memory_space=pltpu.VMEM)
SM = pl.BlockSpec(memory_space=pltpu.SMEM)


def params(limit=VMEM_LIMIT):
    return pltpu.CompilerParams(vmem_limit_bytes=limit)


def pack_kernel(groups, q_ref, k_ref, v_ref, out_ref):
    width = q_ref.shape[2] // groups
    for group in range(groups):
        for branch in range(2):
            for at, ref in enumerate((q_ref, k_ref, v_ref)):
                out_ref[2 * group + branch, :, at * width : (at + 1) * width] = ref[
                    branch, :, group * width : (group + 1) * width
                ]


def pack(q, k, v, groups):
    rows, width = q.shape[1], q.shape[2] // groups
    return pl.pallas_call(
        functools.partial(pack_kernel, groups),
        out_shape=jax.ShapeDtypeStruct((2 * groups, rows, 3 * width), q.dtype),
        in_specs=[VM] * 3,
        out_specs=VM,
        compiler_params=params(2 * VMEM_LIMIT),
    )(q, k, v)


def unpack_kernel(groups, in_ref, out_ref):
    width = in_ref.shape[2]
    for group in range(groups):
        for branch in range(2):
            out_ref[branch, :, group * width : (group + 1) * width] = in_ref[2 * group + branch]


def unpack(x, groups):
    return pl.pallas_call(
        functools.partial(unpack_kernel, groups),
        out_shape=jax.ShapeDtypeStruct((2, x.shape[1], groups * x.shape[2]), x.dtype),
        in_specs=[VM],
        out_specs=VM,
        compiler_params=params(),
    )(x)


def split_kernel(core_ref, held_ref, own_ref, other_ref, q_ref, kv_ref):
    rows, width = held_ref.shape[0], q_ref.shape[1]
    per = own_ref.shape[1]
    core = core_ref[0]
    q_ref[0:rows, :] = held_ref[:, 0:width]
    kv_ref[...] = held_ref[:, width : 3 * width]
    for i, source in enumerate((core, 2 + core)):
        for ref, c in ((own_ref, core), (other_ref, 1 - core)):
            here = pl.ds(pl.multiple_of(rows + 2 * per * i + c * per, per), per)
            q_ref[here, :] = ref[source]


def split(core, held, own, other):
    rows, width = held.shape[0], held.shape[1] // 3
    return pl.pallas_call(
        split_kernel,
        out_shape=(
            jax.ShapeDtypeStruct((rows + 4 * own.shape[1], width), held.dtype),
            jax.ShapeDtypeStruct((rows, 2 * width), held.dtype),
        ),
        in_specs=[SM] + [VM] * 3,
        out_specs=(VM, VM),
        compiler_params=params(),
    )(core, held, own, other)


def nt(a, b):
    return lax.dot_general(a, b, (((1,), (1,)), ((), ())), preferred_element_type=jnp.float32)


def nn(a, b):
    return lax.dot_general(a, b, (((1,), (0,)), ((), ())), preferred_element_type=jnp.float32)


def write_stats(stat_ref, at, logs):
    rows = logs[0].shape[0]
    wide = [jnp.broadcast_to(log, (rows, HD)).T[0:16] for log in logs]
    line = lax.broadcasted_iota(jnp.int32, (16, rows), 0)
    x = jnp.where(line < 4, wide[0], jnp.where(line < 8, wide[1], wide[2]))
    high = x.astype(jnp.bfloat16).astype(jnp.float32)
    mid = (x - high).astype(jnp.bfloat16).astype(jnp.float32)
    low = x - high - mid
    part = jnp.bitwise_and(line, 3)
    x = jnp.where(part == 0, high, jnp.where(part == 1, mid, low))
    stat_ref[at : at + 16, :] = x.astype(jnp.bfloat16)


def read_stat(stats, head):
    return stats[4 * head : 4 * head + 1] + stats[4 * head + 1 : 4 * head + 2] + stats[4 * head + 2 : 4 * head + 3]


def head_cols(head, offset=0):
    return slice((offset + head) * HD, (offset + head + 1) * HD)


def take_block(refs, rows):
    whole = refs[0][...] if len(refs) == 1 else jnp.concatenate([ref[...] for ref in refs], axis=0)
    return whole[0:rows], whole[rows:]


def block_kernel(heads, n_q, n_kv, n_text, *refs):
    refs = list(refs)
    q_refs, kvs = [refs.pop(0) for _ in range(n_q)], [refs.pop(0) for _ in range(n_kv)]
    text_refs = [[refs.pop(0) for _ in range(n)] for n in n_text]
    refs.pop(0)
    out_ref = refs.pop(0)
    rows = out_ref.shape[0] - 16
    q, _ = take_block(q_refs, rows)

    def front(head):
        scores = [nt(q[:, head_cols(head)], kv[:, head_cols(head)]) for kv in kvs]
        top = scores[0].max(axis=-1, keepdims=True)
        for s in scores[1:]:
            top = jnp.maximum(top, s.max(axis=-1, keepdims=True))
        return scores, top * SCALE2

    ahead = front(0)
    logs = []
    for head in range(heads):
        scores, shift = ahead
        if head + 1 < heads:
            ahead = front(head + 1)
        total = acc = 0.0
        for s, kv in zip(scores, kvs):
            w = jnp.exp2(s * SCALE2 - shift)
            total = total + w.sum(axis=-1, keepdims=True)
            acc = acc + nn(w.astype(jnp.bfloat16), kv[:, head_cols(head, heads)])
        out_ref[0:rows, head_cols(head)] = (acc / total).astype(jnp.bfloat16)
        logs.append(shift + jnp.log2(total))
    write_stats(out_ref, rows, logs)
    for i, parts in enumerate(text_refs):
        refs[-1][i] = take_block(parts, rows)[1]


def block_attention(q, kvs, rows, heads, after, text_from=()):
    keys = sum(kv.shape[0] for kv in kvs)
    out = [jax.ShapeDtypeStruct((rows + 16, heads * HD), jnp.bfloat16)]
    if text_from:
        extra = sum(x.shape[0] for x in text_from[0]) - rows
        out.append(jax.ShapeDtypeStruct((len(text_from), extra, heads * HD), jnp.bfloat16))
    args = [*q, *kvs, *(x for block in text_from for x in block), after]
    return pl.pallas_call(
        functools.partial(block_kernel, heads, len(q), len(kvs), tuple(len(block) for block in text_from)),
        out_shape=out,
        in_specs=[VM] * len(args),
        out_specs=[VM] * len(out),
        compiler_params=params(),
        cost_estimate=pl.CostEstimate(
            flops=4 * heads * rows * HD * keys,
            bytes_accessed=4 * keys * heads * HD,
            transcendentals=heads * rows * keys,
        ),
    )(*args)


def text_kernel(heads, place_ref, cols_ref, q_ref, text_ref, values_ref, flags_ref, out_ref, lent_ref, kt, vt, vb):
    rows = lent_ref.shape[0]
    n_y, n_z, extra, _ = text_ref.shape
    per, txt = extra // 2, kt.shape[0]
    z, core = place_ref[0], place_ref[1]
    for y in range(n_y):
        for sz in range(n_z):
            here = pl.ds(pl.multiple_of((y * n_z + lax.rem(z + n_z - sz, n_z)) * per, per), per)
            kt[here, :] = text_ref[y, sz, 0:per]
            vt[here, :] = text_ref[y, sz, per : 2 * per]
            vb[here, :] = values_ref[1, y, sz]
    columns = lax.broadcasted_iota(jnp.int32, (1, txt), 1)
    listed = flags_ref[...] == 1
    for i in range(cols_ref.shape[0]):
        listed = jnp.logical_or(listed, columns == cols_ref[i])
    mask = listed.astype(jnp.float32)
    keep = 1.0 - mask * core.astype(jnp.float32)
    logs = []
    for head in range(heads):
        cols = head_cols(head)
        s = nt(q_ref[0:rows, cols], kt[:, cols])
        shift = s.max(axis=-1, keepdims=True) * SCALE2
        w = jnp.exp2(s * SCALE2 - shift)
        total = w.sum(axis=-1, keepdims=True)
        acc = nn((w * keep).astype(jnp.bfloat16), vt[:, cols])
        borrow = nn((w * mask).astype(jnp.bfloat16), vb[:, cols])
        out_ref[0:rows, cols] = (acc / total).astype(jnp.bfloat16)
        lent_ref[:, cols] = (borrow / total).astype(jnp.bfloat16)
        logs.append(shift + jnp.log2(total))
    write_stats(out_ref, rows, logs)


def text_attention(place, replace_cols, q, text, values, flags, rows, heads):
    txt = text.shape[0] * text.shape[1] * text.shape[2] // 2
    return pl.pallas_call(
        functools.partial(text_kernel, heads),
        out_shape=(
            jax.ShapeDtypeStruct((rows + 16, heads * HD), jnp.bfloat16),
            jax.ShapeDtypeStruct((rows, heads * HD), jnp.bfloat16),
        ),
        in_specs=[SM, SM] + [VM] * 4,
        out_specs=(VM, VM),
        scratch_shapes=[pltpu.VMEM((txt, heads * HD), jnp.bfloat16)] * 3,
        compiler_params=params(),
        cost_estimate=pl.CostEstimate(
            flops=6 * heads * rows * HD * txt,
            bytes_accessed=6 * txt * heads * HD,
            transcendentals=heads * rows * txt,
        ),
    )(place, replace_cols, q, text, values, flags)


def merge_kernel(heads, p0, p1, p2, p3, pt, lent_in, out_ref, lent_ref):
    parts = (p0, p1, p2, p3, pt)
    rows = lent_in.shape[0]
    stats = [p[rows : rows + 16].astype(jnp.float32) for p in parts]
    for head in range(heads):
        cols = head_cols(head)
        logs = [read_stat(s, head) for s in stats]
        top = functools.reduce(jnp.maximum, logs)
        weights = [jnp.exp2(log - top) for log in logs]
        inverse = 1.0 / sum(weights)
        weights = [jnp.broadcast_to(w * inverse, (HD, rows)).T for w in weights]
        result = 0.0
        for p, w in zip(parts, weights):
            result = result + p[0:rows, cols].astype(jnp.float32) * w
        out_ref[:, cols] = result
        lent_ref[:, cols] = (lent_in[:, cols].astype(jnp.float32) * weights[-1]).astype(jnp.bfloat16)


def merge(parts, lent, heads):
    rows = lent.shape[0]
    return pl.pallas_call(
        functools.partial(merge_kernel, heads),
        out_shape=(
            jax.ShapeDtypeStruct((rows, heads * HD), jnp.float32),
            jax.ShapeDtypeStruct((rows, heads * HD), jnp.bfloat16),
        ),
        in_specs=[VM] * 6,
        out_specs=(VM, VM),
        compiler_params=params(),
    )(*parts, lent)


def ring(n, step):
    return [(i, (i + step) % n) for i in range(n)]


def gather_ring(x, axis, n):
    near = {s: lax.ppermute(x, axis, ring(n, s)) for s in (1, n - 1)}
    half = x.shape[0] // 2
    far = [
        lax.ppermute(near[1][:half], axis, ring(n, 1)),
        lax.ppermute(near[n - 1][half:], axis, ring(n, n - 1)),
    ]
    return {1: [near[1]], n // 2: far, n - 1: [near[n - 1]]}


def body(q_img, k_img, v_img, k_txt, v_txt, replace_cols, shared_flags):
    groups = lax.axis_size("z_lo") * lax.axis_size("x")
    n_y, n_z = lax.axis_size("y"), lax.axis_size("z_hi")
    heads = H // groups
    width = heads * HD
    axes = ("z_lo", "x", "core")
    own_text = jnp.concatenate([k_txt, v_txt], axis=0)
    other_text = lax.ppermute(own_text, "core", [(0, 1), (1, 0)])
    packed = pack(q_img, k_img, v_img, groups)
    held = lax.all_to_all(packed, axes, split_axis=0, concat_axis=0, tiled=True)
    rows = held.shape[0] * held.shape[1]
    place = jnp.stack([lax.axis_index(a) for a in ("z_hi", "core")]).astype(jnp.int32)
    q, kv = split(place[1:], held.reshape(rows, 3 * width), own_text, other_text)
    qs = {0: [q]} | gather_ring(q, "z_hi", n_z)
    kvs = [kv] + [piece for block in gather_ring(kv, "y", n_y).values() for piece in block]
    flags = shared_flags.reshape(1, -1)
    parts, before = [], flags
    for s in (1, 3, 2):
        before = block_attention(qs[s], kvs, rows, heads, before)[0]
        parts.append(lax.ppermute(before, "z_hi", ring(n_z, n_z - s)))
    own, text = block_attention(qs[0], kvs, rows, heads, before, [qs[i] for i in range(n_z)])
    text = lax.all_gather(text, "y")
    values = lax.all_gather(text[:, :, text.shape[2] // 2 :], "core")
    txt_part, lent = text_attention(place, replace_cols, q, text, values, flags, rows, heads)
    result, lent = merge([own] + parts + [txt_part], lent, heads)
    borrowed = lax.ppermute(lent, "core", [(0, 1)])
    result = (result + borrowed.astype(jnp.float32)).astype(jnp.bfloat16)
    result = result.reshape(2 * groups, rows // (2 * groups), width)
    back = lax.all_to_all(result, axes, split_axis=0, concat_axis=0, tiled=True)
    return unpack(back, groups)


def solution(mesh):
    fine = Mesh(mesh.devices.reshape(4, 4, 2, 2, 4), ("y", "z_hi", "core", "z_lo", "x"))
    seq, head = ("y", "z_hi", "core"), ("z_lo", "x")
    tokens = P(None, seq + head, None)
    text = P(None, seq, head)
    return jax.shard_map(
        body,
        mesh=fine,
        in_specs=(tokens, tokens, tokens, text, text, P(), P()),
        out_specs=tokens,
        check_vma=False,
    )
```

time: 156 us -> 113 us (0.72)
  Pallas kernels: 39 us -> 17.7 us
  between operations: 13.5 us -> 0.17 us
  blocking collectives: 36.7 us -> 30.6 us
  other arithmetic: 2.52 us -> 0.15 us
  local copies, waits for them, and re-layouts: 4.02 us -> 5.82 us
    all_to_all x2 -> x1, blocking collectives: 36.7 us -> 11.3 us  [body(): back = lax.all_to_all(result, axes, split_axis=0, concat_axis=0, tiled=True)]
    all_gather x0 -> x2, blocking collectives: none -> 19.3 us  [the longest x1 12.4 us: body(): text = lax.all_gather(text, 'y')]
    pallas_call x5 -> x7, Pallas kernels: 35.2 us -> 15.9 us  [the longest x4 12.5 us: block_attention(): pl.pallas_call(functools.partial(block_kernel, heads, len(q), len(kvs), t...]
    all_to_all x0 -> x1, waiting for transfers between devices: none -> 12.1 us  [body(): held = lax.all_to_all(packed, axes, split_axis=0, concat_axis=0, tiled=True)]
    ppermute x12, waiting for transfers between devices: 21.8 us -> 11.8 us  [the longest x4 9.89 us: gather_ring(): near = {s: lax.ppermute(x, axis, ring(n, s)) for s in (1, n - 1)}]
    ppermute x12, starting transfers between devices: 32.2 us -> 23.9 us  [the longest x3 8.78 us: body(): parts.append(lax.ppermute(before, 'z_hi', ring(n_z, n_z - s)))]
    all_to_all x0 -> x1, starting transfers between devices: none -> 7.3 us  [body(): held = lax.all_to_all(packed, axes, split_axis=0, concat_axis=0, tiled=True)]
    ppermute x1, waiting for transfers between devices: 4.66 us -> 2.18 us  [body(): borrowed = lax.ppermute(lent, 'core', [(0, 1)])]
  transfers between devices with their start and end apart: 14 -> 14, of which waited for: 4 -> 7; matrix products, arithmetic and copies ran while one was open for 0% -> 1% of each run, Pallas kernels for 22% -> 13%
where the time goes in v2:
time: 113 us
  starting transfers between devices  32.5 us (29%)
  blocking collectives  30.6 us (27%)
  waiting for transfers between devices  26.1 us (23%)
  Pallas kernels  17.7 us (16%)
  local copies, waits for them, and re-layouts  5.82 us (5%)
    pallas_call x4, Pallas kernels, block_attention(): pl.pallas_call(functools.partial(block_kernel, heads, len(q), len(kvs), t...  12.5 us
    all_gather x1, blocking collectives, body(): text = lax.all_gather(text, 'y')  12.4 us
    all_to_all x1, waiting for transfers between devices, body(): held = lax.all_to_all(packed, axes, split_axis=0, concat_axis=0, tiled=True)  12.1 us
    all_to_all x1, blocking collectives, body(): back = lax.all_to_all(result, axes, split_axis=0, concat_axis=0, tiled=True)  11.3 us
    ppermute x4, waiting for transfers between devices, gather_ring(): near = {s: lax.ppermute(x, axis, ring(n, s)) for s in (1, n - 1)}  9.89 us
    ppermute x3, starting transfers between devices, body(): parts.append(lax.ppermute(before, 'z_hi', ring(n_z, n_z - s)))  8.78 us
    ppermute x4, starting transfers between devices, gather_ring(): near = {s: lax.ppermute(x, axis, ring(n, s)) for s in (1, n - 1)}  7.94 us
    all_to_all x1, starting transfers between devices, body(): held = lax.all_to_all(packed, axes, split_axis=0, concat_axis=0, tiled=True)  7.3 us
  transfers between devices with their start and end apart: 14, of which 7 were waited for; matrix products, arithmetic and copies ran while one was open for 1% of the time, Pallas kernels for 13%

profile of v2, /device:TPU:1, one launch (start us, length us, event | category | flops | bytes accessed | tf_op | source)
XLA Modules:
  0.0 113.0 jit_solution(13679135676806764158)
XLA Ops:
  0.0 1.0 copy-done
  1.0 1.0 copy-done.1
  1.9 1.0 copy-done.2
  2.9 1.0 shard_map.73
  3.9 7.3 %all-to-all-start = ((bf16[16,24,1152]{2,1,0:T(8,128)(2,1)}), bf16[16,24,1152]{2,1,0:T(8,128)(2,1)S(1)}, u32[]{:S(2)}, u32[]{:S(2)}) async-start(bf16[16,24,1152]{2,1,0:T(8,128)(2,1)} %shard_map.73), calls=%async_computation | async-start | bytes 1769472 | tf_op jit(solution)/shard_map/all_to_all | solution.py:286
  11.2 0.7 copy-done.6
  12.1 1.1 collective-permute-done.other_ref
  13.2 12.1 %all-to-all-done = bf16[16,24,1152]{2,1,0:T(8,128)(2,1)S(1)} async-done(((bf16[16,24,1152]{2,1,0:T(8,128)(2,1)}), bf16[16,24,1152]{2,1,0:T(8,128)(2,1)S(1)}, u32[]{:S(2)}, u32[]{:S(2)}) %all-to-all-start) | async-done | bytes 884768 | tf_op jit(solution)/shard_map/all_to_all | solution.py:286
  25.3 2.8 %collective-permute-start.3 = (bf16[384,768]{1,0:T(8,128)(2,1)S(1)}, bf16[384,768]{1,0:T(8,128)(2,1)S(1)}, u32[]{:S(2)}, u32[]{:S(2)}) collective-permute-start(bf16[384,768]{1,0:T(8,128)(2,1)S(1)} %get-tuple-element.14.refs_1_.refs_2_), channel_id=1, source_target_pairs={{0,192},{64,0},{128,64},{192,128},{1,193},{65,1},{129,65},{193,129... | collective-permute-start | bytes 1769480 | tf_op jit(solution)/shard_map/ppermute | solution.py:268
  28.1 5.1 %collective-permute-start.7 = (bf16[448,384]{1,0:T(8,128)(2,1)S(1)}, bf16[448,384]{1,0:T(8,128)(2,1)S(1)}, u32[]{:S(2)}, u32[]{:S(2)}) collective-permute-start(bf16[448,384]{1,0:T(8,128)(2,1)S(1)} %get-tuple-element.13.refs_0_.refs_6_.q_ref), channel_id=1, source_target_pairs={{0,48},{16,0},{32,16},{48,32},{1,49},{17,1},{33,17},{49,33},{2,50}... | collective-permute-start | bytes 1032200 | tf_op jit(solution)/shard_map/ppermute | solution.py:268
  33.3 6.6 %collective-permute-done.3.refs_5_.refs_6_ = bf16[384,768]{1,0:T(8,128)(2,1)S(1)} collective-permute-done((bf16[384,768]{1,0:T(8,128)(2,1)S(1)}, bf16[384,768]{1,0:T(8,128)(2,1)S(1)}, u32[]{:S(2)}, u32[]{:S(2)}) %collective-permute-start.3) | collective-permute-done | bytes 589856 | tf_op jit(solution)/shard_map/ppermute | solution.py:268
  39.9 0.7 slice.21
  40.6 3.4 %collective-permute-start.4 = (bf16[192,768]{1,0:T(8,128)(2,1)}, bf16[192,768]{1,0:T(8,128)(2,1)S(1)}, u32[]{:S(2)}, u32[]{:S(2)}) collective-permute-start(bf16[192,768]{1,0:T(8,128)(2,1)} %slice.21), channel_id=1, source_target_pairs={{0,192},{64,0},{128,64},{192,128},{1,193},{65,1},{129,65},{193,129... | collective-permute-start | bytes 884744 | tf_op jit(solution)/shard_map/ppermute | solution.py:272
  44.0 0.7 slice.20
  44.8 2.3 %collective-permute-done.7.refs_0_.refs_10_ = bf16[448,384]{1,0:T(8,128)(2,1)S(1)} collective-permute-done((bf16[448,384]{1,0:T(8,128)(2,1)S(1)}, bf16[448,384]{1,0:T(8,128)(2,1)S(1)}, u32[]{:S(2)}, u32[]{:S(2)}) %collective-permute-start.7) | collective-permute-done | bytes 344096 | tf_op jit(solution)/shard_map/ppermute | solution.py:268
  47.1 3.6 %collective-permute-start.8 = (bf16[224,384]{1,0:T(8,128)(2,1)S(1)}, bf16[224,384]{1,0:T(8,128)(2,1)S(1)}, u32[]{:S(2)}, u32[]{:S(2)}) collective-permute-start(bf16[224,384]{1,0:T(8,128)(2,1)S(1)} %slice.23), channel_id=1, source_target_pairs={{0,48},{16,0},{32,16},{48,32},{1,49},{17,1},{33,17},{49,33},{2,50}... | collective-permute-start | bytes 516104 | tf_op jit(solution)/shard_map/ppermute | solution.py:272
  50.7 1.0 collective-permute-done.5.refs_0_.refs_7_
  51.8 0.8 collective-permute-done.2.refs_3_.refs_4_
  52.6 3.1 %shard_map.75.refs_6_ = bf16[400,384]{1,0:T(8,128)(2,1)S(1)} custom-call(bf16[448,384]{1,0:T(8,128)(2,1)S(1)} %collective-permute-done.5.refs_0_.refs_7_, bf16[384,768]{1,0:T(8,128)(2,1)S(1)} %get-tuple-element.14.refs_1_.refs_2_, bf16[384,768]{1,0:T(8,128)(2,1)S(1)} %collective-permute-done.1.refs_2_.refs_3_, ...), custom_call_target="tpu_custom_call" | custom-call | flops 905969664 | bytes 2359296 | tf_op jit(solution)/shard_map/pallas_call | solution.py:165
  55.8 5.4 %collective-permute-start.9 = (bf16[400,384]{1,0:T(8,128)(2,1)S(1)}, bf16[400,384]{1,0:T(8,128)(2,1)S(1)}, u32[]{:S(2)}, u32[]{:S(2)}) collective-permute-start(bf16[400,384]{1,0:T(8,128)(2,1)S(1)} %shard_map.75.refs_6_), channel_id=1, source_target_pairs={{0,48},{16,0},{32,16},{48,32},{1,49},{17,1},{33,17},{49,33},{2,50}... | collective-permute-start | bytes 921608 | tf_op jit(solution)/shard_map/ppermute | solution.py:296
  61.1 3.1 %shard_map.76.refs_7_ = bf16[400,384]{1,0:T(8,128)(2,1)S(1)} custom-call(bf16[448,384]{1,0:T(8,128)(2,1)S(1)} %collective-permute-done.7.refs_0_.refs_10_, bf16[384,768]{1,0:T(8,128)(2,1)S(1)} %get-tuple-element.14.refs_1_.refs_2_, bf16[384,768]{1,0:T(8,128)(2,1)S(1)} %collective-permute-done.1.refs_2_.refs_3_, ...), custom_call_target="tpu_custom_call" | custom-call | flops 905969664 | bytes 2359296 | tf_op jit(solution)/shard_map/pallas_call | solution.py:165
  64.4 3.2 %shard_map.77.refs_11_ = bf16[400,384]{1,0:T(8,128)(2,1)S(1)} custom-call(bf16[224,384]{1,0:T(8,128)(2,1)S(1)} %collective-permute-done.6.refs_0_.refs_8_, bf16[224,384]{1,0:T(8,128)(2,1)S(1)} %collective-permute-done.8.refs_1_.refs_9_, bf16[384,768]{1,0:T(8,128)(2,1)S(1)} %get-tuple-element.14.refs_1_.refs_2_, ...), custom_call_target="tpu_custom_call" | custom-call | flops 905969664 | bytes 2359296 | tf_op jit(solution)/shard_map/pallas_call | solution.py:165
  67.5 3.3 %collective-permute-start.11 = (bf16[400,384]{1,0:T(8,128)(2,1)S(1)}, bf16[400,384]{1,0:T(8,128)(2,1)S(1)}, u32[]{:S(2)}, u32[]{:S(2)}) collective-permute-start(bf16[400,384]{1,0:T(8,128)(2,1)S(1)} %shard_map.77.refs_11_), channel_id=1, source_target_pairs={{0,32},{16,48},{32,0},{48,16},{1,33},{17,49},{33,1},{49,17},{2,34}... | collective-permute-start | bytes 921608 | tf_op jit(solution)/shard_map/ppermute | solution.py:296
  70.9 3.1 %shard_map.78 = (bf16[400,384]{1,0:T(8,128)(2,1)S(1)}, bf16[4,64,384]{2,1,0:T(8,128)(2,1)S(1)}) custom-call(bf16[448,384]{1,0:T(8,128)(2,1)S(1)} %get-tuple-element.13.refs_0_.refs_6_.q_ref, bf16[384,768]{1,0:T(8,128)(2,1)S(1)} %get-tuple-element.14.refs_1_.refs_2_, bf16[384,768]{1,0:T(8,128)(2,1)S(1)} %collective-permute-done.1.refs_2_.refs_3_, ...), custom_call_target="tpu_custom_call" | custom-call | flops 905969664 | bytes 2359296 | tf_op jit(solution)/shard_map/pallas_call | solution.py:165
  74.0 12.4 %all-gather = bf16[16,64,384]{2,1,0:T(8,128)(2,1)S(1)} all-gather(bf16[4,64,384]{2,1,0:T(8,128)(2,1)S(1)} %get-tuple-element.16), channel_id=2, replica_groups=mesh['y'=4,'z_hi'=4,'core'=2,'z_lo'=2,'x'=4] {'y'}, dimensions={0}, use_global_device_ids=true | all-gather | bytes 983040 | tf_op jit(solution)/shard_map/all_gather | solution.py:298
  86.4 6.9 %all-gather.1 = bf16[8,4,32,384]{3,2,1,0:T(8,128)(2,1)S(1)} all-gather(bf16[4,4,32,384]{3,2,1,0:T(8,128)(2,1)S(1)} %slice.24), channel_id=3, replica_groups=mesh['y'=4,'z_hi'=4,'core'=2,'z_lo'=2,'x'=4] {'core'}, dimensions={0}, use_global_device_ids=true | all-gather | bytes 1179648 | tf_op jit(solution)/shard_map/all_gather | solution.py:299
  94.0 2.5 %shard_map.79 = (bf16[400,384]{1,0:T(8,128)(2,1)S(1)}, bf16[384,384]{1,0:T(8,128)(2,1)S(1)}) custom-call(s32[2]{0:T(128)S(1)} %pad_add_fusion.place_ref, s32[8]{0:T(128)S(1)} %copy-done.4, bf16[448,384]{1,0:T(8,128)(2,1)S(1)} %get-tuple-element.13.refs_0_.refs_6_.q_ref, bf16[4,4,64,384]{3,2,1,0:T(8,128)(2,1)S(1)} %bitcast.8, ...), custom_call_target="tpu_custom_call" | custom-call | flops 452984832 | bytes 1179648 | tf_op jit(solution)/shard_map/pallas_call | solution.py:213
  96.5 0.9 shard_map.80
  97.4 1.3 %collective-permute-start.12 = (bf16[384,384]{1,0:T(8,128)(2,1)S(1)}, bf16[384,384]{1,0:T(8,128)(2,1)S(1)}, u32[]{:S(2)}, u32[]{:S(2)}) collective-permute-start(bf16[384,384]{1,0:T(8,128)(2,1)S(1)} %get-tuple-element.20), channel_id=1, source_target_pairs={{0,8},{1,9},{2,10},{3,11},{4,12},{5,13},{6,14},{7,15},{16,24},{17,... | collective-permute-start | bytes 884744 | tf_op jit(solution)/shard_map/ppermute | solution.py:302
  98.7 2.2 %collective-permute-done.12 = bf16[384,384]{1,0:T(8,128)(2,1)S(1)} collective-permute-done((bf16[384,384]{1,0:T(8,128)(2,1)S(1)}, bf16[384,384]{1,0:T(8,128)(2,1)S(1)}, u32[]{:S(2)}, u32[]{:S(2)}) %collective-permute-start.12) | collective-permute-done | bytes 294944 | tf_op jit(solution)/shard_map/ppermute | solution.py:302
  101.0 11.3 %all_to_all.10.in_ref = bf16[16,24,384]{2,1,0:T(8,128)(2,1)S(1)} all-to-all(bf16[16,24,384]{2,1,0:T(8,128)(2,1)S(1)} %bitcast.13), channel_id=1, replica_groups=mesh['y'=4,'z_hi'=4,'core'=2,'z_lo'=2,'x'=4] {'z_lo','x','core'}, dimensions={0} | all-to-all | bytes 589824 | tf_op jit(solution)/shard_map/all_to_all | solution.py:305
  112.2 0.7 shard_map.81
  (31 shorter events, 1.3 us)
Async XLA Ops:
  0.0 1.0 copy-start
  1.0 1.0 copy-start.1
  1.9 1.0 copy-start.2
  3.9 7.3 %copy-start.5 = (bf16[2,16,384]{2,1,0:T(8,128)(2,1)S(1)}, bf16[2,16,384]{2,1,0:T(8,128)(2,1)}, u32[]{:S(2)}) copy-start(bf16[2,16,384]{2,1,0:T(8,128)(2,1)} %param.10) | copy-start | bytes 73732
  3.9 21.3 %all-to-all-start = ((bf16[16,24,1152]{2,1,0:T(8,128)(2,1)}), bf16[16,24,1152]{2,1,0:T(8,128)(2,1)S(1)}, u32[]{:S(2)}, u32[]{:S(2)}) async-start(bf16[16,24,1152]{2,1,0:T(8,128)(2,1)} %shard_map.73), calls=%async_computation | async-start | bytes 1769472 | tf_op jit(solution)/shard_map/all_to_all | solution.py:286
  11.2 0.7 copy-start.6
  12.0 1.2 %collective-permute-start = (bf16[4,16,384]{2,1,0:T(8,128)(2,1)S(1)}, bf16[4,16,384]{2,1,0:T(8,128)(2,1)S(1)}, u32[]{:S(2)}, u32[]{:S(2)}) collective-permute-start(bf16[4,16,384]{2,1,0:T(8,128)(2,1)S(1)} %constant_dynamic-update-slice_fusion.own_ref), channel_id=1, source_target_pairs={{0,8},{8,0},{1,9},{9,1},{2,10},{10,2},{3,11},{11,3},{4,12},{12,4},... | collective-permute-start | bytes 147464 | tf_op jit(solution)/shard_map/ppermute | solution.py:284
  25.3 14.6 %collective-permute-start.3 = (bf16[384,768]{1,0:T(8,128)(2,1)S(1)}, bf16[384,768]{1,0:T(8,128)(2,1)S(1)}, u32[]{:S(2)}, u32[]{:S(2)}) collective-permute-start(bf16[384,768]{1,0:T(8,128)(2,1)S(1)} %get-tuple-element.14.refs_1_.refs_2_), channel_id=1, source_target_pairs={{0,192},{64,0},{128,64},{192,128},{1,193},{65,1},{129,65},{193,129... | collective-permute-start | bytes 1769480 | tf_op jit(solution)/shard_map/ppermute | solution.py:268
  28.1 15.9 %collective-permute-start.1 = (bf16[384,768]{1,0:T(8,128)(2,1)S(1)}, bf16[384,768]{1,0:T(8,128)(2,1)S(1)}, u32[]{:S(2)}, u32[]{:S(2)}) collective-permute-start(bf16[384,768]{1,0:T(8,128)(2,1)S(1)} %get-tuple-element.14.refs_1_.refs_2_), channel_id=1, source_target_pairs={{0,64},{64,128},{128,192},{192,0},{1,65},{65,129},{129,193},{193,1... | collective-permute-start | bytes 1769480 | tf_op jit(solution)/shard_map/ppermute | solution.py:268
  28.1 18.9 %collective-permute-start.7 = (bf16[448,384]{1,0:T(8,128)(2,1)S(1)}, bf16[448,384]{1,0:T(8,128)(2,1)S(1)}, u32[]{:S(2)}, u32[]{:S(2)}) collective-permute-start(bf16[448,384]{1,0:T(8,128)(2,1)S(1)} %get-tuple-element.13.refs_0_.refs_6_.q_ref), channel_id=1, source_target_pairs={{0,48},{16,0},{32,16},{48,32},{1,49},{17,1},{33,17},{49,33},{2,50}... | collective-permute-start | bytes 1032200 | tf_op jit(solution)/shard_map/ppermute | solution.py:268
  33.3 18.4 %collective-permute-start.5 = (bf16[448,384]{1,0:T(8,128)(2,1)S(1)}, bf16[448,384]{1,0:T(8,128)(2,1)S(1)}, u32[]{:S(2)}, u32[]{:S(2)}) collective-permute-start(bf16[448,384]{1,0:T(8,128)(2,1)S(1)} %get-tuple-element.13.refs_0_.refs_6_.q_ref), channel_id=1, source_target_pairs={{0,16},{16,32},{32,48},{48,0},{1,17},{17,33},{33,49},{49,1},{2,18}... | collective-permute-start | bytes 1032200 | tf_op jit(solution)/shard_map/ppermute | solution.py:268
  40.6 11.2 %collective-permute-start.4 = (bf16[192,768]{1,0:T(8,128)(2,1)}, bf16[192,768]{1,0:T(8,128)(2,1)S(1)}, u32[]{:S(2)}, u32[]{:S(2)}) collective-permute-start(bf16[192,768]{1,0:T(8,128)(2,1)} %slice.21), channel_id=1, source_target_pairs={{0,192},{64,0},{128,64},{192,128},{1,193},{65,1},{129,65},{193,129... | collective-permute-start | bytes 884744 | tf_op jit(solution)/shard_map/ppermute | solution.py:272
  44.8 7.9 %collective-permute-start.2 = (bf16[192,768]{1,0:T(8,128)(2,1)}, bf16[192,768]{1,0:T(8,128)(2,1)S(1)}, u32[]{:S(2)}, u32[]{:S(2)}) collective-permute-start(bf16[192,768]{1,0:T(8,128)(2,1)} %slice.20), channel_id=1, source_target_pairs={{0,64},{64,128},{128,192},{192,0},{1,65},{65,129},{129,193},{193,1... | collective-permute-start | bytes 884744 | tf_op jit(solution)/shard_map/ppermute | solution.py:271
  47.1 17.3 %collective-permute-start.8 = (bf16[224,384]{1,0:T(8,128)(2,1)S(1)}, bf16[224,384]{1,0:T(8,128)(2,1)S(1)}, u32[]{:S(2)}, u32[]{:S(2)}) collective-permute-start(bf16[224,384]{1,0:T(8,128)(2,1)S(1)} %slice.23), channel_id=1, source_target_pairs={{0,48},{16,0},{32,16},{48,32},{1,49},{17,1},{33,17},{49,33},{2,50}... | collective-permute-start | bytes 516104 | tf_op jit(solution)/shard_map/ppermute | solution.py:272
  51.6 12.7 %collective-permute-start.6 = (bf16[224,384]{1,0:T(8,128)(2,1)S(1)}, bf16[224,384]{1,0:T(8,128)(2,1)S(1)}, u32[]{:S(2)}, u32[]{:S(2)}) collective-permute-start(bf16[224,384]{1,0:T(8,128)(2,1)S(1)} %slice.22), channel_id=1, source_target_pairs={{0,16},{16,32},{32,48},{48,0},{1,17},{17,33},{33,49},{49,1},{2,18}... | collective-permute-start | bytes 516104 | tf_op jit(solution)/shard_map/ppermute | solution.py:271
  51.7 0.9 copy-start.3
  55.8 40.8 %collective-permute-start.9 = (bf16[400,384]{1,0:T(8,128)(2,1)S(1)}, bf16[400,384]{1,0:T(8,128)(2,1)S(1)}, u32[]{:S(2)}, u32[]{:S(2)}) collective-permute-start(bf16[400,384]{1,0:T(8,128)(2,1)S(1)} %shard_map.75.refs_6_), channel_id=1, source_target_pairs={{0,48},{16,0},{32,16},{48,32},{1,49},{17,1},{33,17},{49,33},{2,50}... | collective-permute-start | bytes 921608 | tf_op jit(solution)/shard_map/ppermute | solution.py:296
  64.3 32.2 %collective-permute-start.10 = (bf16[400,384]{1,0:T(8,128)(2,1)S(1)}, bf16[400,384]{1,0:T(8,128)(2,1)S(1)}, u32[]{:S(2)}, u32[]{:S(2)}) collective-permute-start(bf16[400,384]{1,0:T(8,128)(2,1)S(1)} %shard_map.76.refs_7_), channel_id=1, source_target_pairs={{0,16},{16,32},{32,48},{48,0},{1,17},{17,33},{33,49},{49,1},{2,18}... | collective-permute-start | bytes 921608 | tf_op jit(solution)/shard_map/ppermute | solution.py:296
  67.5 28.9 %collective-permute-start.11 = (bf16[400,384]{1,0:T(8,128)(2,1)S(1)}, bf16[400,384]{1,0:T(8,128)(2,1)S(1)}, u32[]{:S(2)}, u32[]{:S(2)}) collective-permute-start(bf16[400,384]{1,0:T(8,128)(2,1)S(1)} %shard_map.77.refs_11_), channel_id=1, source_target_pairs={{0,32},{16,48},{32,0},{48,16},{1,33},{17,49},{33,1},{49,17},{2,34}... | collective-permute-start | bytes 921608 | tf_op jit(solution)/shard_map/ppermute | solution.py:296
  93.4 0.7 copy-start.4
  97.4 3.5 %collective-permute-start.12 = (bf16[384,384]{1,0:T(8,128)(2,1)S(1)}, bf16[384,384]{1,0:T(8,128)(2,1)S(1)}, u32[]{:S(2)}, u32[]{:S(2)}) collective-permute-start(bf16[384,384]{1,0:T(8,128)(2,1)S(1)} %get-tuple-element.20), channel_id=1, source_target_pairs={{0,8},{1,9},{2,10},{3,11},{4,12},{5,13},{6,14},{7,15},{16,24},{17,... | collective-permute-start | bytes 884744 | tf_op jit(solution)/shard_map/ppermute | solution.py:302

commit v3 on v2

--- a/solution.py
+++ b/solution.py
@@ -23,14 +23,21 @@
     return pltpu.CompilerParams(vmem_limit_bytes=limit)
 
 
-def pack_kernel(groups, q_ref, k_ref, v_ref, out_ref):
+def pack_kernel(groups, q_ref, k_ref, v_ref, out_ref, sem):
     width = q_ref.shape[2] // groups
+    copies = []
     for group in range(groups):
         for branch in range(2):
             for at, ref in enumerate((q_ref, k_ref, v_ref)):
-                out_ref[2 * group + branch, :, at * width : (at + 1) * width] = ref[
-                    branch, :, group * width : (group + 1) * width
-                ]
+                copy = pltpu.make_async_copy(
+                    ref.at[branch, :, pl.ds(group * width, width)],
+                    out_ref.at[2 * group + branch, :, pl.ds(at * width, width)],
+                    sem.at[len(copies)],
+                )
+                copy.start()
+                copies.append(copy)
+    for copy in copies:
+        copy.wait()
 
 
 def pack(q, k, v, groups):
@@ -38,9 +45,10 @@
     return pl.pallas_call(
         functools.partial(pack_kernel, groups),
         out_shape=jax.ShapeDtypeStruct((2 * groups, rows, 3 * width), q.dtype),
-        in_specs=[VM] * 3,
+        in_specs=[pl.BlockSpec(memory_space=pl.ANY)] * 3,
         out_specs=VM,
-        compiler_params=params(2 * VMEM_LIMIT),
+        scratch_shapes=[pltpu.SemaphoreType.DMA((6 * groups,))],
+        compiler_params=params(58 * 1024 * 1024),
     )(q, k, v)
 
 
@@ -121,14 +129,8 @@
     return whole[0:rows], whole[rows:]
 
 
-def block_kernel(heads, n_q, n_kv, n_text, *refs):
-    refs = list(refs)
-    q_refs, kvs = [refs.pop(0) for _ in range(n_q)], [refs.pop(0) for _ in range(n_kv)]
-    text_refs = [[refs.pop(0) for _ in range(n)] for n in n_text]
-    refs.pop(0)
-    out_ref = refs.pop(0)
+def attend(heads, q, kvs, out_ref):
     rows = out_ref.shape[0] - 16
-    q, _ = take_block(q_refs, rows)
 
     def front(head):
         scores = [nt(q[:, head_cols(head)], kv[:, head_cols(head)]) for kv in kvs]
@@ -151,27 +153,41 @@
         out_ref[0:rows, head_cols(head)] = (acc / total).astype(jnp.bfloat16)
         logs.append(shift + jnp.log2(total))
     write_stats(out_ref, rows, logs)
-    for i, parts in enumerate(text_refs):
-        refs[-1][i] = take_block(parts, rows)[1]
-
-
-def block_attention(q, kvs, rows, heads, after, text_from=()):
+
+
+def block_kernel(heads, n_q, n_kv, n_text, n_after, *refs):
+    refs = list(refs)
+    blocks = [[refs.pop(0) for _ in range(n)] for n in n_q]
+    kvs = [refs.pop(0) for _ in range(n_kv)]
+    texts = [[refs.pop(0) for _ in range(n)] for n in n_text]
+    for _ in range(n_after):
+        refs.pop(0)
+    for block in blocks:
+        out_ref = refs.pop(0)
+        attend(heads, take_block(block, out_ref.shape[0] - 16)[0], kvs, out_ref)
+    for i, parts in enumerate(texts):
+        refs[0][i] = take_block(parts, kvs[0].shape[0])[1]
+
+
+def block_attention(blocks, kvs, rows, heads, after, text_from=()):
     keys = sum(kv.shape[0] for kv in kvs)
-    out = [jax.ShapeDtypeStruct((rows + 16, heads * HD), jnp.bfloat16)]
+    out = [jax.ShapeDtypeStruct((rows + 16, heads * HD), jnp.bfloat16)] * len(blocks)
     if text_from:
         extra = sum(x.shape[0] for x in text_from[0]) - rows
         out.append(jax.ShapeDtypeStruct((len(text_from), extra, heads * HD), jnp.bfloat16))
-    args = [*q, *kvs, *(x for block in text_from for x in block), after]
-    return pl.pallas_call(
-        functools.partial(block_kernel, heads, len(q), len(kvs), tuple(len(block) for block in text_from)),
+    args = [x for block in blocks for x in block] + kvs + [x for block in text_from for x in block] + list(after)
+    return pl.pallas_call(
+        functools.partial(
+            block_kernel, heads, [len(b) for b in blocks], len(kvs), [len(b) for b in text_from], len(after)
+        ),
         out_shape=out,
         in_specs=[VM] * len(args),
         out_specs=[VM] * len(out),
         compiler_params=params(),
         cost_estimate=pl.CostEstimate(
-            flops=4 * heads * rows * HD * keys,
+            flops=4 * len(blocks) * heads * rows * HD * keys,
             bytes_accessed=4 * keys * heads * HD,
-            transcendentals=heads * rows * keys,
+            transcendentals=len(blocks) * heads * rows * keys,
         ),
     )(*args)
 
@@ -290,11 +306,9 @@
     qs = {0: [q]} | gather_ring(q, "z_hi", n_z)
     kvs = [kv] + [piece for block in gather_ring(kv, "y", n_y).values() for piece in block]
     flags = shared_flags.reshape(1, -1)
-    parts, before = [], flags
-    for s in (1, 3, 2):
-        before = block_attention(qs[s], kvs, rows, heads, before)[0]
-        parts.append(lax.ppermute(before, "z_hi", ring(n_z, n_z - s)))
-    own, text = block_attention(qs[0], kvs, rows, heads, before, [qs[i] for i in range(n_z)])
+    near = block_attention([qs[1], qs[3]], kvs, rows, heads, [])
+    far, own, text = block_attention([qs[2], qs[0]], kvs, rows, heads, near, [qs[i] for i in range(n_z)])
+    parts = [lax.ppermute(x, "z_hi", ring(n_z, n_z - s)) for s, x in ((1, near[0]), (3, near[1]), (2, far))]
     text = lax.all_gather(text, "y")
     values = lax.all_gather(text[:, :, text.shape[2] // 2 :], "core")
     txt_part, lent = text_attention(place, replace_cols, q, text, values, flags, rows, heads)

time: 113 us -> 111 us (0.982)
  local copies, waits for them, and re-layouts: 5.82 us -> 2.97 us
    unnamed x15 -> x9, local copies, waits for them, and re-layouts: 4.27 us -> 1.41 us
    pallas_call x1, Pallas kernels: 1.01 us -> 2.48 us  [pack(): pl.pallas_call(functools.partial(pack_kernel, groups), out_shape=jax.Shap...]
    pallas_call x4 -> x2, Pallas kernels: 12.5 us -> 11.8 us  [block_attention(): pl.pallas_call(functools.partial(block_kernel, heads, [len(b) for b in bl...]
where the time goes in v3:
time: 111 us; the launch traced here: 110 us
  starting transfers between devices  32.3 us (29%)
  blocking collectives  30.4 us (27%)
  waiting for transfers between devices  25.9 us (23%)
  Pallas kernels  18.4 us (17%)
  local copies, waits for them, and re-layouts  2.97 us (3%)
    all_gather x1, blocking collectives, body(): text = lax.all_gather(text, 'y')  12.4 us
    all_to_all x1, waiting for transfers between devices, body(): held = lax.all_to_all(packed, axes, split_axis=0, concat_axis=0, tiled=True)  12.1 us
    pallas_call x2, Pallas kernels, block_attention(): pl.pallas_call(functools.partial(block_kernel, heads, [len(b) for b in bl...  11.8 us
    all_to_all x1, blocking collectives, body(): back = lax.all_to_all(result, axes, split_axis=0, concat_axis=0, tiled=True)  11.3 us
    ppermute x4, waiting for transfers between devices, gather_ring(): near = {s: lax.ppermute(x, axis, ring(n, s)) for s in (1, n - 1)}  9.88 us
    ppermute x3, starting transfers between devices, body(): lax.ppermute(x, 'z_hi', ring(n_z, n_z - s))  8.53 us
    ppermute x4, starting transfers between devices, gather_ring(): near = {s: lax.ppermute(x, axis, ring(n, s)) for s in (1, n - 1)}  7.94 us
    all_to_all x1, starting transfers between devices, body(): held = lax.all_to_all(packed, axes, split_axis=0, concat_axis=0, tiled=True)  7.18 us
  transfers between devices with their start and end apart: 14, of which 7 were waited for; matrix products, arithmetic and copies ran while one was open for 1% of the time, Pallas kernels for 13%

profile of v3, /device:TPU:1, one launch (start us, length us, event | category | flops | bytes accessed | tf_op | source)
XLA Modules:
  0.0 110.3 jit_solution(3944960965656595531)
XLA Ops:
  0.0 2.5 %shard_map.73 = bf16[16,24,1152]{2,1,0:T(8,128)(2,1)} custom-call(bf16[2,24,3072]{2,1,0:T(8,128)(2,1)} %q_ref.1, bf16[2,24,3072]{2,1,0:T(8,128)(2,1)} %k_ref.1, bf16[2,24,3072]{2,1,0:T(8,128)(2,1)} %v_ref.1), custom_call_target="tpu_custom_call" | custom-call | tf_op jit(solution)/shard_map/pallas_call | solution.py:45
  2.5 7.2 %all-to-all-start = ((bf16[16,24,1152]{2,1,0:T(8,128)(2,1)}), bf16[16,24,1152]{2,1,0:T(8,128)(2,1)S(1)}, u32[]{:S(2)}, u32[]{:S(2)}) async-start(bf16[16,24,1152]{2,1,0:T(8,128)(2,1)} %shard_map.73), calls=%async_computation | async-start | bytes 1769472 | tf_op jit(solution)/shard_map/all_to_all | solution.py:302
  9.7 0.7 copy-done.3
  10.4 0.1 collective-permute-start
  10.5 1.1 %collective-permute-done.other_ref = bf16[4,16,384]{2,1,0:T(8,128)(2,1)S(1)} collective-permute-done((bf16[4,16,384]{2,1,0:T(8,128)(2,1)S(1)}, bf16[4,16,384]{2,1,0:T(8,128)(2,1)S(1)}, u32[]{:S(2)}, u32[]{:S(2)}) %collective-permute-start) | collective-permute-done | bytes 49184 | tf_op jit(solution)/shard_map/ppermute | solution.py:300
  11.7 12.1 %all-to-all-done = bf16[16,24,1152]{2,1,0:T(8,128)(2,1)S(1)} async-done(((bf16[16,24,1152]{2,1,0:T(8,128)(2,1)}), bf16[16,24,1152]{2,1,0:T(8,128)(2,1)S(1)}, u32[]{:S(2)}, u32[]{:S(2)}) %all-to-all-start) | async-done | bytes 884768 | tf_op jit(solution)/shard_map/all_to_all | solution.py:302
  23.8 2.8 %collective-permute-start.7 = (bf16[384,768]{1,0:T(8,128)(2,1)S(1)}, bf16[384,768]{1,0:T(8,128)(2,1)S(1)}, u32[]{:S(2)}, u32[]{:S(2)}) collective-permute-start(bf16[384,768]{1,0:T(8,128)(2,1)S(1)} %get-tuple-element.17.refs_2_.refs_3_), channel_id=1, source_target_pairs={{0,192},{64,0},{128,64},{192,128},{1,193},{65,1},{129,65},{193,129... | collective-permute-start | bytes 1769480 | tf_op jit(solution)/shard_map/ppermute | solution.py:284
  26.6 5.1 %collective-permute-start.3 = (bf16[448,384]{1,0:T(8,128)(2,1)S(1)}, bf16[448,384]{1,0:T(8,128)(2,1)S(1)}, u32[]{:S(2)}, u32[]{:S(2)}) collective-permute-start(bf16[448,384]{1,0:T(8,128)(2,1)S(1)} %get-tuple-element.16.refs_2_.refs_8_.q_ref), channel_id=1, source_target_pairs={{0,48},{16,0},{32,16},{48,32},{1,49},{17,1},{33,17},{49,33},{2,50}... | collective-permute-start | bytes 1032200 | tf_op jit(solution)/shard_map/ppermute | solution.py:284
  31.7 6.6 %collective-permute-done.7.refs_6_.refs_7_ = bf16[384,768]{1,0:T(8,128)(2,1)S(1)} collective-permute-done((bf16[384,768]{1,0:T(8,128)(2,1)S(1)}, bf16[384,768]{1,0:T(8,128)(2,1)S(1)}, u32[]{:S(2)}, u32[]{:S(2)}) %collective-permute-start.7) | collective-permute-done | bytes 589856 | tf_op jit(solution)/shard_map/ppermute | solution.py:284
  38.4 0.7 slice.23
  39.1 3.4 %collective-permute-start.8 = (bf16[192,768]{1,0:T(8,128)(2,1)}, bf16[192,768]{1,0:T(8,128)(2,1)S(1)}, u32[]{:S(2)}, u32[]{:S(2)}) collective-permute-start(bf16[192,768]{1,0:T(8,128)(2,1)} %slice.23), channel_id=1, source_target_pairs={{0,192},{64,0},{128,64},{192,128},{1,193},{65,1},{129,65},{193,129... | collective-permute-start | bytes 884744 | tf_op jit(solution)/shard_map/ppermute | solution.py:288
  42.5 0.7 slice.22
  43.3 2.3 %collective-permute-done.3.refs_1_.refs_12_ = bf16[448,384]{1,0:T(8,128)(2,1)S(1)} collective-permute-done((bf16[448,384]{1,0:T(8,128)(2,1)S(1)}, bf16[448,384]{1,0:T(8,128)(2,1)S(1)}, u32[]{:S(2)}, u32[]{:S(2)}) %collective-permute-start.3) | collective-permute-done | bytes 344096 | tf_op jit(solution)/shard_map/ppermute | solution.py:284
  45.6 3.6 %collective-permute-start.4 = (bf16[224,384]{1,0:T(8,128)(2,1)S(1)}, bf16[224,384]{1,0:T(8,128)(2,1)S(1)}, u32[]{:S(2)}, u32[]{:S(2)}) collective-permute-start(bf16[224,384]{1,0:T(8,128)(2,1)S(1)} %slice.21), channel_id=1, source_target_pairs={{0,48},{16,0},{32,16},{48,32},{1,49},{17,1},{33,17},{49,33},{2,50}... | collective-permute-start | bytes 516104 | tf_op jit(solution)/shard_map/ppermute | solution.py:288
  49.1 1.0 collective-permute-done.1.refs_0_.refs_9_
  50.1 0.3 collective-permute-start.2
  50.4 0.1 pad_add_fusion.place_ref
  50.5 0.7 collective-permute-done.6.refs_4_.refs_5_
  51.1 5.9 %shard_map.75 = (bf16[400,384]{1,0:T(8,128)(2,1)S(1)}, bf16[400,384]{1,0:T(8,128)(2,1)S(1)}) custom-call(bf16[448,384]{1,0:T(8,128)(2,1)S(1)} %collective-permute-done.1.refs_0_.refs_9_, bf16[448,384]{1,0:T(8,128)(2,1)S(1)} %collective-permute-done.3.refs_1_.refs_12_, bf16[384,768]{1,0:T(8,128)(2,1)S(1)} %get-tuple-element.17.refs_2_.refs_3_, ...), custom_call_target="tpu_custom_call" | custom-call | flops 1811939328 | bytes 2359296 | tf_op jit(solution)/shard_map/pallas_call | solution.py:179
  57.0 5.2 %collective-permute-start.9 = (bf16[400,384]{1,0:T(8,128)(2,1)S(1)}, bf16[400,384]{1,0:T(8,128)(2,1)S(1)}, u32[]{:S(2)}, u32[]{:S(2)}) collective-permute-start(bf16[400,384]{1,0:T(8,128)(2,1)S(1)} %get-tuple-element.18.refs_13_), channel_id=1, source_target_pairs={{0,48},{16,0},{32,16},{48,32},{1,49},{17,1},{33,17},{49,33},{2,50}... | collective-permute-start | bytes 921608 | tf_op jit(solution)/shard_map/ppermute | solution.py:311
  62.2 5.9 %shard_map.76 = (bf16[400,384]{1,0:T(8,128)(2,1)S(1)}, bf16[400,384]{1,0:T(8,128)(2,1)S(1)}, bf16[4,64,384]{2,1,0:T(8,128)(2,1)S(1)}) custom-call(bf16[224,384]{1,0:T(8,128)(2,1)S(1)} %collective-permute-done.2.refs_0_.refs_10_, bf16[224,384]{1,0:T(8,128)(2,1)S(1)} %collective-permute-done.4.refs_1_.refs_11_, ...), custom_call_target="tpu_custom_call" | custom-call | flops 1811939328 | bytes 2359296 | tf_op jit(solution)/shard_map/pallas_call | solution.py:179
  68.1 3.3 %collective-permute-start.11 = (bf16[400,384]{1,0:T(8,128)(2,1)S(1)}, bf16[400,384]{1,0:T(8,128)(2,1)S(1)}, u32[]{:S(2)}, u32[]{:S(2)}) collective-permute-start(bf16[400,384]{1,0:T(8,128)(2,1)S(1)} %get-tuple-element.21), channel_id=1, source_target_pairs={{0,32},{16,48},{32,0},{48,16},{1,33},{17,49},{33,1},{49,17},{2,34}... | collective-permute-start | bytes 921608 | tf_op jit(solution)/shard_map/ppermute | solution.py:311
  71.5 12.4 %all-gather = bf16[16,64,384]{2,1,0:T(8,128)(2,1)S(1)} all-gather(bf16[4,64,384]{2,1,0:T(8,128)(2,1)S(1)} %get-tuple-element.22), channel_id=2, replica_groups=mesh['y'=4,'z_hi'=4,'core'=2,'z_lo'=2,'x'=4] {'y'}, dimensions={0}, use_global_device_ids=true | all-gather | bytes 983040 | tf_op jit(solution)/shard_map/all_gather | solution.py:312
  83.9 6.8 %all-gather.1 = bf16[8,4,32,384]{3,2,1,0:T(8,128)(2,1)S(1)} all-gather(bf16[4,4,32,384]{3,2,1,0:T(8,128)(2,1)S(1)} %slice.24), channel_id=3, replica_groups=mesh['y'=4,'z_hi'=4,'core'=2,'z_lo'=2,'x'=4] {'core'}, dimensions={0}, use_global_device_ids=true | all-gather | bytes 1179648 | tf_op jit(solution)/shard_map/all_gather | solution.py:313
  90.6 0.7 copy-done
  91.3 2.5 %shard_map.77 = (bf16[400,384]{1,0:T(8,128)(2,1)S(1)}, bf16[384,384]{1,0:T(8,128)(2,1)S(1)}) custom-call(s32[2]{0:T(128)S(1)} %pad_add_fusion.place_ref, s32[8]{0:T(128)S(1)} %copy-done.1, bf16[448,384]{1,0:T(8,128)(2,1)S(1)} %get-tuple-element.16.refs_2_.refs_8_.q_ref, bf16[4,4,64,384]{3,2,1,0:T(8,128)(2,1)S(1)} %bitcast.8, ...), custom_call_target="tpu_custom_call" | custom-call | flops 452984832 | bytes 1179648 | tf_op jit(solution)/shard_map/pallas_call | solution.py:229
  93.8 0.9 shard_map.78
  94.7 1.3 %collective-permute-start.12 = (bf16[384,384]{1,0:T(8,128)(2,1)S(1)}, bf16[384,384]{1,0:T(8,128)(2,1)S(1)}, u32[]{:S(2)}, u32[]{:S(2)}) collective-permute-start(bf16[384,384]{1,0:T(8,128)(2,1)S(1)} %get-tuple-element.26), channel_id=1, source_target_pairs={{0,8},{1,9},{2,10},{3,11},{4,12},{5,13},{6,14},{7,15},{16,24},{17,... | collective-permute-start | bytes 884744 | tf_op jit(solution)/shard_map/ppermute | solution.py:316
  96.0 2.2 %collective-permute-done.12 = bf16[384,384]{1,0:T(8,128)(2,1)S(1)} collective-permute-done((bf16[384,384]{1,0:T(8,128)(2,1)S(1)}, bf16[384,384]{1,0:T(8,128)(2,1)S(1)}, u32[]{:S(2)}, u32[]{:S(2)}) %collective-permute-start.12) | collective-permute-done | bytes 294944 | tf_op jit(solution)/shard_map/ppermute | solution.py:316
  98.2 0.1 add_convert_fusion
  98.3 11.3 %all_to_all.10.in_ref = bf16[16,24,384]{2,1,0:T(8,128)(2,1)S(1)} all-to-all(bf16[16,24,384]{2,1,0:T(8,128)(2,1)S(1)} %bitcast.12), channel_id=1, replica_groups=mesh['y'=4,'z_hi'=4,'core'=2,'z_lo'=2,'x'=4] {'z_lo','x','core'}, dimensions={0} | all-to-all | bytes 589824 | tf_op jit(solution)/shard_map/all_to_all | solution.py:319
  109.5 0.7 shard_map.79
  (23 shorter events, 0.2 us)
Async XLA Ops:
  2.5 7.2 %copy-start.2 = (bf16[2,16,384]{2,1,0:T(8,128)(2,1)S(1)}, bf16[2,16,384]{2,1,0:T(8,128)(2,1)}, u32[]{:S(2)}) copy-start(bf16[2,16,384]{2,1,0:T(8,128)(2,1)} %param.10) | copy-start | bytes 73732
  2.5 21.2 %all-to-all-start = ((bf16[16,24,1152]{2,1,0:T(8,128)(2,1)}), bf16[16,24,1152]{2,1,0:T(8,128)(2,1)S(1)}, u32[]{:S(2)}, u32[]{:S(2)}) async-start(bf16[16,24,1152]{2,1,0:T(8,128)(2,1)} %shard_map.73), calls=%async_computation | async-start | bytes 1769472 | tf_op jit(solution)/shard_map/all_to_all | solution.py:302
  9.7 0.7 copy-start.3
  10.4 1.2 %collective-permute-start = (bf16[4,16,384]{2,1,0:T(8,128)(2,1)S(1)}, bf16[4,16,384]{2,1,0:T(8,128)(2,1)S(1)}, u32[]{:S(2)}, u32[]{:S(2)}) collective-permute-start(bf16[4,16,384]{2,1,0:T(8,128)(2,1)S(1)} %constant_dynamic-update-slice_fusion.own_ref), channel_id=1, source_target_pairs={{0,8},{8,0},{1,9},{9,1},{2,10},{10,2},{3,11},{11,3},{4,12},{12,4},... | collective-permute-start | bytes 147464 | tf_op jit(solution)/shard_map/ppermute | solution.py:300
  23.8 14.6 %collective-permute-start.7 = (bf16[384,768]{1,0:T(8,128)(2,1)S(1)}, bf16[384,768]{1,0:T(8,128)(2,1)S(1)}, u32[]{:S(2)}, u32[]{:S(2)}) collective-permute-start(bf16[384,768]{1,0:T(8,128)(2,1)S(1)} %get-tuple-element.17.refs_2_.refs_3_), channel_id=1, source_target_pairs={{0,192},{64,0},{128,64},{192,128},{1,193},{65,1},{129,65},{193,129... | collective-permute-start | bytes 1769480 | tf_op jit(solution)/shard_map/ppermute | solution.py:284
  26.6 15.9 %collective-permute-start.5 = (bf16[384,768]{1,0:T(8,128)(2,1)S(1)}, bf16[384,768]{1,0:T(8,128)(2,1)S(1)}, u32[]{:S(2)}, u32[]{:S(2)}) collective-permute-start(bf16[384,768]{1,0:T(8,128)(2,1)S(1)} %get-tuple-element.17.refs_2_.refs_3_), channel_id=1, source_target_pairs={{0,64},{64,128},{128,192},{192,0},{1,65},{65,129},{129,193},{193,1... | collective-permute-start | bytes 1769480 | tf_op jit(solution)/shard_map/ppermute | solution.py:284
  26.6 18.9 %collective-permute-start.3 = (bf16[448,384]{1,0:T(8,128)(2,1)S(1)}, bf16[448,384]{1,0:T(8,128)(2,1)S(1)}, u32[]{:S(2)}, u32[]{:S(2)}) collective-permute-start(bf16[448,384]{1,0:T(8,128)(2,1)S(1)} %get-tuple-element.16.refs_2_.refs_8_.q_ref), channel_id=1, source_target_pairs={{0,48},{16,0},{32,16},{48,32},{1,49},{17,1},{33,17},{49,33},{2,50}... | collective-permute-start | bytes 1032200 | tf_op jit(solution)/shard_map/ppermute | solution.py:284
  31.7 18.4 %collective-permute-start.1 = (bf16[448,384]{1,0:T(8,128)(2,1)S(1)}, bf16[448,384]{1,0:T(8,128)(2,1)S(1)}, u32[]{:S(2)}, u32[]{:S(2)}) collective-permute-start(bf16[448,384]{1,0:T(8,128)(2,1)S(1)} %get-tuple-element.16.refs_2_.refs_8_.q_ref), channel_id=1, source_target_pairs={{0,16},{16,32},{32,48},{48,0},{1,17},{17,33},{33,49},{49,1},{2,18}... | collective-permute-start | bytes 1032200 | tf_op jit(solution)/shard_map/ppermute | solution.py:284
  39.1 11.4 %collective-permute-start.8 = (bf16[192,768]{1,0:T(8,128)(2,1)}, bf16[192,768]{1,0:T(8,128)(2,1)S(1)}, u32[]{:S(2)}, u32[]{:S(2)}) collective-permute-start(bf16[192,768]{1,0:T(8,128)(2,1)} %slice.23), channel_id=1, source_target_pairs={{0,192},{64,0},{128,64},{192,128},{1,193},{65,1},{129,65},{193,129... | collective-permute-start | bytes 884744 | tf_op jit(solution)/shard_map/ppermute | solution.py:288
  43.3 7.9 %collective-permute-start.6 = (bf16[192,768]{1,0:T(8,128)(2,1)}, bf16[192,768]{1,0:T(8,128)(2,1)S(1)}, u32[]{:S(2)}, u32[]{:S(2)}) collective-permute-start(bf16[192,768]{1,0:T(8,128)(2,1)} %slice.22), channel_id=1, source_target_pairs={{0,64},{64,128},{128,192},{192,0},{1,65},{65,129},{129,193},{193,1... | collective-permute-start | bytes 884744 | tf_op jit(solution)/shard_map/ppermute | solution.py:287
  45.6 16.7 %collective-permute-start.4 = (bf16[224,384]{1,0:T(8,128)(2,1)S(1)}, bf16[224,384]{1,0:T(8,128)(2,1)S(1)}, u32[]{:S(2)}, u32[]{:S(2)}) collective-permute-start(bf16[224,384]{1,0:T(8,128)(2,1)S(1)} %slice.21), channel_id=1, source_target_pairs={{0,48},{16,0},{32,16},{48,32},{1,49},{17,1},{33,17},{49,33},{2,50}... | collective-permute-start | bytes 516104 | tf_op jit(solution)/shard_map/ppermute | solution.py:288
  50.1 12.1 %collective-permute-start.2 = (bf16[224,384]{1,0:T(8,128)(2,1)S(1)}, bf16[224,384]{1,0:T(8,128)(2,1)S(1)}, u32[]{:S(2)}, u32[]{:S(2)}) collective-permute-start(bf16[224,384]{1,0:T(8,128)(2,1)S(1)} %slice.20), channel_id=1, source_target_pairs={{0,16},{16,32},{32,48},{48,0},{1,17},{17,33},{33,49},{49,1},{2,18}... | collective-permute-start | bytes 516104 | tf_op jit(solution)/shard_map/ppermute | solution.py:287
  57.0 36.8 %collective-permute-start.9 = (bf16[400,384]{1,0:T(8,128)(2,1)S(1)}, bf16[400,384]{1,0:T(8,128)(2,1)S(1)}, u32[]{:S(2)}, u32[]{:S(2)}) collective-permute-start(bf16[400,384]{1,0:T(8,128)(2,1)S(1)} %get-tuple-element.18.refs_13_), channel_id=1, source_target_pairs={{0,48},{16,0},{32,16},{48,32},{1,49},{17,1},{33,17},{49,33},{2,50}... | collective-permute-start | bytes 921608 | tf_op jit(solution)/shard_map/ppermute | solution.py:311
  62.2 31.6 %collective-permute-start.10 = (bf16[400,384]{1,0:T(8,128)(2,1)S(1)}, bf16[400,384]{1,0:T(8,128)(2,1)S(1)}, u32[]{:S(2)}, u32[]{:S(2)}) collective-permute-start(bf16[400,384]{1,0:T(8,128)(2,1)S(1)} %get-tuple-element.19.refs_14_), channel_id=1, source_target_pairs={{0,16},{16,32},{32,48},{48,0},{1,17},{17,33},{33,49},{49,1},{2,18}... | collective-permute-start | bytes 921608 | tf_op jit(solution)/shard_map/ppermute | solution.py:311
  68.1 25.6 %collective-permute-start.11 = (bf16[400,384]{1,0:T(8,128)(2,1)S(1)}, bf16[400,384]{1,0:T(8,128)(2,1)S(1)}, u32[]{:S(2)}, u32[]{:S(2)}) collective-permute-start(bf16[400,384]{1,0:T(8,128)(2,1)S(1)} %get-tuple-element.21), channel_id=1, source_target_pairs={{0,32},{16,48},{32,0},{48,16},{1,33},{17,49},{33,1},{49,17},{2,34}... | collective-permute-start | bytes 921608 | tf_op jit(solution)/shard_map/ppermute | solution.py:311
  90.6 0.7 copy-start
  90.6 0.7 copy-start.1
  94.7 3.5 %collective-permute-start.12 = (bf16[384,384]{1,0:T(8,128)(2,1)S(1)}, bf16[384,384]{1,0:T(8,128)(2,1)S(1)}, u32[]{:S(2)}, u32[]{:S(2)}) collective-permute-start(bf16[384,384]{1,0:T(8,128)(2,1)S(1)} %get-tuple-element.26), channel_id=1, source_target_pairs={{0,8},{1,9},{2,10},{3,11},{4,12},{5,13},{6,14},{7,15},{16,24},{17,... | collective-permute-start | bytes 884744 | tf_op jit(solution)/shard_map/ppermute | solution.py:316

commit v4 on v3

--- a/solution.py
+++ b/solution.py
@@ -69,12 +69,13 @@
     )(x)
 
 
-def split_kernel(core_ref, held_ref, own_ref, other_ref, q_ref, kv_ref):
+def split_kernel(core_ref, held_ref, own_ref, other_ref, q_ref, k_ref, v_ref):
     rows, width = held_ref.shape[0], q_ref.shape[1]
     per = own_ref.shape[1]
     core = core_ref[0]
     q_ref[0:rows, :] = held_ref[:, 0:width]
-    kv_ref[...] = held_ref[:, width : 3 * width]
+    k_ref[...] = held_ref[:, width : 2 * width]
+    v_ref[...] = held_ref[:, 2 * width : 3 * width]
     for i, source in enumerate((core, 2 + core)):
         for ref, c in ((own_ref, core), (other_ref, 1 - core)):
             here = pl.ds(pl.multiple_of(rows + 2 * per * i + c * per, per), per)
@@ -87,10 +88,11 @@
         split_kernel,
         out_shape=(
             jax.ShapeDtypeStruct((rows + 4 * own.shape[1], width), held.dtype),
-            jax.ShapeDtypeStruct((rows, 2 * width), held.dtype),
+            jax.ShapeDtypeStruct((rows, width), held.dtype),
+            jax.ShapeDtypeStruct((rows, width), held.dtype),
         ),
         in_specs=[SM] + [VM] * 3,
-        out_specs=(VM, VM),
+        out_specs=(VM, VM, VM),
         compiler_params=params(),
     )(core, held, own, other)
 
@@ -129,11 +131,11 @@
     return whole[0:rows], whole[rows:]
 
 
-def attend(heads, q, kvs, out_ref):
+def attend(heads, q, keys, values, out_ref):
     rows = out_ref.shape[0] - 16
 
     def front(head):
-        scores = [nt(q[:, head_cols(head)], kv[:, head_cols(head)]) for kv in kvs]
+        scores = [nt(q[:, head_cols(head)], k[:, head_cols(head)]) for k in keys]
         top = scores[0].max(axis=-1, keepdims=True)
         for s in scores[1:]:
             top = jnp.maximum(top, s.max(axis=-1, keepdims=True))
@@ -146,48 +148,49 @@
         if head + 1 < heads:
             ahead = front(head + 1)
         total = acc = 0.0
-        for s, kv in zip(scores, kvs):
+        for s, v in zip(scores, values):
             w = jnp.exp2(s * SCALE2 - shift)
             total = total + w.sum(axis=-1, keepdims=True)
-            acc = acc + nn(w.astype(jnp.bfloat16), kv[:, head_cols(head, heads)])
+            acc = acc + nn(w.astype(jnp.bfloat16), v[:, head_cols(head)])
         out_ref[0:rows, head_cols(head)] = (acc / total).astype(jnp.bfloat16)
         logs.append(shift + jnp.log2(total))
     write_stats(out_ref, rows, logs)
 
 
-def block_kernel(heads, n_q, n_kv, n_text, n_after, *refs):
+def block_kernel(heads, n_q, n_keys, n_text, n_after, *refs):
     refs = list(refs)
     blocks = [[refs.pop(0) for _ in range(n)] for n in n_q]
-    kvs = [refs.pop(0) for _ in range(n_kv)]
+    keys = [refs.pop(0) for _ in range(n_keys)]
+    values = [refs.pop(0) for _ in range(n_keys)]
     texts = [[refs.pop(0) for _ in range(n)] for n in n_text]
     for _ in range(n_after):
         refs.pop(0)
     for block in blocks:
         out_ref = refs.pop(0)
-        attend(heads, take_block(block, out_ref.shape[0] - 16)[0], kvs, out_ref)
+        attend(heads, take_block(block, out_ref.shape[0] - 16)[0], keys, values, out_ref)
     for i, parts in enumerate(texts):
-        refs[0][i] = take_block(parts, kvs[0].shape[0])[1]
-
-
-def block_attention(blocks, kvs, rows, heads, after, text_from=()):
-    keys = sum(kv.shape[0] for kv in kvs)
+        refs[0][i] = take_block(parts, keys[0].shape[0])[1]
+
+
+def block_attention(blocks, keys, values, rows, heads, after, text_from=()):
+    n_keys = sum(k.shape[0] for k in keys)
     out = [jax.ShapeDtypeStruct((rows + 16, heads * HD), jnp.bfloat16)] * len(blocks)
     if text_from:
         extra = sum(x.shape[0] for x in text_from[0]) - rows
         out.append(jax.ShapeDtypeStruct((len(text_from), extra, heads * HD), jnp.bfloat16))
-    args = [x for block in blocks for x in block] + kvs + [x for block in text_from for x in block] + list(after)
+    args = [x for block in blocks for x in block] + keys + values + [x for block in text_from for x in block] + list(after)
     return pl.pallas_call(
         functools.partial(
-            block_kernel, heads, [len(b) for b in blocks], len(kvs), [len(b) for b in text_from], len(after)
+            block_kernel, heads, [len(b) for b in blocks], len(keys), [len(b) for b in text_from], len(after)
         ),
         out_shape=out,
         in_specs=[VM] * len(args),
         out_specs=[VM] * len(out),
         compiler_params=params(),
         cost_estimate=pl.CostEstimate(
-            flops=4 * len(blocks) * heads * rows * HD * keys,
-            bytes_accessed=4 * keys * heads * HD,
-            transcendentals=len(blocks) * heads * rows * keys,
+            flops=4 * len(blocks) * heads * rows * HD * n_keys,
+            bytes_accessed=4 * n_keys * heads * HD,
+            transcendentals=len(blocks) * heads * rows * n_keys,
         ),
     )(*args)
 
@@ -302,12 +305,16 @@
     held = lax.all_to_all(packed, axes, split_axis=0, concat_axis=0, tiled=True)
     rows = held.shape[0] * held.shape[1]
     place = jnp.stack([lax.axis_index(a) for a in ("z_hi", "core")]).astype(jnp.int32)
-    q, kv = split(place[1:], held.reshape(rows, 3 * width), own_text, other_text)
+    q, k, v = split(place[1:], held.reshape(rows, 3 * width), own_text, other_text)
     qs = {0: [q]} | gather_ring(q, "z_hi", n_z)
-    kvs = [kv] + [piece for block in gather_ring(kv, "y", n_y).values() for piece in block]
+    up, down = ring(n_y, 1), ring(n_y, n_y - 1)
+    keys = [k, lax.ppermute(k, "y", up), lax.ppermute(k, "y", down)]
+    values = [v, lax.ppermute(v, "y", up), lax.ppermute(v, "y", down)]
+    keys.append(lax.ppermute(keys[1], "y", up))
+    values.append(lax.ppermute(values[2], "y", down))
     flags = shared_flags.reshape(1, -1)
-    near = block_attention([qs[1], qs[3]], kvs, rows, heads, [])
-    far, own, text = block_attention([qs[2], qs[0]], kvs, rows, heads, near, [qs[i] for i in range(n_z)])
+    near = block_attention([qs[1], qs[3]], keys, values, rows, heads, [])
+    far, own, text = block_attention([qs[2], qs[0]], keys, values, rows, heads, near, [qs[i] for i in range(n_z)])
     parts = [lax.ppermute(x, "z_hi", ring(n_z, n_z - s)) for s, x in ((1, near[0]), (3, near[1]), (2, far))]
     text = lax.all_gather(text, "y")
     values = lax.all_gather(text[:, :, text.shape[2] // 2 :], "core")

time: 111 us -> 109 us (0.982)
  waiting for transfers between devices: 25.9 us -> 28.1 us
  blocking collectives: 30.4 us -> 28.4 us
  local copies, waits for them, and re-layouts: 2.97 us -> 1.5 us
    ppermute x0 -> x6, starting transfers between devices: none -> 8.2 us  [the longest x2 2.76 us: body(): keys = [k, lax.ppermute(k, 'y', up), lax.ppermute(k, 'y', down)]]
    ppermute x2 -> x1, starting transfers between devices: 6.99 us -> 0.67 us  [gather_ring(): lax.ppermute(near[n - 1][half:], axis, ring(n, n - 1))]
    ppermute x0 -> x6, waiting for transfers between devices: none -> 4.49 us  [the longest x2 4.48 us: body(): keys = [k, lax.ppermute(k, 'y', up), lax.ppermute(k, 'y', down)]]
    ppermute x4 -> x2, starting transfers between devices: 7.94 us -> 5.2 us  [gather_ring(): near = {s: lax.ppermute(x, axis, ring(n, s)) for s in (1, n - 1)}]
    ppermute x3, starting transfers between devices: 8.53 us -> 6.6 us  [body(): lax.ppermute(x, 'z_hi', ring(n_z, n_z - s))]
    ppermute x2 -> x1, starting transfers between devices: 0.27 us -> 1.96 us  [gather_ring(): lax.ppermute(near[1][:half], axis, ring(n, 1))]
    ppermute x4 -> x2, waiting for transfers between devices: 9.88 us -> 8.2 us  [gather_ring(): near = {s: lax.ppermute(x, axis, ring(n, s)) for s in (1, n - 1)}]
  transfers between devices with their start and end apart: 14 -> 16, of which waited for: 7 -> 6; matrix products, arithmetic and copies ran while one was open for 1% -> 0% of each run, Pallas kernels for 13% -> 14%
where the time goes in v4:
time: 109 us
  starting transfers between devices  31.2 us (29%)
  blocking collectives  28.4 us (26%)
  waiting for transfers between devices  28.1 us (26%)
  Pallas kernels  19.1 us (18%)
  local copies, waits for them, and re-layouts  1.5 us (1%)
    pallas_call x2, Pallas kernels, block_attention(): pl.pallas_call(functools.partial(block_kernel, heads, [len(b) for b in bl...  12.5 us
    all_gather x1, blocking collectives, body(): text = lax.all_gather(text, 'y')  12.1 us
    all_to_all x1, waiting for transfers between devices, body(): held = lax.all_to_all(packed, axes, split_axis=0, concat_axis=0, tiled=True)  12.1 us
    all_to_all x1, blocking collectives, body(): back = lax.all_to_all(result, axes, split_axis=0, concat_axis=0, tiled=True)  10.4 us
    ppermute x2, waiting for transfers between devices, gather_ring(): near = {s: lax.ppermute(x, axis, ring(n, s)) for s in (1, n - 1)}  8.2 us
    all_to_all x1, starting transfers between devices, body(): held = lax.all_to_all(packed, axes, split_axis=0, concat_axis=0, tiled=True)  7.18 us
    ppermute x3, starting transfers between devices, body(): lax.ppermute(x, 'z_hi', ring(n_z, n_z - s))  6.6 us
    all_gather x1, blocking collectives, body(): values = lax.all_gather(text[:, :, text.shape[2] // 2:], 'core')  5.89 us
  transfers between devices with their start and end apart: 16, of which 6 were waited for; matrix products, arithmetic and copies ran while one was open for 0% of the time, Pallas kernels for 14%

profile of v4, /device:TPU:1, one launch (start us, length us, event | category | flops | bytes accessed | tf_op | source)
XLA Modules:
  0.0 108.6 jit_solution(2248252415543928512)
XLA Ops:
  0.0 2.5 %shard_map.73 = bf16[16,24,1152]{2,1,0:T(8,128)(2,1)} custom-call(bf16[2,24,3072]{2,1,0:T(8,128)(2,1)} %q_ref.1, bf16[2,24,3072]{2,1,0:T(8,128)(2,1)} %k_ref.1, bf16[2,24,3072]{2,1,0:T(8,128)(2,1)} %v_ref.1), custom_call_target="tpu_custom_call" | custom-call | tf_op jit(solution)/shard_map/pallas_call | solution.py:45
  2.5 7.2 %all-to-all-start = ((bf16[16,24,1152]{2,1,0:T(8,128)(2,1)}), bf16[16,24,1152]{2,1,0:T(8,128)(2,1)S(1)}, u32[]{:S(2)}, u32[]{:S(2)}) async-start(bf16[16,24,1152]{2,1,0:T(8,128)(2,1)} %shard_map.73), calls=%async_computation | async-start | bytes 1769472 | tf_op jit(solution)/shard_map/all_to_all | solution.py:305
  9.7 0.7 copy-done.3
  10.4 0.1 collective-permute-start
  10.5 1.1 %collective-permute-done.other_ref = bf16[4,16,384]{2,1,0:T(8,128)(2,1)S(1)} collective-permute-done((bf16[4,16,384]{2,1,0:T(8,128)(2,1)S(1)}, bf16[4,16,384]{2,1,0:T(8,128)(2,1)S(1)}, u32[]{:S(2)}, u32[]{:S(2)}) %collective-permute-start) | collective-permute-done | bytes 49184 | tf_op jit(solution)/shard_map/ppermute | solution.py:303
  11.7 12.1 %all-to-all-done = bf16[16,24,1152]{2,1,0:T(8,128)(2,1)S(1)} async-done(((bf16[16,24,1152]{2,1,0:T(8,128)(2,1)}), bf16[16,24,1152]{2,1,0:T(8,128)(2,1)S(1)}, u32[]{:S(2)}, u32[]{:S(2)}) %all-to-all-start) | async-done | bytes 884768 | tf_op jit(solution)/shard_map/all_to_all | solution.py:305
  23.7 0.1 shard_map.74
  23.8 5.2 %collective-permute-start.3 = (bf16[448,384]{1,0:T(8,128)(2,1)S(1)}, bf16[448,384]{1,0:T(8,128)(2,1)S(1)}, u32[]{:S(2)}, u32[]{:S(2)}) collective-permute-start(bf16[448,384]{1,0:T(8,128)(2,1)S(1)} %get-tuple-element.17.refs_2_.refs_11_.q_ref), channel_id=1, source_target_pairs={{0,48},{16,0},{32,16},{48,32},{1,49},{17,1},{33,17},{49,33},{2,50}... | collective-permute-start | bytes 1032200 | tf_op jit(solution)/shard_map/ppermute | solution.py:287
  29.0 1.3 %collective-permute-start.5 = (bf16[384,384]{1,0:T(8,128)(2,1)S(1)}, bf16[384,384]{1,0:T(8,128)(2,1)S(1)}, u32[]{:S(2)}, u32[]{:S(2)}) collective-permute-start(bf16[384,384]{1,0:T(8,128)(2,1)S(1)} %get-tuple-element.18.refs_2_.refs_3_), channel_id=1, source_target_pairs={{0,64},{64,128},{128,192},{192,0},{1,65},{65,129},{129,193},{193,1... | collective-permute-start | bytes 884744 | tf_op jit(solution)/shard_map/ppermute | solution.py:311
  30.3 1.4 %collective-permute-start.9 = (bf16[384,384]{1,0:T(8,128)(2,1)S(1)}, bf16[384,384]{1,0:T(8,128)(2,1)S(1)}, u32[]{:S(2)}, u32[]{:S(2)}) collective-permute-start(bf16[384,384]{1,0:T(8,128)(2,1)S(1)} %get-tuple-element.19.refs_6_.refs_7_), channel_id=1, source_target_pairs={{0,192},{64,0},{128,64},{192,128},{1,193},{65,1},{129,65},{193,129... | collective-permute-start | bytes 884744 | tf_op jit(solution)/shard_map/ppermute | solution.py:312
  31.8 1.5 %collective-permute-start.6 = (bf16[384,384]{1,0:T(8,128)(2,1)S(1)}, bf16[384,384]{1,0:T(8,128)(2,1)S(1)}, u32[]{:S(2)}, u32[]{:S(2)}) collective-permute-start(bf16[384,384]{1,0:T(8,128)(2,1)S(1)} %get-tuple-element.18.refs_2_.refs_3_), channel_id=1, source_target_pairs={{0,192},{64,0},{128,64},{192,128},{1,193},{65,1},{129,65},{193,129... | collective-permute-start | bytes 884744 | tf_op jit(solution)/shard_map/ppermute | solution.py:311
  33.2 4.5 %collective-permute-done.5.refs_3_.refs_4_ = bf16[384,384]{1,0:T(8,128)(2,1)S(1)} collective-permute-done((bf16[384,384]{1,0:T(8,128)(2,1)S(1)}, bf16[384,384]{1,0:T(8,128)(2,1)S(1)}, u32[]{:S(2)}, u32[]{:S(2)}) %collective-permute-start.5) | collective-permute-done | bytes 294944 | tf_op jit(solution)/shard_map/ppermute | solution.py:311
  37.7 1.3 %collective-permute-start.7 = (bf16[384,384]{1,0:T(8,128)(2,1)S(1)}, bf16[384,384]{1,0:T(8,128)(2,1)S(1)}, u32[]{:S(2)}, u32[]{:S(2)}) collective-permute-start(bf16[384,384]{1,0:T(8,128)(2,1)S(1)} %collective-permute-done.5.refs_3_.refs_4_), channel_id=1, source_target_pairs={{0,64},{64,128},{128,192},{192,0},{1,65},{65,129},{129,193},{193,1... | collective-permute-start | bytes 884744 | tf_op jit(solution)/shard_map/ppermute | solution.py:313
  39.0 3.9 %collective-permute-done.3.refs_1_.refs_15_ = bf16[448,384]{1,0:T(8,128)(2,1)S(1)} collective-permute-done((bf16[448,384]{1,0:T(8,128)(2,1)S(1)}, bf16[448,384]{1,0:T(8,128)(2,1)S(1)}, u32[]{:S(2)}, u32[]{:S(2)}) %collective-permute-start.3) | collective-permute-done | bytes 344096 | tf_op jit(solution)/shard_map/ppermute | solution.py:287
  42.8 2.7 %collective-permute-start.10 = (bf16[384,384]{1,0:T(8,128)(2,1)S(1)}, bf16[384,384]{1,0:T(8,128)(2,1)}, u32[]{:S(2)}, u32[]{:S(2)}) collective-permute-start(bf16[384,384]{1,0:T(8,128)(2,1)S(1)} %collective-permute-done.9.refs_8_.refs_9_), channel_id=1, source_target_pairs={{0,192},{64,0},{128,64},{192,128},{1,193},{65,1},{129,65},{193,129... | collective-permute-start | bytes 884744 | tf_op jit(solution)/shard_map/ppermute | solution.py:314
  45.6 4.3 %collective-permute-done.1.refs_0_.refs_12_ = bf16[448,384]{1,0:T(8,128)(2,1)S(1)} collective-permute-done((bf16[448,384]{1,0:T(8,128)(2,1)S(1)}, bf16[448,384]{1,0:T(8,128)(2,1)S(1)}, u32[]{:S(2)}, u32[]{:S(2)}) %collective-permute-start.1) | collective-permute-done | bytes 344096 | tf_op jit(solution)/shard_map/ppermute | solution.py:287
  49.9 0.7 collective-permute-start.4
  50.6 2.0 %collective-permute-start.2 = (bf16[224,384]{1,0:T(8,128)(2,1)S(1)}, bf16[224,384]{1,0:T(8,128)(2,1)S(1)}, u32[]{:S(2)}, u32[]{:S(2)}) collective-permute-start(bf16[224,384]{1,0:T(8,128)(2,1)S(1)} %slice.12), channel_id=1, source_target_pairs={{0,16},{16,32},{32,48},{48,0},{1,17},{17,33},{33,49},{49,1},{2,18}... | collective-permute-start | bytes 516104 | tf_op jit(solution)/shard_map/ppermute | solution.py:290
  52.7 6.2 %shard_map.75 = (bf16[400,384]{1,0:T(8,128)(2,1)S(1)}, bf16[400,384]{1,0:T(8,128)(2,1)S(1)}) custom-call(bf16[448,384]{1,0:T(8,128)(2,1)S(1)} %collective-permute-done.1.refs_0_.refs_12_, bf16[448,384]{1,0:T(8,128)(2,1)S(1)} %collective-permute-done.3.refs_1_.refs_15_, bf16[384,384]{1,0:T(8,128)(2,1)S(1)} %get-tuple-element.18.refs_2_.refs_3_, ...), custom_call_target="tpu_custom_call" | custom-call | flops 1811939328 | bytes 2359296 | tf_op jit(solution)/shard_map/pallas_call | solution.py:182
  58.9 1.9 %collective-permute-start.11 = (bf16[400,384]{1,0:T(8,128)(2,1)S(1)}, bf16[400,384]{1,0:T(8,128)(2,1)S(1)}, u32[]{:S(2)}, u32[]{:S(2)}) collective-permute-start(bf16[400,384]{1,0:T(8,128)(2,1)S(1)} %get-tuple-element.20.refs_16_), channel_id=1, source_target_pairs={{0,48},{16,0},{32,16},{48,32},{1,49},{17,1},{33,17},{49,33},{2,50}... | collective-permute-start | bytes 921608 | tf_op jit(solution)/shard_map/ppermute | solution.py:318
  60.8 0.7 collective-permute-start.12
  61.6 6.3 %shard_map.76 = (bf16[400,384]{1,0:T(8,128)(2,1)S(1)}, bf16[400,384]{1,0:T(8,128)(2,1)S(1)}, bf16[4,64,384]{2,1,0:T(8,128)(2,1)S(1)}) custom-call(bf16[224,384]{1,0:T(8,128)(2,1)S(1)} %collective-permute-done.2.refs_0_.refs_13_, bf16[224,384]{1,0:T(8,128)(2,1)S(1)} %collective-permute-done.4.refs_1_.refs_14_, ...), custom_call_target="tpu_custom_call" | custom-call | flops 1811939328 | bytes 2359296 | tf_op jit(solution)/shard_map/pallas_call | solution.py:182
  67.9 3.9 %collective-permute-start.13 = (bf16[400,384]{1,0:T(8,128)(2,1)S(1)}, bf16[400,384]{1,0:T(8,128)(2,1)S(1)}, u32[]{:S(2)}, u32[]{:S(2)}) collective-permute-start(bf16[400,384]{1,0:T(8,128)(2,1)S(1)} %get-tuple-element.23), channel_id=1, source_target_pairs={{0,32},{16,48},{32,0},{48,16},{1,33},{17,49},{33,1},{49,17},{2,34}... | collective-permute-start | bytes 921608 | tf_op jit(solution)/shard_map/ppermute | solution.py:318
  71.8 12.1 %all-gather = bf16[16,64,384]{2,1,0:T(8,128)(2,1)S(1)} all-gather(bf16[4,64,384]{2,1,0:T(8,128)(2,1)S(1)} %get-tuple-element.24), channel_id=2, replica_groups=mesh['y'=4,'z_hi'=4,'core'=2,'z_lo'=2,'x'=4] {'y'}, dimensions={0}, use_global_device_ids=true | all-gather | bytes 983040 | tf_op jit(solution)/shard_map/all_gather | solution.py:319
  84.0 5.9 %all-gather.1 = bf16[8,4,32,384]{3,2,1,0:T(8,128)(2,1)S(1)} all-gather(bf16[4,4,32,384]{3,2,1,0:T(8,128)(2,1)S(1)} %slice.14), channel_id=3, replica_groups=mesh['y'=4,'z_hi'=4,'core'=2,'z_lo'=2,'x'=4] {'core'}, dimensions={0}, use_global_device_ids=true | all-gather | bytes 1179648 | tf_op jit(solution)/shard_map/all_gather | solution.py:320
  89.9 0.7 copy-done
  90.6 2.5 %shard_map.77 = (bf16[400,384]{1,0:T(8,128)(2,1)S(1)}, bf16[384,384]{1,0:T(8,128)(2,1)S(1)}) custom-call(s32[2]{0:T(128)S(1)} %pad_add_fusion.place_ref, s32[8]{0:T(128)S(1)} %copy-done.1, bf16[448,384]{1,0:T(8,128)(2,1)S(1)} %get-tuple-element.17.refs_2_.refs_11_.q_ref, bf16[4,4,64,384]{3,2,1,0:T(8,128)(2,1)S(1)} %bitcast.8, ...), custom_call_target="tpu_custom_call" | custom-call | flops 452984832 | bytes 1179648 | tf_op jit(solution)/shard_map/pallas_call | solution.py:232
  93.1 0.9 shard_map.78
  93.9 1.3 %collective-permute-start.14 = (bf16[384,384]{1,0:T(8,128)(2,1)S(1)}, bf16[384,384]{1,0:T(8,128)(2,1)S(1)}, u32[]{:S(2)}, u32[]{:S(2)}) collective-permute-start(bf16[384,384]{1,0:T(8,128)(2,1)S(1)} %get-tuple-element.28), channel_id=1, source_target_pairs={{0,8},{1,9},{2,10},{3,11},{4,12},{5,13},{6,14},{7,15},{16,24},{17,... | collective-permute-start | bytes 884744 | tf_op jit(solution)/shard_map/ppermute | solution.py:323
  95.2 2.2 %collective-permute-done.14 = bf16[384,384]{1,0:T(8,128)(2,1)S(1)} collective-permute-done((bf16[384,384]{1,0:T(8,128)(2,1)S(1)}, bf16[384,384]{1,0:T(8,128)(2,1)S(1)}, u32[]{:S(2)}, u32[]{:S(2)}) %collective-permute-start.14) | collective-permute-done | bytes 294944 | tf_op jit(solution)/shard_map/ppermute | solution.py:323
  97.5 10.4 %all_to_all.10.in_ref = bf16[16,24,384]{2,1,0:T(8,128)(2,1)S(1)} all-to-all(bf16[16,24,384]{2,1,0:T(8,128)(2,1)S(1)} %bitcast.12), channel_id=1, replica_groups=mesh['y'=4,'z_hi'=4,'core'=2,'z_lo'=2,'x'=4] {'z_lo','x','core'}, dimensions={0} | all-to-all | bytes 589824 | tf_op jit(solution)/shard_map/all_to_all | solution.py:326
  107.9 0.7 shard_map.79
  (25 shorter events, 0.3 us)
Async XLA Ops:
  2.5 7.2 %copy-start.2 = (bf16[2,16,384]{2,1,0:T(8,128)(2,1)S(1)}, bf16[2,16,384]{2,1,0:T(8,128)(2,1)}, u32[]{:S(2)}) copy-start(bf16[2,16,384]{2,1,0:T(8,128)(2,1)} %param.10) | copy-start | bytes 73732
  2.5 21.2 %all-to-all-start = ((bf16[16,24,1152]{2,1,0:T(8,128)(2,1)}), bf16[16,24,1152]{2,1,0:T(8,128)(2,1)S(1)}, u32[]{:S(2)}, u32[]{:S(2)}) async-start(bf16[16,24,1152]{2,1,0:T(8,128)(2,1)} %shard_map.73), calls=%async_computation | async-start | bytes 1769472 | tf_op jit(solution)/shard_map/all_to_all | solution.py:305
  9.7 0.7 copy-start.3
  10.4 1.2 %collective-permute-start = (bf16[4,16,384]{2,1,0:T(8,128)(2,1)S(1)}, bf16[4,16,384]{2,1,0:T(8,128)(2,1)S(1)}, u32[]{:S(2)}, u32[]{:S(2)}) collective-permute-start(bf16[4,16,384]{2,1,0:T(8,128)(2,1)S(1)} %constant_dynamic-update-slice_fusion.own_ref), channel_id=1, source_target_pairs={{0,8},{8,0},{1,9},{9,1},{2,10},{10,2},{3,11},{11,3},{4,12},{12,4},... | collective-permute-start | bytes 147464 | tf_op jit(solution)/shard_map/ppermute | solution.py:303
  23.8 19.0 %collective-permute-start.3 = (bf16[448,384]{1,0:T(8,128)(2,1)S(1)}, bf16[448,384]{1,0:T(8,128)(2,1)S(1)}, u32[]{:S(2)}, u32[]{:S(2)}) collective-permute-start(bf16[448,384]{1,0:T(8,128)(2,1)S(1)} %get-tuple-element.17.refs_2_.refs_11_.q_ref), channel_id=1, source_target_pairs={{0,48},{16,0},{32,16},{48,32},{1,49},{17,1},{33,17},{49,33},{2,50}... | collective-permute-start | bytes 1032200 | tf_op jit(solution)/shard_map/ppermute | solution.py:287
  29.0 8.7 %collective-permute-start.5 = (bf16[384,384]{1,0:T(8,128)(2,1)S(1)}, bf16[384,384]{1,0:T(8,128)(2,1)S(1)}, u32[]{:S(2)}, u32[]{:S(2)}) collective-permute-start(bf16[384,384]{1,0:T(8,128)(2,1)S(1)} %get-tuple-element.18.refs_2_.refs_3_), channel_id=1, source_target_pairs={{0,64},{64,128},{128,192},{192,0},{1,65},{65,129},{129,193},{193,1... | collective-permute-start | bytes 884744 | tf_op jit(solution)/shard_map/ppermute | solution.py:311
  30.3 7.4 %collective-permute-start.9 = (bf16[384,384]{1,0:T(8,128)(2,1)S(1)}, bf16[384,384]{1,0:T(8,128)(2,1)S(1)}, u32[]{:S(2)}, u32[]{:S(2)}) collective-permute-start(bf16[384,384]{1,0:T(8,128)(2,1)S(1)} %get-tuple-element.19.refs_6_.refs_7_), channel_id=1, source_target_pairs={{0,192},{64,0},{128,64},{192,128},{1,193},{65,1},{129,65},{193,129... | collective-permute-start | bytes 884744 | tf_op jit(solution)/shard_map/ppermute | solution.py:312
  31.8 18.2 %collective-permute-start.1 = (bf16[448,384]{1,0:T(8,128)(2,1)S(1)}, bf16[448,384]{1,0:T(8,128)(2,1)S(1)}, u32[]{:S(2)}, u32[]{:S(2)}) collective-permute-start(bf16[448,384]{1,0:T(8,128)(2,1)S(1)} %get-tuple-element.17.refs_2_.refs_11_.q_ref), channel_id=1, source_target_pairs={{0,16},{16,32},{32,48},{48,0},{1,17},{17,33},{33,49},{49,1},{2,18}... | collective-permute-start | bytes 1032200 | tf_op jit(solution)/shard_map/ppermute | solution.py:287
  31.8 18.9 %collective-permute-start.6 = (bf16[384,384]{1,0:T(8,128)(2,1)S(1)}, bf16[384,384]{1,0:T(8,128)(2,1)S(1)}, u32[]{:S(2)}, u32[]{:S(2)}) collective-permute-start(bf16[384,384]{1,0:T(8,128)(2,1)S(1)} %get-tuple-element.18.refs_2_.refs_3_), channel_id=1, source_target_pairs={{0,192},{64,0},{128,64},{192,128},{1,193},{65,1},{129,65},{193,129... | collective-permute-start | bytes 884744 | tf_op jit(solution)/shard_map/ppermute | solution.py:311
  37.7 15.0 %collective-permute-start.8 = (bf16[384,384]{1,0:T(8,128)(2,1)S(1)}, bf16[384,384]{1,0:T(8,128)(2,1)S(1)}, u32[]{:S(2)}, u32[]{:S(2)}) collective-permute-start(bf16[384,384]{1,0:T(8,128)(2,1)S(1)} %get-tuple-element.19.refs_6_.refs_7_), channel_id=1, source_target_pairs={{0,64},{64,128},{128,192},{192,0},{1,65},{65,129},{129,193},{193,1... | collective-permute-start | bytes 884744 | tf_op jit(solution)/shard_map/ppermute | solution.py:312
  37.7 15.0 %collective-permute-start.7 = (bf16[384,384]{1,0:T(8,128)(2,1)S(1)}, bf16[384,384]{1,0:T(8,128)(2,1)S(1)}, u32[]{:S(2)}, u32[]{:S(2)}) collective-permute-start(bf16[384,384]{1,0:T(8,128)(2,1)S(1)} %collective-permute-done.5.refs_3_.refs_4_), channel_id=1, source_target_pairs={{0,64},{64,128},{128,192},{192,0},{1,65},{65,129},{129,193},{193,1... | collective-permute-start | bytes 884744 | tf_op jit(solution)/shard_map/ppermute | solution.py:313
  42.8 9.8 %collective-permute-start.10 = (bf16[384,384]{1,0:T(8,128)(2,1)S(1)}, bf16[384,384]{1,0:T(8,128)(2,1)}, u32[]{:S(2)}, u32[]{:S(2)}) collective-permute-start(bf16[384,384]{1,0:T(8,128)(2,1)S(1)} %collective-permute-done.9.refs_8_.refs_9_), channel_id=1, source_target_pairs={{0,192},{64,0},{128,64},{192,128},{1,193},{65,1},{129,65},{193,129... | collective-permute-start | bytes 884744 | tf_op jit(solution)/shard_map/ppermute | solution.py:314
  49.9 11.7 %collective-permute-start.4 = (bf16[224,384]{1,0:T(8,128)(2,1)S(1)}, bf16[224,384]{1,0:T(8,128)(2,1)S(1)}, u32[]{:S(2)}, u32[]{:S(2)}) collective-permute-start(bf16[224,384]{1,0:T(8,128)(2,1)S(1)} %slice.13), channel_id=1, source_target_pairs={{0,48},{16,0},{32,16},{48,32},{1,49},{17,1},{33,17},{49,33},{2,50}... | collective-permute-start | bytes 516104 | tf_op jit(solution)/shard_map/ppermute | solution.py:291
  50.6 11.0 %collective-permute-start.2 = (bf16[224,384]{1,0:T(8,128)(2,1)S(1)}, bf16[224,384]{1,0:T(8,128)(2,1)S(1)}, u32[]{:S(2)}, u32[]{:S(2)}) collective-permute-start(bf16[224,384]{1,0:T(8,128)(2,1)S(1)} %slice.12), channel_id=1, source_target_pairs={{0,16},{16,32},{32,48},{48,0},{1,17},{17,33},{33,49},{49,1},{2,18}... | collective-permute-start | bytes 516104 | tf_op jit(solution)/shard_map/ppermute | solution.py:290
  58.9 34.1 %collective-permute-start.11 = (bf16[400,384]{1,0:T(8,128)(2,1)S(1)}, bf16[400,384]{1,0:T(8,128)(2,1)S(1)}, u32[]{:S(2)}, u32[]{:S(2)}) collective-permute-start(bf16[400,384]{1,0:T(8,128)(2,1)S(1)} %get-tuple-element.20.refs_16_), channel_id=1, source_target_pairs={{0,48},{16,0},{32,16},{48,32},{1,49},{17,1},{33,17},{49,33},{2,50}... | collective-permute-start | bytes 921608 | tf_op jit(solution)/shard_map/ppermute | solution.py:318
  60.8 32.2 %collective-permute-start.12 = (bf16[400,384]{1,0:T(8,128)(2,1)S(1)}, bf16[400,384]{1,0:T(8,128)(2,1)S(1)}, u32[]{:S(2)}, u32[]{:S(2)}) collective-permute-start(bf16[400,384]{1,0:T(8,128)(2,1)S(1)} %get-tuple-element.21.refs_17_), channel_id=1, source_target_pairs={{0,16},{16,32},{32,48},{48,0},{1,17},{17,33},{33,49},{49,1},{2,18}... | collective-permute-start | bytes 921608 | tf_op jit(solution)/shard_map/ppermute | solution.py:318
  67.9 25.2 %collective-permute-start.13 = (bf16[400,384]{1,0:T(8,128)(2,1)S(1)}, bf16[400,384]{1,0:T(8,128)(2,1)S(1)}, u32[]{:S(2)}, u32[]{:S(2)}) collective-permute-start(bf16[400,384]{1,0:T(8,128)(2,1)S(1)} %get-tuple-element.23), channel_id=1, source_target_pairs={{0,32},{16,48},{32,0},{48,16},{1,33},{17,49},{33,1},{49,17},{2,34}... | collective-permute-start | bytes 921608 | tf_op jit(solution)/shard_map/ppermute | solution.py:318
  89.9 0.7 copy-start
  89.9 0.7 copy-start.1
  93.9 3.5 %collective-permute-start.14 = (bf16[384,384]{1,0:T(8,128)(2,1)S(1)}, bf16[384,384]{1,0:T(8,128)(2,1)S(1)}, u32[]{:S(2)}, u32[]{:S(2)}) collective-permute-start(bf16[384,384]{1,0:T(8,128)(2,1)S(1)} %get-tuple-element.28), channel_id=1, source_target_pairs={{0,8},{1,9},{2,10},{3,11},{4,12},{5,13},{6,14},{7,15},{16,24},{17,... | collective-permute-start | bytes 884744 | tf_op jit(solution)/shard_map/ppermute | solution.py:323

commit v5 on v4

--- a/solution.py
+++ b/solution.py
@@ -14,6 +14,7 @@
 LOG2E = 1.4426950408889634
 SCALE2 = LOG2E / math.sqrt(HD)
 VMEM_LIMIT = 24 * 1024 * 1024
+PACK_LIMIT = 58 * 1024 * 1024
 
 VM = pl.BlockSpec(memory_space=pltpu.VMEM)
 SM = pl.BlockSpec(memory_space=pltpu.SMEM)
@@ -23,21 +24,14 @@
     return pltpu.CompilerParams(vmem_limit_bytes=limit)
 
 
-def pack_kernel(groups, q_ref, k_ref, v_ref, out_ref, sem):
+def pack_kernel(groups, q_ref, k_ref, v_ref, out_ref):
     width = q_ref.shape[2] // groups
-    copies = []
     for group in range(groups):
         for branch in range(2):
             for at, ref in enumerate((q_ref, k_ref, v_ref)):
-                copy = pltpu.make_async_copy(
-                    ref.at[branch, :, pl.ds(group * width, width)],
-                    out_ref.at[2 * group + branch, :, pl.ds(at * width, width)],
-                    sem.at[len(copies)],
-                )
-                copy.start()
-                copies.append(copy)
-    for copy in copies:
-        copy.wait()
+                out_ref[2 * group + branch, :, at * width : (at + 1) * width] = ref[
+                    branch, :, group * width : (group + 1) * width
+                ]
 
 
 def pack(q, k, v, groups):
@@ -45,10 +39,9 @@
     return pl.pallas_call(
         functools.partial(pack_kernel, groups),
         out_shape=jax.ShapeDtypeStruct((2 * groups, rows, 3 * width), q.dtype),
-        in_specs=[pl.BlockSpec(memory_space=pl.ANY)] * 3,
+        in_specs=[VM] * 3,
         out_specs=VM,
-        scratch_shapes=[pltpu.SemaphoreType.DMA((6 * groups,))],
-        compiler_params=params(58 * 1024 * 1024),
+        compiler_params=params(PACK_LIMIT),
     )(q, k, v)
 
 
@@ -131,33 +124,57 @@
     return whole[0:rows], whole[rows:]
 
 
-def attend(heads, q, keys, values, out_ref):
-    rows = out_ref.shape[0] - 16
-
-    def front(head):
-        scores = [nt(q[:, head_cols(head)], k[:, head_cols(head)]) for k in keys]
+def attend(heads, qs, keys, values, outs):
+    rows = keys[0].shape[0]
+
+    def front(block, head):
+        q = qs[block][:, head_cols(head)]
+        scores = [nt(q, k[:, head_cols(head)]) for k in keys]
         top = scores[0].max(axis=-1, keepdims=True)
         for s in scores[1:]:
             top = jnp.maximum(top, s.max(axis=-1, keepdims=True))
         return scores, top * SCALE2
 
-    ahead = front(0)
+    items = [(block, head) for block in range(len(qs)) for head in range(heads)]
+    ahead = front(*items[0])
     logs = []
-    for head in range(heads):
+    for n, (block, head) in enumerate(items):
         scores, shift = ahead
-        if head + 1 < heads:
-            ahead = front(head + 1)
+        if n + 1 < len(items):
+            ahead = front(*items[n + 1])
         total = acc = 0.0
         for s, v in zip(scores, values):
             w = jnp.exp2(s * SCALE2 - shift)
             total = total + w.sum(axis=-1, keepdims=True)
             acc = acc + nn(w.astype(jnp.bfloat16), v[:, head_cols(head)])
-        out_ref[0:rows, head_cols(head)] = (acc / total).astype(jnp.bfloat16)
+        outs[block][0:rows, head_cols(head)] = (acc / total).astype(jnp.bfloat16)
         logs.append(shift + jnp.log2(total))
-    write_stats(out_ref, rows, logs)
-
-
-def block_kernel(heads, n_q, n_keys, n_text, n_after, *refs):
+        if head + 1 == heads:
+            write_stats(outs[block], rows, logs[-heads:])
+
+
+def log_of(n):
+    return n.bit_length() - 1
+
+
+def write_mask(n_z, z, cols_ref, flags_ref, mask_ref):
+    txt = flags_ref.shape[1]
+    columns = lax.broadcasted_iota(jnp.int32, (1, txt), 1)
+    listed = flags_ref[...] == 1
+    for i in range(cols_ref.shape[0]):
+        listed = jnp.logical_or(listed, columns == cols_ref[i])
+    mask = jnp.broadcast_to(listed.astype(jnp.float32), (16, txt)).astype(jnp.bfloat16)
+    per = txt // (n_z * n_z)
+    place = lax.broadcasted_iota(jnp.int32, (txt, txt), 1)
+    pair = lax.shift_right_logical(place, log_of(per))
+    steps = jnp.bitwise_and(pair, n_z - 1)
+    pair = pair - steps + jnp.bitwise_and(z + n_z - steps, n_z - 1)
+    column = pair * per + jnp.bitwise_and(place, per - 1)
+    chosen = lax.broadcasted_iota(jnp.int32, (txt, txt), 0) == column
+    mask_ref[...] = nn(mask, chosen.astype(jnp.float32).astype(jnp.bfloat16))[0:1]
+
+
+def block_kernel(heads, n_q, n_keys, n_text, n_after, with_mask, *refs):
     refs = list(refs)
     blocks = [[refs.pop(0) for _ in range(n)] for n in n_q]
     keys = [refs.pop(0) for _ in range(n_keys)]
@@ -165,26 +182,40 @@
     texts = [[refs.pop(0) for _ in range(n)] for n in n_text]
     for _ in range(n_after):
         refs.pop(0)
-    for block in blocks:
-        out_ref = refs.pop(0)
-        attend(heads, take_block(block, out_ref.shape[0] - 16)[0], keys, values, out_ref)
+    if with_mask:
+        place_ref, cols_ref, flags_ref = [refs.pop(0) for _ in range(3)]
+        write_mask(4, place_ref[0], cols_ref, flags_ref, refs[-1])
+    rows = keys[0].shape[0]
+    attend(heads, [take_block(block, rows)[0] for block in blocks], keys, values, refs[: len(blocks)])
     for i, parts in enumerate(texts):
-        refs[0][i] = take_block(parts, keys[0].shape[0])[1]
-
-
-def block_attention(blocks, keys, values, rows, heads, after, text_from=()):
+        text = take_block(parts, rows)[1]
+        half = text.shape[0] // 2
+        refs[-1][0, i] = text[:half]
+        refs[-1][1, i] = text[half:]
+
+
+def block_attention(blocks, keys, values, rows, heads, after, text_from=(), mask_from=()):
     n_keys = sum(k.shape[0] for k in keys)
     out = [jax.ShapeDtypeStruct((rows + 16, heads * HD), jnp.bfloat16)] * len(blocks)
     if text_from:
-        extra = sum(x.shape[0] for x in text_from[0]) - rows
-        out.append(jax.ShapeDtypeStruct((len(text_from), extra, heads * HD), jnp.bfloat16))
-    args = [x for block in blocks for x in block] + keys + values + [x for block in text_from for x in block] + list(after)
+        half = (sum(x.shape[0] for x in text_from[0]) - rows) // 2
+        out.append(jax.ShapeDtypeStruct((2, len(text_from), half, heads * HD), jnp.bfloat16))
+    if mask_from:
+        out.append(jax.ShapeDtypeStruct(mask_from[2].shape, jnp.float32))
+    args = [x for block in blocks for x in block] + keys + values + [x for block in text_from for x in block]
+    args += list(after)
     return pl.pallas_call(
         functools.partial(
-            block_kernel, heads, [len(b) for b in blocks], len(keys), [len(b) for b in text_from], len(after)
+            block_kernel,
+            heads,
+            [len(b) for b in blocks],
+            len(keys),
+            [len(b) for b in text_from],
+            len(after),
+            bool(mask_from),
         ),
         out_shape=out,
-        in_specs=[VM] * len(args),
+        in_specs=[VM] * len(args) + [SM, SM, VM][: len(mask_from)],
         out_specs=[VM] * len(out),
         compiler_params=params(),
         cost_estimate=pl.CostEstimate(
@@ -192,59 +223,57 @@
             bytes_accessed=4 * n_keys * heads * HD,
             transcendentals=len(blocks) * heads * rows * n_keys,
         ),
-    )(*args)
-
-
-def text_kernel(heads, place_ref, cols_ref, q_ref, text_ref, values_ref, flags_ref, out_ref, lent_ref, kt, vt, vb):
+    )(*args, *mask_from)
+
+
+def text_kernel(heads, core_ref, q_ref, text_ref, values_ref, mask_ref, out_ref, lent_ref):
     rows = lent_ref.shape[0]
-    n_y, n_z, extra, _ = text_ref.shape
-    per, txt = extra // 2, kt.shape[0]
-    z, core = place_ref[0], place_ref[1]
-    for y in range(n_y):
-        for sz in range(n_z):
-            here = pl.ds(pl.multiple_of((y * n_z + lax.rem(z + n_z - sz, n_z)) * per, per), per)
-            kt[here, :] = text_ref[y, sz, 0:per]
-            vt[here, :] = text_ref[y, sz, per : 2 * per]
-            vb[here, :] = values_ref[1, y, sz]
-    columns = lax.broadcasted_iota(jnp.int32, (1, txt), 1)
-    listed = flags_ref[...] == 1
-    for i in range(cols_ref.shape[0]):
-        listed = jnp.logical_or(listed, columns == cols_ref[i])
-    mask = listed.astype(jnp.float32)
-    keep = 1.0 - mask * core.astype(jnp.float32)
+    n_y = text_ref.shape[0]
+    mask = mask_ref[...]
+    keep = 1.0 - mask * core_ref[0].astype(jnp.float32)
+
+    def joined(pieces):
+        return jnp.concatenate([piece.reshape(-1, HD) for piece in pieces], axis=0)
+
+    def front(head):
+        cols = head_cols(head)
+        s = nt(q_ref[0:rows, cols], joined([text_ref[y, 0, :, :, cols] for y in range(n_y)]))
+        return s, s.max(axis=-1, keepdims=True) * SCALE2
+
+    ahead = front(0)
     logs = []
     for head in range(heads):
         cols = head_cols(head)
-        s = nt(q_ref[0:rows, cols], kt[:, cols])
-        shift = s.max(axis=-1, keepdims=True) * SCALE2
+        s, shift = ahead
+        if head + 1 < heads:
+            ahead = front(head + 1)
         w = jnp.exp2(s * SCALE2 - shift)
         total = w.sum(axis=-1, keepdims=True)
-        acc = nn((w * keep).astype(jnp.bfloat16), vt[:, cols])
-        borrow = nn((w * mask).astype(jnp.bfloat16), vb[:, cols])
+        acc = nn((w * keep).astype(jnp.bfloat16), joined([text_ref[y, 1, :, :, cols] for y in range(n_y)]))
+        borrow = nn((w * mask).astype(jnp.bfloat16), joined([values_ref[1, y, :, :, cols] for y in range(n_y)]))
         out_ref[0:rows, cols] = (acc / total).astype(jnp.bfloat16)
         lent_ref[:, cols] = (borrow / total).astype(jnp.bfloat16)
         logs.append(shift + jnp.log2(total))
     write_stats(out_ref, rows, logs)
 
 
-def text_attention(place, replace_cols, q, text, values, flags, rows, heads):
-    txt = text.shape[0] * text.shape[1] * text.shape[2] // 2
+def text_attention(core, q, text, values, mask, rows, heads):
+    txt = mask.shape[1]
     return pl.pallas_call(
         functools.partial(text_kernel, heads),
         out_shape=(
             jax.ShapeDtypeStruct((rows + 16, heads * HD), jnp.bfloat16),
             jax.ShapeDtypeStruct((rows, heads * HD), jnp.bfloat16),
         ),
-        in_specs=[SM, SM] + [VM] * 4,
+        in_specs=[SM] + [VM] * 4,
         out_specs=(VM, VM),
-        scratch_shapes=[pltpu.VMEM((txt, heads * HD), jnp.bfloat16)] * 3,
         compiler_params=params(),
         cost_estimate=pl.CostEstimate(
             flops=6 * heads * rows * HD * txt,
             bytes_accessed=6 * txt * heads * HD,
             transcendentals=heads * rows * txt,
         ),
-    )(place, replace_cols, q, text, values, flags)
+    )(core, q, text, values, mask)
 
 
 def merge_kernel(heads, p0, p1, p2, p3, pt, lent_in, out_ref, lent_ref):
@@ -313,12 +342,15 @@
     keys.append(lax.ppermute(keys[1], "y", up))
     values.append(lax.ppermute(values[2], "y", down))
     flags = shared_flags.reshape(1, -1)
-    near = block_attention([qs[1], qs[3]], keys, values, rows, heads, [])
-    far, own, text = block_attention([qs[2], qs[0]], keys, values, rows, heads, near, [qs[i] for i in range(n_z)])
+    mask_from = (place[:1], replace_cols, flags)
+    *near, mask = block_attention([qs[1], qs[3]], keys, values, rows, heads, [], mask_from=mask_from)
+    far = block_attention([qs[2]], keys, values, rows, heads, near)
+    own, text = block_attention([qs[0]], keys, values, rows, heads, far, [qs[i] for i in range(n_z)])
+    far = far[0]
     parts = [lax.ppermute(x, "z_hi", ring(n_z, n_z - s)) for s, x in ((1, near[0]), (3, near[1]), (2, far))]
     text = lax.all_gather(text, "y")
-    values = lax.all_gather(text[:, :, text.shape[2] // 2 :], "core")
-    txt_part, lent = text_attention(place, replace_cols, q, text, values, flags, rows, heads)
+    values = lax.all_gather(text[:, 1], "core")
+    txt_part, lent = text_attention(place[1:], q, text, values, mask, rows, heads)
     result, lent = merge([own] + parts + [txt_part], lent, heads)
     borrowed = lax.ppermute(lent, "core", [(0, 1)])
     result = (result + borrowed.astype(jnp.float32)).astype(jnp.bfloat16)

time: 109 us -> 109 us (level)
  local copies, waits for them, and re-layouts: 1.5 us -> 2.81 us
    pallas_call x2 -> x3, Pallas kernels: 12.5 us -> 12.9 us  [block_attention(): pl.pallas_call(functools.partial(block_kernel, heads, [len(b) for b in bl...]
  transfers between devices with their start and end apart: 16 -> 16, of which waited for: 6 -> 6; matrix products, arithmetic and copies ran while one was open for 0% -> 1% of each run, Pallas kernels for 14% -> 13%
where the time goes in v5:
time: 109 us; the launch traced here: 108 us
  starting transfers between devices  30.9 us (28%)
  blocking collectives  28.4 us (26%)
  waiting for transfers between devices  27.4 us (25%)
  Pallas kernels  18.2 us (17%)
  local copies, waits for them, and re-layouts  2.81 us (3%)
    pallas_call x3, Pallas kernels, block_attention(): pl.pallas_call(functools.partial(block_kernel, heads, [len(b) for b in bl...  12.9 us
    all_gather x1, blocking collectives, body(): text = lax.all_gather(text, 'y')  12.1 us
    all_to_all x1, waiting for transfers between devices, body(): held = lax.all_to_all(packed, axes, split_axis=0, concat_axis=0, tiled=True)  12.1 us
    all_to_all x1, blocking collectives, body(): back = lax.all_to_all(result, axes, split_axis=0, concat_axis=0, tiled=True)  10.5 us
    ppermute x2, waiting for transfers between devices, gather_ring(): near = {s: lax.ppermute(x, axis, ring(n, s)) for s in (1, n - 1)}  7.54 us
    all_to_all x1, starting transfers between devices, body(): held = lax.all_to_all(packed, axes, split_axis=0, concat_axis=0, tiled=True)  7.3 us
    ppermute x3, starting transfers between devices, body(): lax.ppermute(x, 'z_hi', ring(n_z, n_z - s))  6.48 us
    all_gather x1, blocking collectives, body(): values = lax.all_gather(text[:, 1], 'core')  5.9 us
  transfers between devices with their start and end apart: 16, of which 6 were waited for; matrix products, arithmetic and copies ran while one was open for 1% of the time, Pallas kernels for 13%

profile of v5, /device:TPU:1, one launch (start us, length us, event | category | flops | bytes accessed | tf_op | source)
XLA Modules:
  0.0 108.0 jit_solution(7221909337955858372)
XLA Ops:
  0.0 2.1 %shard_map.73 = bf16[16,24,1152]{2,1,0:T(8,128)(2,1)} custom-call(bf16[2,24,3072]{2,1,0:T(8,128)(2,1)} %q_ref.1, bf16[2,24,3072]{2,1,0:T(8,128)(2,1)} %k_ref.1, bf16[2,24,3072]{2,1,0:T(8,128)(2,1)} %v_ref.1), custom_call_target="tpu_custom_call" | custom-call | tf_op jit(solution)/shard_map/pallas_call | solution.py:39
  2.1 7.3 %all-to-all-start = ((bf16[16,24,1152]{2,1,0:T(8,128)(2,1)}), bf16[16,24,1152]{2,1,0:T(8,128)(2,1)S(1)}, u32[]{:S(2)}, u32[]{:S(2)}) async-start(bf16[16,24,1152]{2,1,0:T(8,128)(2,1)} %shard_map.73), calls=%async_computation | async-start | bytes 1769472 | tf_op jit(solution)/shard_map/all_to_all | solution.py:334
  9.5 0.7 copy-done.3
  10.3 1.1 %collective-permute-done.other_ref = bf16[4,16,384]{2,1,0:T(8,128)(2,1)S(1)} collective-permute-done((bf16[4,16,384]{2,1,0:T(8,128)(2,1)S(1)}, bf16[4,16,384]{2,1,0:T(8,128)(2,1)S(1)}, u32[]{:S(2)}, u32[]{:S(2)}) %collective-permute-start) | collective-permute-done | bytes 49184 | tf_op jit(solution)/shard_map/ppermute | solution.py:332
  11.4 12.1 %all-to-all-done = bf16[16,24,1152]{2,1,0:T(8,128)(2,1)S(1)} async-done(((bf16[16,24,1152]{2,1,0:T(8,128)(2,1)}), bf16[16,24,1152]{2,1,0:T(8,128)(2,1)S(1)}, u32[]{:S(2)}, u32[]{:S(2)}) %all-to-all-start) | async-done | bytes 884768 | tf_op jit(solution)/shard_map/all_to_all | solution.py:334
  23.6 5.2 %collective-permute-start.9 = (bf16[448,384]{1,0:T(8,128)(2,1)S(1)}, bf16[448,384]{1,0:T(8,128)(2,1)S(1)}, u32[]{:S(2)}, u32[]{:S(2)}) collective-permute-start(bf16[448,384]{1,0:T(8,128)(2,1)S(1)} %get-tuple-element.17.refs_0_.refs_9_.q_ref), channel_id=1, source_target_pairs={{0,48},{16,0},{32,16},{48,32},{1,49},{17,1},{33,17},{49,33},{2,50}... | collective-permute-start | bytes 1032200 | tf_op jit(solution)/shard_map/ppermute | solution.py:316
  28.8 1.3 %collective-permute-start.1 = (bf16[384,384]{1,0:T(8,128)(2,1)S(1)}, bf16[384,384]{1,0:T(8,128)(2,1)S(1)}, u32[]{:S(2)}, u32[]{:S(2)}) collective-permute-start(bf16[384,384]{1,0:T(8,128)(2,1)S(1)} %get-tuple-element.18.refs_2_.refs_1_), channel_id=1, source_target_pairs={{0,64},{64,128},{128,192},{192,0},{1,65},{65,129},{129,193},{193,1... | collective-permute-start | bytes 884744 | tf_op jit(solution)/shard_map/ppermute | solution.py:340
  30.1 1.4 %collective-permute-start.5 = (bf16[384,384]{1,0:T(8,128)(2,1)S(1)}, bf16[384,384]{1,0:T(8,128)(2,1)S(1)}, u32[]{:S(2)}, u32[]{:S(2)}) collective-permute-start(bf16[384,384]{1,0:T(8,128)(2,1)S(1)} %get-tuple-element.19.refs_6_.refs_5_), channel_id=1, source_target_pairs={{0,192},{64,0},{128,64},{192,128},{1,193},{65,1},{129,65},{193,129... | collective-permute-start | bytes 884744 | tf_op jit(solution)/shard_map/ppermute | solution.py:341
  31.5 1.5 %collective-permute-start.2 = (bf16[384,384]{1,0:T(8,128)(2,1)S(1)}, bf16[384,384]{1,0:T(8,128)(2,1)S(1)}, u32[]{:S(2)}, u32[]{:S(2)}) collective-permute-start(bf16[384,384]{1,0:T(8,128)(2,1)S(1)} %get-tuple-element.18.refs_2_.refs_1_), channel_id=1, source_target_pairs={{0,192},{64,0},{128,64},{192,128},{1,193},{65,1},{129,65},{193,129... | collective-permute-start | bytes 884744 | tf_op jit(solution)/shard_map/ppermute | solution.py:340
  33.0 4.5 %collective-permute-done.1.refs_3_.refs_2_ = bf16[384,384]{1,0:T(8,128)(2,1)S(1)} collective-permute-done((bf16[384,384]{1,0:T(8,128)(2,1)S(1)}, bf16[384,384]{1,0:T(8,128)(2,1)S(1)}, u32[]{:S(2)}, u32[]{:S(2)}) %collective-permute-start.1) | collective-permute-done | bytes 294944 | tf_op jit(solution)/shard_map/ppermute | solution.py:340
  37.5 1.3 %collective-permute-start.3 = (bf16[384,384]{1,0:T(8,128)(2,1)S(1)}, bf16[384,384]{1,0:T(8,128)(2,1)S(1)}, u32[]{:S(2)}, u32[]{:S(2)}) collective-permute-start(bf16[384,384]{1,0:T(8,128)(2,1)S(1)} %collective-permute-done.1.refs_3_.refs_2_), channel_id=1, source_target_pairs={{0,64},{64,128},{128,192},{192,0},{1,65},{65,129},{129,193},{193,1... | collective-permute-start | bytes 884744 | tf_op jit(solution)/shard_map/ppermute | solution.py:342
  38.7 3.9 %collective-permute-done.9.refs_1_.refs_13_ = bf16[448,384]{1,0:T(8,128)(2,1)S(1)} collective-permute-done((bf16[448,384]{1,0:T(8,128)(2,1)S(1)}, bf16[448,384]{1,0:T(8,128)(2,1)S(1)}, u32[]{:S(2)}, u32[]{:S(2)}) %collective-permute-start.9) | collective-permute-done | bytes 344096 | tf_op jit(solution)/shard_map/ppermute | solution.py:316
  42.6 2.7 %collective-permute-start.6 = (bf16[384,384]{1,0:T(8,128)(2,1)S(1)}, bf16[384,384]{1,0:T(8,128)(2,1)S(1)}, u32[]{:S(2)}, u32[]{:S(2)}) collective-permute-start(bf16[384,384]{1,0:T(8,128)(2,1)S(1)} %collective-permute-done.5.refs_8_.refs_7_), channel_id=1, source_target_pairs={{0,192},{64,0},{128,64},{192,128},{1,193},{65,1},{129,65},{193,129... | collective-permute-start | bytes 884744 | tf_op jit(solution)/shard_map/ppermute | solution.py:343
  45.3 0.7 slice.13
  46.0 3.7 %collective-permute-done.7.refs_0_.refs_10_ = bf16[448,384]{1,0:T(8,128)(2,1)S(1)} collective-permute-done((bf16[448,384]{1,0:T(8,128)(2,1)S(1)}, bf16[448,384]{1,0:T(8,128)(2,1)S(1)}, u32[]{:S(2)}, u32[]{:S(2)}) %collective-permute-start.7) | collective-permute-done | bytes 344096 | tf_op jit(solution)/shard_map/ppermute | solution.py:316
  49.7 0.7 collective-permute-start.10
  50.4 0.7 slice.12
  51.0 1.7 %collective-permute-start.8 = (bf16[224,384]{1,0:T(8,128)(2,1)}, bf16[224,384]{1,0:T(8,128)(2,1)}, u32[]{:S(2)}, u32[]{:S(2)}) collective-permute-start(bf16[224,384]{1,0:T(8,128)(2,1)} %slice.12), channel_id=1, source_target_pairs={{0,16},{16,32},{32,48},{48,0},{1,17},{17,33},{33,49},{49,1},{2,18}... | collective-permute-start | bytes 516104 | tf_op jit(solution)/shard_map/ppermute | solution.py:319
  52.8 0.6 copy-done
  53.4 5.7 %shard_map.75 = (bf16[400,384]{1,0:T(8,128)(2,1)S(1)}, bf16[400,384]{1,0:T(8,128)(2,1)S(1)}, f32[1,512]{1,0:T(1,128)S(1)}) custom-call(bf16[448,384]{1,0:T(8,128)(2,1)S(1)} %collective-permute-done.7.refs_0_.refs_10_, bf16[448,384]{1,0:T(8,128)(2,1)S(1)} %collective-permute-done.9.refs_1_.refs_13_, bf16[384,384]{1,0:T(8,128)(2,1)S(1)} %get-tuple-element.18.refs_2_.refs_1_, ...), custom_call_target="tpu_custom_call" | custom-call | flops 1811939328 | bytes 2359296 | tf_op jit(solution)/shard_map/pallas_call | solution.py:207
  59.1 2.0 %collective-permute-start.11 = (bf16[400,384]{1,0:T(8,128)(2,1)S(1)}, bf16[400,384]{1,0:T(8,128)(2,1)S(1)}, u32[]{:S(2)}, u32[]{:S(2)}) collective-permute-start(bf16[400,384]{1,0:T(8,128)(2,1)S(1)} %get-tuple-element.20.refs_10_), channel_id=1, source_target_pairs={{0,48},{16,0},{32,16},{48,32},{1,49},{17,1},{33,17},{49,33},{2,50}... | collective-permute-start | bytes 921608 | tf_op jit(solution)/shard_map/ppermute | solution.py:350
  61.6 3.6 %shard_map.76.refs_14_ = bf16[400,384]{1,0:T(8,128)(2,1)S(1)} custom-call(bf16[224,384]{1,0:T(8,128)(2,1)} %collective-permute-done.8.refs_0_.refs_11_, bf16[224,384]{1,0:T(8,128)(2,1)} %collective-permute-done.10.refs_1_.refs_12_, bf16[384,384]{1,0:T(8,128)(2,1)S(1)} %get-tuple-element.18.refs_2_.refs_1_, ...), custom_call_target="tpu_custom_call" | custom-call | flops 905969664 | bytes 2359296 | tf_op jit(solution)/shard_map/pallas_call | solution.py:207
  65.2 4.0 %collective-permute-start.13 = (bf16[400,384]{1,0:T(8,128)(2,1)S(1)}, bf16[400,384]{1,0:T(8,128)(2,1)S(1)}, u32[]{:S(2)}, u32[]{:S(2)}) collective-permute-start(bf16[400,384]{1,0:T(8,128)(2,1)S(1)} %shard_map.76.refs_14_), channel_id=1, source_target_pairs={{0,32},{16,48},{32,0},{48,16},{1,33},{17,49},{33,1},{49,17},{2,34}... | collective-permute-start | bytes 921608 | tf_op jit(solution)/shard_map/ppermute | solution.py:350
  69.2 3.6 %shard_map.77 = (bf16[400,384]{1,0:T(8,128)(2,1)S(1)}, bf16[2,4,32,384]{3,2,1,0:T(8,128)(2,1)S(1)}) custom-call(bf16[448,384]{1,0:T(8,128)(2,1)S(1)} %get-tuple-element.17.refs_0_.refs_9_.q_ref, bf16[384,384]{1,0:T(8,128)(2,1)S(1)} %get-tuple-element.18.refs_2_.refs_1_, bf16[384,384]{1,0:T(8,128)(2,1)S(1)} %collective-permute-done.1.refs_3_.refs_2_, ...), custom_call_target="tpu_custom_call" | custom-call | flops 905969664 | bytes 2359296 | tf_op jit(solution)/shard_map/pallas_call | solution.py:207
  72.8 12.1 %all-gather = bf16[8,4,32,384]{3,2,1,0:T(8,128)(2,1)S(1)} all-gather(bf16[2,4,32,384]{3,2,1,0:T(8,128)(2,1)S(1)} %get-tuple-element.23), channel_id=2, replica_groups=mesh['y'=4,'z_hi'=4,'core'=2,'z_lo'=2,'x'=4] {'y'}, dimensions={0}, use_global_device_ids=true | all-gather | bytes 983040 | tf_op jit(solution)/shard_map/all_gather | solution.py:351
  85.0 5.9 %all-gather.1 = bf16[8,1,4,32,384]{4,3,2,1,0:T(8,128)(2,1)S(1)} all-gather(bf16[4,1,4,32,384]{4,3,2,1,0:T(8,128)(2,1)S(1)} %slice.14), channel_id=3, replica_groups=mesh['y'=4,'z_hi'=4,'core'=2,'z_lo'=2,'x'=4] {'core'}, dimensions={0}, use_global_device_ids=true | all-gather | bytes 1179648 | tf_op jit(solution)/shard_map/all_gather | solution.py:352
  90.9 1.4 %shard_map.78 = (bf16[400,384]{1,0:T(8,128)(2,1)S(1)}, bf16[384,384]{1,0:T(8,128)(2,1)S(1)}) custom-call(s32[1]{0:T(128)} %bitcast.core_ref, bf16[448,384]{1,0:T(8,128)(2,1)S(1)} %get-tuple-element.17.refs_0_.refs_9_.q_ref, bf16[4,2,4,32,384]{4,3,2,1,0:T(8,128)(2,1)S(1)} %bitcast.8, bf16[2,4,4,32,384]{4,3,2,1,0:T(8,128)(2,1)S(1)} %bitcast.10, ...), custom_call_target="tpu_custom_call" | custom-call | flops 452984832 | bytes 1179648 | tf_op jit(solution)/shard_map/pallas_call | solution.py:262
  92.3 0.9 shard_map.79
  93.2 1.3 %collective-permute-start.14 = (bf16[384,384]{1,0:T(8,128)(2,1)S(1)}, bf16[384,384]{1,0:T(8,128)(2,1)S(1)}, u32[]{:S(2)}, u32[]{:S(2)}) collective-permute-start(bf16[384,384]{1,0:T(8,128)(2,1)S(1)} %get-tuple-element.28), channel_id=1, source_target_pairs={{0,8},{1,9},{2,10},{3,11},{4,12},{5,13},{6,14},{7,15},{16,24},{17,... | collective-permute-start | bytes 884744 | tf_op jit(solution)/shard_map/ppermute | solution.py:355
  94.5 2.2 %collective-permute-done.14 = bf16[384,384]{1,0:T(8,128)(2,1)S(1)} collective-permute-done((bf16[384,384]{1,0:T(8,128)(2,1)S(1)}, bf16[384,384]{1,0:T(8,128)(2,1)S(1)}, u32[]{:S(2)}, u32[]{:S(2)}) %collective-permute-start.14) | collective-permute-done | bytes 294944 | tf_op jit(solution)/shard_map/ppermute | solution.py:355
  96.8 10.5 %all_to_all.10.in_ref = bf16[16,24,384]{2,1,0:T(8,128)(2,1)S(1)} all-to-all(bf16[16,24,384]{2,1,0:T(8,128)(2,1)S(1)} %bitcast.12), channel_id=1, replica_groups=mesh['y'=4,'z_hi'=4,'core'=2,'z_lo'=2,'x'=4] {'z_lo','x','core'}, dimensions={0} | all-to-all | bytes 589824 | tf_op jit(solution)/shard_map/all_to_all | solution.py:358
  107.2 0.7 shard_map.80
  (25 shorter events, 0.9 us)
Async XLA Ops:
  2.1 7.3 %copy-start.2 = (bf16[2,16,384]{2,1,0:T(8,128)(2,1)S(1)}, bf16[2,16,384]{2,1,0:T(8,128)(2,1)}, u32[]{:S(2)}) copy-start(bf16[2,16,384]{2,1,0:T(8,128)(2,1)} %param.10) | copy-start | bytes 73732
  2.1 21.3 %all-to-all-start = ((bf16[16,24,1152]{2,1,0:T(8,128)(2,1)}), bf16[16,24,1152]{2,1,0:T(8,128)(2,1)S(1)}, u32[]{:S(2)}, u32[]{:S(2)}) async-start(bf16[16,24,1152]{2,1,0:T(8,128)(2,1)} %shard_map.73), calls=%async_computation | async-start | bytes 1769472 | tf_op jit(solution)/shard_map/all_to_all | solution.py:334
  9.5 0.7 copy-start.3
  10.2 1.2 %collective-permute-start = (bf16[4,16,384]{2,1,0:T(8,128)(2,1)S(1)}, bf16[4,16,384]{2,1,0:T(8,128)(2,1)S(1)}, u32[]{:S(2)}, u32[]{:S(2)}) collective-permute-start(bf16[4,16,384]{2,1,0:T(8,128)(2,1)S(1)} %constant_dynamic-update-slice_fusion.own_ref), channel_id=1, source_target_pairs={{0,8},{8,0},{1,9},{9,1},{2,10},{10,2},{3,11},{11,3},{4,12},{12,4},... | collective-permute-start | bytes 147464 | tf_op jit(solution)/shard_map/ppermute | solution.py:332
  23.6 19.0 %collective-permute-start.9 = (bf16[448,384]{1,0:T(8,128)(2,1)S(1)}, bf16[448,384]{1,0:T(8,128)(2,1)S(1)}, u32[]{:S(2)}, u32[]{:S(2)}) collective-permute-start(bf16[448,384]{1,0:T(8,128)(2,1)S(1)} %get-tuple-element.17.refs_0_.refs_9_.q_ref), channel_id=1, source_target_pairs={{0,48},{16,0},{32,16},{48,32},{1,49},{17,1},{33,17},{49,33},{2,50}... | collective-permute-start | bytes 1032200 | tf_op jit(solution)/shard_map/ppermute | solution.py:316
  28.8 8.7 %collective-permute-start.1 = (bf16[384,384]{1,0:T(8,128)(2,1)S(1)}, bf16[384,384]{1,0:T(8,128)(2,1)S(1)}, u32[]{:S(2)}, u32[]{:S(2)}) collective-permute-start(bf16[384,384]{1,0:T(8,128)(2,1)S(1)} %get-tuple-element.18.refs_2_.refs_1_), channel_id=1, source_target_pairs={{0,64},{64,128},{128,192},{192,0},{1,65},{65,129},{129,193},{193,1... | collective-permute-start | bytes 884744 | tf_op jit(solution)/shard_map/ppermute | solution.py:340
  30.1 7.4 %collective-permute-start.5 = (bf16[384,384]{1,0:T(8,128)(2,1)S(1)}, bf16[384,384]{1,0:T(8,128)(2,1)S(1)}, u32[]{:S(2)}, u32[]{:S(2)}) collective-permute-start(bf16[384,384]{1,0:T(8,128)(2,1)S(1)} %get-tuple-element.19.refs_6_.refs_5_), channel_id=1, source_target_pairs={{0,192},{64,0},{128,64},{192,128},{1,193},{65,1},{129,65},{193,129... | collective-permute-start | bytes 884744 | tf_op jit(solution)/shard_map/ppermute | solution.py:341
  31.5 18.2 %collective-permute-start.7 = (bf16[448,384]{1,0:T(8,128)(2,1)S(1)}, bf16[448,384]{1,0:T(8,128)(2,1)S(1)}, u32[]{:S(2)}, u32[]{:S(2)}) collective-permute-start(bf16[448,384]{1,0:T(8,128)(2,1)S(1)} %get-tuple-element.17.refs_0_.refs_9_.q_ref), channel_id=1, source_target_pairs={{0,16},{16,32},{32,48},{48,0},{1,17},{17,33},{33,49},{49,1},{2,18}... | collective-permute-start | bytes 1032200 | tf_op jit(solution)/shard_map/ppermute | solution.py:316
  31.5 19.5 %collective-permute-start.2 = (bf16[384,384]{1,0:T(8,128)(2,1)S(1)}, bf16[384,384]{1,0:T(8,128)(2,1)S(1)}, u32[]{:S(2)}, u32[]{:S(2)}) collective-permute-start(bf16[384,384]{1,0:T(8,128)(2,1)S(1)} %get-tuple-element.18.refs_2_.refs_1_), channel_id=1, source_target_pairs={{0,192},{64,0},{128,64},{192,128},{1,193},{65,1},{129,65},{193,129... | collective-permute-start | bytes 884744 | tf_op jit(solution)/shard_map/ppermute | solution.py:340
  37.5 15.3 %collective-permute-start.4 = (bf16[384,384]{1,0:T(8,128)(2,1)S(1)}, bf16[384,384]{1,0:T(8,128)(2,1)S(1)}, u32[]{:S(2)}, u32[]{:S(2)}) collective-permute-start(bf16[384,384]{1,0:T(8,128)(2,1)S(1)} %get-tuple-element.19.refs_6_.refs_5_), channel_id=1, source_target_pairs={{0,64},{64,128},{128,192},{192,0},{1,65},{65,129},{129,193},{193,1... | collective-permute-start | bytes 884744 | tf_op jit(solution)/shard_map/ppermute | solution.py:341
  37.5 15.3 %collective-permute-start.3 = (bf16[384,384]{1,0:T(8,128)(2,1)S(1)}, bf16[384,384]{1,0:T(8,128)(2,1)S(1)}, u32[]{:S(2)}, u32[]{:S(2)}) collective-permute-start(bf16[384,384]{1,0:T(8,128)(2,1)S(1)} %collective-permute-done.1.refs_3_.refs_2_), channel_id=1, source_target_pairs={{0,64},{64,128},{128,192},{192,0},{1,65},{65,129},{129,193},{193,1... | collective-permute-start | bytes 884744 | tf_op jit(solution)/shard_map/ppermute | solution.py:342
  42.6 10.2 %collective-permute-start.6 = (bf16[384,384]{1,0:T(8,128)(2,1)S(1)}, bf16[384,384]{1,0:T(8,128)(2,1)S(1)}, u32[]{:S(2)}, u32[]{:S(2)}) collective-permute-start(bf16[384,384]{1,0:T(8,128)(2,1)S(1)} %collective-permute-done.5.refs_8_.refs_7_), channel_id=1, source_target_pairs={{0,192},{64,0},{128,64},{192,128},{1,193},{65,1},{129,65},{193,129... | collective-permute-start | bytes 884744 | tf_op jit(solution)/shard_map/ppermute | solution.py:343
  49.7 11.9 %collective-permute-start.10 = (bf16[224,384]{1,0:T(8,128)(2,1)}, bf16[224,384]{1,0:T(8,128)(2,1)}, u32[]{:S(2)}, u32[]{:S(2)}) collective-permute-start(bf16[224,384]{1,0:T(8,128)(2,1)} %slice.13), channel_id=1, source_target_pairs={{0,48},{16,0},{32,16},{48,32},{1,49},{17,1},{33,17},{49,33},{2,50}... | collective-permute-start | bytes 516104 | tf_op jit(solution)/shard_map/ppermute | solution.py:320
  51.0 10.5 %collective-permute-start.8 = (bf16[224,384]{1,0:T(8,128)(2,1)}, bf16[224,384]{1,0:T(8,128)(2,1)}, u32[]{:S(2)}, u32[]{:S(2)}) collective-permute-start(bf16[224,384]{1,0:T(8,128)(2,1)} %slice.12), channel_id=1, source_target_pairs={{0,16},{16,32},{32,48},{48,0},{1,17},{17,33},{33,49},{49,1},{2,18}... | collective-permute-start | bytes 516104 | tf_op jit(solution)/shard_map/ppermute | solution.py:319
  52.7 0.7 copy-start
  52.8 0.7 copy-start.1
  59.1 33.2 %collective-permute-start.11 = (bf16[400,384]{1,0:T(8,128)(2,1)S(1)}, bf16[400,384]{1,0:T(8,128)(2,1)S(1)}, u32[]{:S(2)}, u32[]{:S(2)}) collective-permute-start(bf16[400,384]{1,0:T(8,128)(2,1)S(1)} %get-tuple-element.20.refs_10_), channel_id=1, source_target_pairs={{0,48},{16,0},{32,16},{48,32},{1,49},{17,1},{33,17},{49,33},{2,50}... | collective-permute-start | bytes 921608 | tf_op jit(solution)/shard_map/ppermute | solution.py:350
  61.1 31.3 %collective-permute-start.12 = (bf16[400,384]{1,0:T(8,128)(2,1)S(1)}, bf16[400,384]{1,0:T(8,128)(2,1)S(1)}, u32[]{:S(2)}, u32[]{:S(2)}) collective-permute-start(bf16[400,384]{1,0:T(8,128)(2,1)S(1)} %get-tuple-element.21.refs_11_), channel_id=1, source_target_pairs={{0,16},{16,32},{32,48},{48,0},{1,17},{17,33},{33,49},{49,1},{2,18}... | collective-permute-start | bytes 921608 | tf_op jit(solution)/shard_map/ppermute | solution.py:350
  65.2 27.1 %collective-permute-start.13 = (bf16[400,384]{1,0:T(8,128)(2,1)S(1)}, bf16[400,384]{1,0:T(8,128)(2,1)S(1)}, u32[]{:S(2)}, u32[]{:S(2)}) collective-permute-start(bf16[400,384]{1,0:T(8,128)(2,1)S(1)} %shard_map.76.refs_14_), channel_id=1, source_target_pairs={{0,32},{16,48},{32,0},{48,16},{1,33},{17,49},{33,1},{49,17},{2,34}... | collective-permute-start | bytes 921608 | tf_op jit(solution)/shard_map/ppermute | solution.py:350
  93.2 3.5 %collective-permute-start.14 = (bf16[384,384]{1,0:T(8,128)(2,1)S(1)}, bf16[384,384]{1,0:T(8,128)(2,1)S(1)}, u32[]{:S(2)}, u32[]{:S(2)}) collective-permute-start(bf16[384,384]{1,0:T(8,128)(2,1)S(1)} %get-tuple-element.28), channel_id=1, source_target_pairs={{0,8},{1,9},{2,10},{3,11},{4,12},{5,13},{6,14},{7,15},{16,24},{17,... | collective-permute-start | bytes 884744 | tf_op jit(solution)/shard_map/ppermute | solution.py:355

commit v6 on v5

--- a/solution.py
+++ b/solution.py
@@ -119,34 +119,36 @@
     return slice((offset + head) * HD, (offset + head + 1) * HD)
 
 
-def take_block(refs, rows):
-    whole = refs[0][...] if len(refs) == 1 else jnp.concatenate([ref[...] for ref in refs], axis=0)
-    return whole[0:rows], whole[rows:]
+def take_rows(refs, first, last, cols):
+    pieces, at = [], 0
+    for ref in refs:
+        low, high = max(first - at, 0), min(last - at, ref.shape[0])
+        if low < high:
+            pieces.append(ref[low:high, cols])
+        at += ref.shape[0]
+    return pieces[0] if len(pieces) == 1 else jnp.concatenate(pieces, axis=0)
 
 
 def attend(heads, qs, keys, values, outs):
     rows = keys[0].shape[0]
 
+    def joined(refs, head):
+        return jnp.concatenate([ref[:, head_cols(head)] for ref in refs], axis=0)
+
     def front(block, head):
-        q = qs[block][:, head_cols(head)]
-        scores = [nt(q, k[:, head_cols(head)]) for k in keys]
-        top = scores[0].max(axis=-1, keepdims=True)
-        for s in scores[1:]:
-            top = jnp.maximum(top, s.max(axis=-1, keepdims=True))
-        return scores, top * SCALE2
+        s = nt(take_rows(qs[block], 0, rows, head_cols(head)), joined(keys, head))
+        return s, s.max(axis=-1, keepdims=True) * SCALE2
 
     items = [(block, head) for block in range(len(qs)) for head in range(heads)]
     ahead = front(*items[0])
     logs = []
     for n, (block, head) in enumerate(items):
-        scores, shift = ahead
+        s, shift = ahead
         if n + 1 < len(items):
             ahead = front(*items[n + 1])
-        total = acc = 0.0
-        for s, v in zip(scores, values):
-            w = jnp.exp2(s * SCALE2 - shift)
-            total = total + w.sum(axis=-1, keepdims=True)
-            acc = acc + nn(w.astype(jnp.bfloat16), v[:, head_cols(head)])
+        w = jnp.exp2(s * SCALE2 - shift)
+        total = w.sum(axis=-1, keepdims=True)
+        acc = nn(w.astype(jnp.bfloat16), joined(values, head))
         outs[block][0:rows, head_cols(head)] = (acc / total).astype(jnp.bfloat16)
         logs.append(shift + jnp.log2(total))
         if head + 1 == heads:
@@ -186,12 +188,12 @@
         place_ref, cols_ref, flags_ref = [refs.pop(0) for _ in range(3)]
         write_mask(4, place_ref[0], cols_ref, flags_ref, refs[-1])
     rows = keys[0].shape[0]
-    attend(heads, [take_block(block, rows)[0] for block in blocks], keys, values, refs[: len(blocks)])
+    attend(heads, blocks, keys, values, refs[: len(blocks)])
     for i, parts in enumerate(texts):
-        text = take_block(parts, rows)[1]
-        half = text.shape[0] // 2
-        refs[-1][0, i] = text[:half]
-        refs[-1][1, i] = text[half:]
+        half = refs[-1].shape[2]
+        for kind in range(2):
+            first = rows + kind * half
+            refs[-1][kind, i] = take_rows(parts, first, first + half, slice(None))
 
 
 def block_attention(blocks, keys, values, rows, heads, after, text_from=(), mask_from=()):

time: 109 us -> 109 us (level)
  no operation moved by 1% of the time
where the time goes in v6:
time: 109 us; the launch traced here: 108 us
  starting transfers between devices  30.9 us (28%)
  blocking collectives  28.3 us (26%)
  waiting for transfers between devices  27.4 us (25%)
  Pallas kernels  18.4 us (17%)
  local copies, waits for them, and re-layouts  2.81 us (3%)
    pallas_call x3, Pallas kernels, block_attention(): pl.pallas_call(functools.partial(block_kernel, heads, [len(b) for b in bl...  13.1 us
    all_to_all x1, waiting for transfers between devices, body(): held = lax.all_to_all(packed, axes, split_axis=0, concat_axis=0, tiled=True)  12.1 us
    all_gather x1, blocking collectives, body(): text = lax.all_gather(text, 'y')  11.8 us
    all_to_all x1, blocking collectives, body(): back = lax.all_to_all(result, axes, split_axis=0, concat_axis=0, tiled=True)  10.4 us
    ppermute x2, waiting for transfers between devices, gather_ring(): near = {s: lax.ppermute(x, axis, ring(n, s)) for s in (1, n - 1)}  7.54 us
    all_to_all x1, starting transfers between devices, body(): held = lax.all_to_all(packed, axes, split_axis=0, concat_axis=0, tiled=True)  7.3 us
    ppermute x3, starting transfers between devices, body(): lax.ppermute(x, 'z_hi', ring(n_z, n_z - s))  6.48 us
    all_gather x1, blocking collectives, body(): values = lax.all_gather(text[:, 1], 'core')  6.13 us
  transfers between devices with their start and end apart: 16, of which 6 were waited for; matrix products, arithmetic and copies ran while one was open for 1% of the time, Pallas kernels for 13%

profile of v6, /device:TPU:1, one launch (start us, length us, event | category | flops | bytes accessed | tf_op | source)
XLA Modules:
  0.0 108.1 jit_solution(18166623962595806344)
XLA Ops:
  0.0 2.1 %shard_map.73 = bf16[16,24,1152]{2,1,0:T(8,128)(2,1)} custom-call(bf16[2,24,3072]{2,1,0:T(8,128)(2,1)} %q_ref.1, bf16[2,24,3072]{2,1,0:T(8,128)(2,1)} %k_ref.1, bf16[2,24,3072]{2,1,0:T(8,128)(2,1)} %v_ref.1), custom_call_target="tpu_custom_call" | custom-call | tf_op jit(solution)/shard_map/pallas_call | solution.py:39
  2.1 7.3 %all-to-all-start = ((bf16[16,24,1152]{2,1,0:T(8,128)(2,1)}), bf16[16,24,1152]{2,1,0:T(8,128)(2,1)S(1)}, u32[]{:S(2)}, u32[]{:S(2)}) async-start(bf16[16,24,1152]{2,1,0:T(8,128)(2,1)} %shard_map.73), calls=%async_computation | async-start | bytes 1769472 | tf_op jit(solution)/shard_map/all_to_all | solution.py:336
  9.5 0.7 copy-done.3
  10.3 1.1 %collective-permute-done.other_ref = bf16[4,16,384]{2,1,0:T(8,128)(2,1)S(1)} collective-permute-done((bf16[4,16,384]{2,1,0:T(8,128)(2,1)S(1)}, bf16[4,16,384]{2,1,0:T(8,128)(2,1)S(1)}, u32[]{:S(2)}, u32[]{:S(2)}) %collective-permute-start) | collective-permute-done | bytes 49184 | tf_op jit(solution)/shard_map/ppermute | solution.py:334
  11.4 12.1 %all-to-all-done = bf16[16,24,1152]{2,1,0:T(8,128)(2,1)S(1)} async-done(((bf16[16,24,1152]{2,1,0:T(8,128)(2,1)}), bf16[16,24,1152]{2,1,0:T(8,128)(2,1)S(1)}, u32[]{:S(2)}, u32[]{:S(2)}) %all-to-all-start) | async-done | bytes 884768 | tf_op jit(solution)/shard_map/all_to_all | solution.py:336
  23.6 5.2 %collective-permute-start.9 = (bf16[448,384]{1,0:T(8,128)(2,1)S(1)}, bf16[448,384]{1,0:T(8,128)(2,1)S(1)}, u32[]{:S(2)}, u32[]{:S(2)}) collective-permute-start(bf16[448,384]{1,0:T(8,128)(2,1)S(1)} %get-tuple-element.17.refs_0_.refs_9_.q_ref), channel_id=1, source_target_pairs={{0,48},{16,0},{32,16},{48,32},{1,49},{17,1},{33,17},{49,33},{2,50}... | collective-permute-start | bytes 1032200 | tf_op jit(solution)/shard_map/ppermute | solution.py:318
  28.8 1.3 %collective-permute-start.1 = (bf16[384,384]{1,0:T(8,128)(2,1)S(1)}, bf16[384,384]{1,0:T(8,128)(2,1)S(1)}, u32[]{:S(2)}, u32[]{:S(2)}) collective-permute-start(bf16[384,384]{1,0:T(8,128)(2,1)S(1)} %get-tuple-element.18.refs_2_.refs_1_), channel_id=1, source_target_pairs={{0,64},{64,128},{128,192},{192,0},{1,65},{65,129},{129,193},{193,1... | collective-permute-start | bytes 884744 | tf_op jit(solution)/shard_map/ppermute | solution.py:342
  30.1 1.4 %collective-permute-start.5 = (bf16[384,384]{1,0:T(8,128)(2,1)S(1)}, bf16[384,384]{1,0:T(8,128)(2,1)S(1)}, u32[]{:S(2)}, u32[]{:S(2)}) collective-permute-start(bf16[384,384]{1,0:T(8,128)(2,1)S(1)} %get-tuple-element.19.refs_6_.refs_5_), channel_id=1, source_target_pairs={{0,192},{64,0},{128,64},{192,128},{1,193},{65,1},{129,65},{193,129... | collective-permute-start | bytes 884744 | tf_op jit(solution)/shard_map/ppermute | solution.py:343
  31.5 1.5 %collective-permute-start.2 = (bf16[384,384]{1,0:T(8,128)(2,1)S(1)}, bf16[384,384]{1,0:T(8,128)(2,1)S(1)}, u32[]{:S(2)}, u32[]{:S(2)}) collective-permute-start(bf16[384,384]{1,0:T(8,128)(2,1)S(1)} %get-tuple-element.18.refs_2_.refs_1_), channel_id=1, source_target_pairs={{0,192},{64,0},{128,64},{192,128},{1,193},{65,1},{129,65},{193,129... | collective-permute-start | bytes 884744 | tf_op jit(solution)/shard_map/ppermute | solution.py:342
  33.0 4.5 %collective-permute-done.1.refs_3_.refs_2_ = bf16[384,384]{1,0:T(8,128)(2,1)S(1)} collective-permute-done((bf16[384,384]{1,0:T(8,128)(2,1)S(1)}, bf16[384,384]{1,0:T(8,128)(2,1)S(1)}, u32[]{:S(2)}, u32[]{:S(2)}) %collective-permute-start.1) | collective-permute-done | bytes 294944 | tf_op jit(solution)/shard_map/ppermute | solution.py:342
  37.5 1.3 %collective-permute-start.3 = (bf16[384,384]{1,0:T(8,128)(2,1)S(1)}, bf16[384,384]{1,0:T(8,128)(2,1)S(1)}, u32[]{:S(2)}, u32[]{:S(2)}) collective-permute-start(bf16[384,384]{1,0:T(8,128)(2,1)S(1)} %collective-permute-done.1.refs_3_.refs_2_), channel_id=1, source_target_pairs={{0,64},{64,128},{128,192},{192,0},{1,65},{65,129},{129,193},{193,1... | collective-permute-start | bytes 884744 | tf_op jit(solution)/shard_map/ppermute | solution.py:344
  38.7 3.9 %collective-permute-done.9.refs_1_.refs_13_ = bf16[448,384]{1,0:T(8,128)(2,1)S(1)} collective-permute-done((bf16[448,384]{1,0:T(8,128)(2,1)S(1)}, bf16[448,384]{1,0:T(8,128)(2,1)S(1)}, u32[]{:S(2)}, u32[]{:S(2)}) %collective-permute-start.9) | collective-permute-done | bytes 344096 | tf_op jit(solution)/shard_map/ppermute | solution.py:318
  42.6 2.7 %collective-permute-start.6 = (bf16[384,384]{1,0:T(8,128)(2,1)S(1)}, bf16[384,384]{1,0:T(8,128)(2,1)S(1)}, u32[]{:S(2)}, u32[]{:S(2)}) collective-permute-start(bf16[384,384]{1,0:T(8,128)(2,1)S(1)} %collective-permute-done.5.refs_8_.refs_7_), channel_id=1, source_target_pairs={{0,192},{64,0},{128,64},{192,128},{1,193},{65,1},{129,65},{193,129... | collective-permute-start | bytes 884744 | tf_op jit(solution)/shard_map/ppermute | solution.py:345
  45.3 0.7 slice.13
  46.0 3.7 %collective-permute-done.7.refs_0_.refs_10_ = bf16[448,384]{1,0:T(8,128)(2,1)S(1)} collective-permute-done((bf16[448,384]{1,0:T(8,128)(2,1)S(1)}, bf16[448,384]{1,0:T(8,128)(2,1)S(1)}, u32[]{:S(2)}, u32[]{:S(2)}) %collective-permute-start.7) | collective-permute-done | bytes 344096 | tf_op jit(solution)/shard_map/ppermute | solution.py:318
  49.7 0.7 collective-permute-start.10
  50.4 0.7 slice.12
  51.0 1.7 %collective-permute-start.8 = (bf16[224,384]{1,0:T(8,128)(2,1)}, bf16[224,384]{1,0:T(8,128)(2,1)}, u32[]{:S(2)}, u32[]{:S(2)}) collective-permute-start(bf16[224,384]{1,0:T(8,128)(2,1)} %slice.12), channel_id=1, source_target_pairs={{0,16},{16,32},{32,48},{48,0},{1,17},{17,33},{33,49},{49,1},{2,18}... | collective-permute-start | bytes 516104 | tf_op jit(solution)/shard_map/ppermute | solution.py:321
  52.8 0.6 copy-done
  53.4 5.5 %shard_map.75 = (bf16[400,384]{1,0:T(8,128)(2,1)S(1)}, bf16[400,384]{1,0:T(8,128)(2,1)S(1)}, f32[1,512]{1,0:T(1,128)S(1)}) custom-call(bf16[448,384]{1,0:T(8,128)(2,1)S(1)} %collective-permute-done.7.refs_0_.refs_10_, bf16[448,384]{1,0:T(8,128)(2,1)S(1)} %collective-permute-done.9.refs_1_.refs_13_, bf16[384,384]{1,0:T(8,128)(2,1)S(1)} %get-tuple-element.18.refs_2_.refs_1_, ...), custom_call_target="tpu_custom_call" | custom-call | flops 1811939328 | bytes 2359296 | tf_op jit(solution)/shard_map/pallas_call | solution.py:209
  59.0 2.0 %collective-permute-start.11 = (bf16[400,384]{1,0:T(8,128)(2,1)S(1)}, bf16[400,384]{1,0:T(8,128)(2,1)S(1)}, u32[]{:S(2)}, u32[]{:S(2)}) collective-permute-start(bf16[400,384]{1,0:T(8,128)(2,1)S(1)} %get-tuple-element.20.refs_10_), channel_id=1, source_target_pairs={{0,48},{16,0},{32,16},{48,32},{1,49},{17,1},{33,17},{49,33},{2,50}... | collective-permute-start | bytes 921608 | tf_op jit(solution)/shard_map/ppermute | solution.py:352
  61.4 3.8 %shard_map.76.refs_14_ = bf16[400,384]{1,0:T(8,128)(2,1)S(1)} custom-call(bf16[224,384]{1,0:T(8,128)(2,1)} %collective-permute-done.8.refs_0_.refs_11_, bf16[224,384]{1,0:T(8,128)(2,1)} %collective-permute-done.10.refs_1_.refs_12_, bf16[384,384]{1,0:T(8,128)(2,1)S(1)} %get-tuple-element.18.refs_2_.refs_1_, ...), custom_call_target="tpu_custom_call" | custom-call | flops 905969664 | bytes 2359296 | tf_op jit(solution)/shard_map/pallas_call | solution.py:209
  65.2 4.0 %collective-permute-start.13 = (bf16[400,384]{1,0:T(8,128)(2,1)S(1)}, bf16[400,384]{1,0:T(8,128)(2,1)S(1)}, u32[]{:S(2)}, u32[]{:S(2)}) collective-permute-start(bf16[400,384]{1,0:T(8,128)(2,1)S(1)} %shard_map.76.refs_14_), channel_id=1, source_target_pairs={{0,32},{16,48},{32,0},{48,16},{1,33},{17,49},{33,1},{49,17},{2,34}... | collective-permute-start | bytes 921608 | tf_op jit(solution)/shard_map/ppermute | solution.py:352
  69.3 3.8 %shard_map.77 = (bf16[400,384]{1,0:T(8,128)(2,1)S(1)}, bf16[2,4,32,384]{3,2,1,0:T(8,128)(2,1)S(1)}) custom-call(bf16[448,384]{1,0:T(8,128)(2,1)S(1)} %get-tuple-element.17.refs_0_.refs_9_.q_ref, bf16[384,384]{1,0:T(8,128)(2,1)S(1)} %get-tuple-element.18.refs_2_.refs_1_, bf16[384,384]{1,0:T(8,128)(2,1)S(1)} %collective-permute-done.1.refs_3_.refs_2_, ...), custom_call_target="tpu_custom_call" | custom-call | flops 905969664 | bytes 2359296 | tf_op jit(solution)/shard_map/pallas_call | solution.py:209
  73.1 11.8 %all-gather = bf16[8,4,32,384]{3,2,1,0:T(8,128)(2,1)S(1)} all-gather(bf16[2,4,32,384]{3,2,1,0:T(8,128)(2,1)S(1)} %get-tuple-element.23), channel_id=2, replica_groups=mesh['y'=4,'z_hi'=4,'core'=2,'z_lo'=2,'x'=4] {'y'}, dimensions={0}, use_global_device_ids=true | all-gather | bytes 983040 | tf_op jit(solution)/shard_map/all_gather | solution.py:353
  85.0 6.1 %all-gather.1 = bf16[8,1,4,32,384]{4,3,2,1,0:T(8,128)(2,1)S(1)} all-gather(bf16[4,1,4,32,384]{4,3,2,1,0:T(8,128)(2,1)S(1)} %slice.14), channel_id=3, replica_groups=mesh['y'=4,'z_hi'=4,'core'=2,'z_lo'=2,'x'=4] {'core'}, dimensions={0}, use_global_device_ids=true | all-gather | bytes 1179648 | tf_op jit(solution)/shard_map/all_gather | solution.py:354
  91.1 1.4 %shard_map.78 = (bf16[400,384]{1,0:T(8,128)(2,1)S(1)}, bf16[384,384]{1,0:T(8,128)(2,1)S(1)}) custom-call(s32[1]{0:T(128)} %bitcast.core_ref, bf16[448,384]{1,0:T(8,128)(2,1)S(1)} %get-tuple-element.17.refs_0_.refs_9_.q_ref, bf16[4,2,4,32,384]{4,3,2,1,0:T(8,128)(2,1)S(1)} %bitcast.8, bf16[2,4,4,32,384]{4,3,2,1,0:T(8,128)(2,1)S(1)} %bitcast.10, ...), custom_call_target="tpu_custom_call" | custom-call | flops 452984832 | bytes 1179648 | tf_op jit(solution)/shard_map/pallas_call | solution.py:264
  92.6 0.9 shard_map.79
  93.5 1.3 %collective-permute-start.14 = (bf16[384,384]{1,0:T(8,128)(2,1)S(1)}, bf16[384,384]{1,0:T(8,128)(2,1)S(1)}, u32[]{:S(2)}, u32[]{:S(2)}) collective-permute-start(bf16[384,384]{1,0:T(8,128)(2,1)S(1)} %get-tuple-element.28), channel_id=1, source_target_pairs={{0,8},{1,9},{2,10},{3,11},{4,12},{5,13},{6,14},{7,15},{16,24},{17,... | collective-permute-start | bytes 884744 | tf_op jit(solution)/shard_map/ppermute | solution.py:357
  94.8 2.2 %collective-permute-done.14 = bf16[384,384]{1,0:T(8,128)(2,1)S(1)} collective-permute-done((bf16[384,384]{1,0:T(8,128)(2,1)S(1)}, bf16[384,384]{1,0:T(8,128)(2,1)S(1)}, u32[]{:S(2)}, u32[]{:S(2)}) %collective-permute-start.14) | collective-permute-done | bytes 294944 | tf_op jit(solution)/shard_map/ppermute | solution.py:357
  97.0 10.4 %all_to_all.10.in_ref = bf16[16,24,384]{2,1,0:T(8,128)(2,1)S(1)} all-to-all(bf16[16,24,384]{2,1,0:T(8,128)(2,1)S(1)} %bitcast.12), channel_id=1, replica_groups=mesh['y'=4,'z_hi'=4,'core'=2,'z_lo'=2,'x'=4] {'z_lo','x','core'}, dimensions={0} | all-to-all | bytes 589824 | tf_op jit(solution)/shard_map/all_to_all | solution.py:360
  107.4 0.7 shard_map.80
  (25 shorter events, 0.9 us)
Async XLA Ops:
  2.1 7.3 %copy-start.2 = (bf16[2,16,384]{2,1,0:T(8,128)(2,1)S(1)}, bf16[2,16,384]{2,1,0:T(8,128)(2,1)}, u32[]{:S(2)}) copy-start(bf16[2,16,384]{2,1,0:T(8,128)(2,1)} %param.10) | copy-start | bytes 73732
  2.1 21.3 %all-to-all-start = ((bf16[16,24,1152]{2,1,0:T(8,128)(2,1)}), bf16[16,24,1152]{2,1,0:T(8,128)(2,1)S(1)}, u32[]{:S(2)}, u32[]{:S(2)}) async-start(bf16[16,24,1152]{2,1,0:T(8,128)(2,1)} %shard_map.73), calls=%async_computation | async-start | bytes 1769472 | tf_op jit(solution)/shard_map/all_to_all | solution.py:336
  9.5 0.7 copy-start.3
  10.2 1.2 %collective-permute-start = (bf16[4,16,384]{2,1,0:T(8,128)(2,1)S(1)}, bf16[4,16,384]{2,1,0:T(8,128)(2,1)S(1)}, u32[]{:S(2)}, u32[]{:S(2)}) collective-permute-start(bf16[4,16,384]{2,1,0:T(8,128)(2,1)S(1)} %constant_dynamic-update-slice_fusion.own_ref), channel_id=1, source_target_pairs={{0,8},{8,0},{1,9},{9,1},{2,10},{10,2},{3,11},{11,3},{4,12},{12,4},... | collective-permute-start | bytes 147464 | tf_op jit(solution)/shard_map/ppermute | solution.py:334
  23.6 19.0 %collective-permute-start.9 = (bf16[448,384]{1,0:T(8,128)(2,1)S(1)}, bf16[448,384]{1,0:T(8,128)(2,1)S(1)}, u32[]{:S(2)}, u32[]{:S(2)}) collective-permute-start(bf16[448,384]{1,0:T(8,128)(2,1)S(1)} %get-tuple-element.17.refs_0_.refs_9_.q_ref), channel_id=1, source_target_pairs={{0,48},{16,0},{32,16},{48,32},{1,49},{17,1},{33,17},{49,33},{2,50}... | collective-permute-start | bytes 1032200 | tf_op jit(solution)/shard_map/ppermute | solution.py:318
  28.8 8.7 %collective-permute-start.1 = (bf16[384,384]{1,0:T(8,128)(2,1)S(1)}, bf16[384,384]{1,0:T(8,128)(2,1)S(1)}, u32[]{:S(2)}, u32[]{:S(2)}) collective-permute-start(bf16[384,384]{1,0:T(8,128)(2,1)S(1)} %get-tuple-element.18.refs_2_.refs_1_), channel_id=1, source_target_pairs={{0,64},{64,128},{128,192},{192,0},{1,65},{65,129},{129,193},{193,1... | collective-permute-start | bytes 884744 | tf_op jit(solution)/shard_map/ppermute | solution.py:342
  30.1 7.4 %collective-permute-start.5 = (bf16[384,384]{1,0:T(8,128)(2,1)S(1)}, bf16[384,384]{1,0:T(8,128)(2,1)S(1)}, u32[]{:S(2)}, u32[]{:S(2)}) collective-permute-start(bf16[384,384]{1,0:T(8,128)(2,1)S(1)} %get-tuple-element.19.refs_6_.refs_5_), channel_id=1, source_target_pairs={{0,192},{64,0},{128,64},{192,128},{1,193},{65,1},{129,65},{193,129... | collective-permute-start | bytes 884744 | tf_op jit(solution)/shard_map/ppermute | solution.py:343
  31.5 18.2 %collective-permute-start.7 = (bf16[448,384]{1,0:T(8,128)(2,1)S(1)}, bf16[448,384]{1,0:T(8,128)(2,1)S(1)}, u32[]{:S(2)}, u32[]{:S(2)}) collective-permute-start(bf16[448,384]{1,0:T(8,128)(2,1)S(1)} %get-tuple-element.17.refs_0_.refs_9_.q_ref), channel_id=1, source_target_pairs={{0,16},{16,32},{32,48},{48,0},{1,17},{17,33},{33,49},{49,1},{2,18}... | collective-permute-start | bytes 1032200 | tf_op jit(solution)/shard_map/ppermute | solution.py:318
  31.5 19.5 %collective-permute-start.2 = (bf16[384,384]{1,0:T(8,128)(2,1)S(1)}, bf16[384,384]{1,0:T(8,128)(2,1)S(1)}, u32[]{:S(2)}, u32[]{:S(2)}) collective-permute-start(bf16[384,384]{1,0:T(8,128)(2,1)S(1)} %get-tuple-element.18.refs_2_.refs_1_), channel_id=1, source_target_pairs={{0,192},{64,0},{128,64},{192,128},{1,193},{65,1},{129,65},{193,129... | collective-permute-start | bytes 884744 | tf_op jit(solution)/shard_map/ppermute | solution.py:342
  37.5 15.3 %collective-permute-start.4 = (bf16[384,384]{1,0:T(8,128)(2,1)S(1)}, bf16[384,384]{1,0:T(8,128)(2,1)S(1)}, u32[]{:S(2)}, u32[]{:S(2)}) collective-permute-start(bf16[384,384]{1,0:T(8,128)(2,1)S(1)} %get-tuple-element.19.refs_6_.refs_5_), channel_id=1, source_target_pairs={{0,64},{64,128},{128,192},{192,0},{1,65},{65,129},{129,193},{193,1... | collective-permute-start | bytes 884744 | tf_op jit(solution)/shard_map/ppermute | solution.py:343
  37.5 15.3 %collective-permute-start.3 = (bf16[384,384]{1,0:T(8,128)(2,1)S(1)}, bf16[384,384]{1,0:T(8,128)(2,1)S(1)}, u32[]{:S(2)}, u32[]{:S(2)}) collective-permute-start(bf16[384,384]{1,0:T(8,128)(2,1)S(1)} %collective-permute-done.1.refs_3_.refs_2_), channel_id=1, source_target_pairs={{0,64},{64,128},{128,192},{192,0},{1,65},{65,129},{129,193},{193,1... | collective-permute-start | bytes 884744 | tf_op jit(solution)/shard_map/ppermute | solution.py:344
  42.6 10.2 %collective-permute-start.6 = (bf16[384,384]{1,0:T(8,128)(2,1)S(1)}, bf16[384,384]{1,0:T(8,128)(2,1)S(1)}, u32[]{:S(2)}, u32[]{:S(2)}) collective-permute-start(bf16[384,384]{1,0:T(8,128)(2,1)S(1)} %collective-permute-done.5.refs_8_.refs_7_), channel_id=1, source_target_pairs={{0,192},{64,0},{128,64},{192,128},{1,193},{65,1},{129,65},{193,129... | collective-permute-start | bytes 884744 | tf_op jit(solution)/shard_map/ppermute | solution.py:345
  49.7 11.7 %collective-permute-start.10 = (bf16[224,384]{1,0:T(8,128)(2,1)}, bf16[224,384]{1,0:T(8,128)(2,1)}, u32[]{:S(2)}, u32[]{:S(2)}) collective-permute-start(bf16[224,384]{1,0:T(8,128)(2,1)} %slice.13), channel_id=1, source_target_pairs={{0,48},{16,0},{32,16},{48,32},{1,49},{17,1},{33,17},{49,33},{2,50}... | collective-permute-start | bytes 516104 | tf_op jit(solution)/shard_map/ppermute | solution.py:322
  51.0 10.4 %collective-permute-start.8 = (bf16[224,384]{1,0:T(8,128)(2,1)}, bf16[224,384]{1,0:T(8,128)(2,1)}, u32[]{:S(2)}, u32[]{:S(2)}) collective-permute-start(bf16[224,384]{1,0:T(8,128)(2,1)} %slice.12), channel_id=1, source_target_pairs={{0,16},{16,32},{32,48},{48,0},{1,17},{17,33},{33,49},{49,1},{2,18}... | collective-permute-start | bytes 516104 | tf_op jit(solution)/shard_map/ppermute | solution.py:321
  52.7 0.7 copy-start
  52.8 0.7 copy-start.1
  59.0 33.6 %collective-permute-start.11 = (bf16[400,384]{1,0:T(8,128)(2,1)S(1)}, bf16[400,384]{1,0:T(8,128)(2,1)S(1)}, u32[]{:S(2)}, u32[]{:S(2)}) collective-permute-start(bf16[400,384]{1,0:T(8,128)(2,1)S(1)} %get-tuple-element.20.refs_10_), channel_id=1, source_target_pairs={{0,48},{16,0},{32,16},{48,32},{1,49},{17,1},{33,17},{49,33},{2,50}... | collective-permute-start | bytes 921608 | tf_op jit(solution)/shard_map/ppermute | solution.py:352
  60.9 31.6 %collective-permute-start.12 = (bf16[400,384]{1,0:T(8,128)(2,1)S(1)}, bf16[400,384]{1,0:T(8,128)(2,1)S(1)}, u32[]{:S(2)}, u32[]{:S(2)}) collective-permute-start(bf16[400,384]{1,0:T(8,128)(2,1)S(1)} %get-tuple-element.21.refs_11_), channel_id=1, source_target_pairs={{0,16},{16,32},{32,48},{48,0},{1,17},{17,33},{33,49},{49,1},{2,18}... | collective-permute-start | bytes 921608 | tf_op jit(solution)/shard_map/ppermute | solution.py:352
  65.2 27.3 %collective-permute-start.13 = (bf16[400,384]{1,0:T(8,128)(2,1)S(1)}, bf16[400,384]{1,0:T(8,128)(2,1)S(1)}, u32[]{:S(2)}, u32[]{:S(2)}) collective-permute-start(bf16[400,384]{1,0:T(8,128)(2,1)S(1)} %shard_map.76.refs_14_), channel_id=1, source_target_pairs={{0,32},{16,48},{32,0},{48,16},{1,33},{17,49},{33,1},{49,17},{2,34}... | collective-permute-start | bytes 921608 | tf_op jit(solution)/shard_map/ppermute | solution.py:352
  93.5 3.5 %collective-permute-start.14 = (bf16[384,384]{1,0:T(8,128)(2,1)S(1)}, bf16[384,384]{1,0:T(8,128)(2,1)S(1)}, u32[]{:S(2)}, u32[]{:S(2)}) collective-permute-start(bf16[384,384]{1,0:T(8,128)(2,1)S(1)} %get-tuple-element.28), channel_id=1, source_target_pairs={{0,8},{1,9},{2,10},{3,11},{4,12},{5,13},{6,14},{7,15},{16,24},{17,... | collective-permute-start | bytes 884744 | tf_op jit(solution)/shard_map/ppermute | solution.py:357

commit v7 on v6

--- a/solution.py
+++ b/solution.py
@@ -346,9 +346,7 @@
     flags = shared_flags.reshape(1, -1)
     mask_from = (place[:1], replace_cols, flags)
     *near, mask = block_attention([qs[1], qs[3]], keys, values, rows, heads, [], mask_from=mask_from)
-    far = block_attention([qs[2]], keys, values, rows, heads, near)
-    own, text = block_attention([qs[0]], keys, values, rows, heads, far, [qs[i] for i in range(n_z)])
-    far = far[0]
+    far, own, text = block_attention([qs[2], qs[0]], keys, values, rows, heads, near, [qs[i] for i in range(n_z)])
     parts = [lax.ppermute(x, "z_hi", ring(n_z, n_z - s)) for s, x in ((1, near[0]), (3, near[1]), (2, far))]
     text = lax.all_gather(text, "y")
     values = lax.all_gather(text[:, 1], "core")

time: 109 us -> 109 us (level)
  blocking collectives: 28.3 us -> 29.7 us
  Pallas kernels: 18.4 us -> 17.2 us
    all_to_all x1, blocking collectives: 10.4 us -> 11.7 us  [body(): back = lax.all_to_all(result, axes, split_axis=0, concat_axis=0, tiled=True)]
    pallas_call x3 -> x2, Pallas kernels: 13.1 us -> 11.9 us  [block_attention(): pl.pallas_call(functools.partial(block_kernel, heads, [len(b) for b in bl...]
  transfers between devices with their start and end apart: 16 -> 16, of which waited for: 6 -> 6; matrix products, arithmetic and copies ran while one was open for 1% -> 1% of each run, Pallas kernels for 13% -> 12%
where the time goes in v7:
time: 109 us; the launch traced here: 108 us
  starting transfers between devices  30.9 us (28%)
  blocking collectives  29.7 us (27%)
  waiting for transfers between devices  28.1 us (26%)
  Pallas kernels  17.2 us (16%)
  local copies, waits for them, and re-layouts  2.14 us (2%)
    all_to_all x1, waiting for transfers between devices, body(): held = lax.all_to_all(packed, axes, split_axis=0, concat_axis=0, tiled=True)  12.1 us
    all_gather x1, blocking collectives, body(): text = lax.all_gather(text, 'y')  12 us
    pallas_call x2, Pallas kernels, block_attention(): pl.pallas_call(functools.partial(block_kernel, heads, [len(b) for b in bl...  11.9 us
    all_to_all x1, blocking collectives, body(): back = lax.all_to_all(result, axes, split_axis=0, concat_axis=0, tiled=True)  11.7 us
    ppermute x2, waiting for transfers between devices, gather_ring(): near = {s: lax.ppermute(x, axis, ring(n, s)) for s in (1, n - 1)}  8.2 us
    all_to_all x1, starting transfers between devices, body(): held = lax.all_to_all(packed, axes, split_axis=0, concat_axis=0, tiled=True)  7.3 us
    ppermute x3, starting transfers between devices, body(): lax.ppermute(x, 'z_hi', ring(n_z, n_z - s))  6.48 us
    all_gather x1, blocking collectives, body(): values = lax.all_gather(text[:, 1], 'core')  6 us
  transfers between devices with their start and end apart: 16, of which 6 were waited for; matrix products, arithmetic and copies ran while one was open for 1% of the time, Pallas kernels for 12%

profile of v7, /device:TPU:1, one launch (start us, length us, event | category | flops | bytes accessed | tf_op | source)
XLA Modules:
  0.0 108.3 jit_solution(15638413524371224303)
XLA Ops:
  0.0 2.1 %shard_map.73 = bf16[16,24,1152]{2,1,0:T(8,128)(2,1)} custom-call(bf16[2,24,3072]{2,1,0:T(8,128)(2,1)} %q_ref.1, bf16[2,24,3072]{2,1,0:T(8,128)(2,1)} %k_ref.1, bf16[2,24,3072]{2,1,0:T(8,128)(2,1)} %v_ref.1), custom_call_target="tpu_custom_call" | custom-call | tf_op jit(solution)/shard_map/pallas_call | solution.py:39
  2.1 7.3 %all-to-all-start = ((bf16[16,24,1152]{2,1,0:T(8,128)(2,1)}), bf16[16,24,1152]{2,1,0:T(8,128)(2,1)S(1)}, u32[]{:S(2)}, u32[]{:S(2)}) async-start(bf16[16,24,1152]{2,1,0:T(8,128)(2,1)} %shard_map.73), calls=%async_computation | async-start | bytes 1769472 | tf_op jit(solution)/shard_map/all_to_all | solution.py:336
  9.5 0.7 copy-done.3
  10.2 0.1 collective-permute-start
  10.3 1.1 %collective-permute-done.other_ref = bf16[4,16,384]{2,1,0:T(8,128)(2,1)S(1)} collective-permute-done((bf16[4,16,384]{2,1,0:T(8,128)(2,1)S(1)}, bf16[4,16,384]{2,1,0:T(8,128)(2,1)S(1)}, u32[]{:S(2)}, u32[]{:S(2)}) %collective-permute-start) | collective-permute-done | bytes 49184 | tf_op jit(solution)/shard_map/ppermute | solution.py:334
  11.4 12.1 %all-to-all-done = bf16[16,24,1152]{2,1,0:T(8,128)(2,1)S(1)} async-done(((bf16[16,24,1152]{2,1,0:T(8,128)(2,1)}), bf16[16,24,1152]{2,1,0:T(8,128)(2,1)S(1)}, u32[]{:S(2)}, u32[]{:S(2)}) %all-to-all-start) | async-done | bytes 884768 | tf_op jit(solution)/shard_map/all_to_all | solution.py:336
  23.6 5.2 %collective-permute-start.3 = (bf16[448,384]{1,0:T(8,128)(2,1)S(1)}, bf16[448,384]{1,0:T(8,128)(2,1)S(1)}, u32[]{:S(2)}, u32[]{:S(2)}) collective-permute-start(bf16[448,384]{1,0:T(8,128)(2,1)S(1)} %get-tuple-element.18.refs_2_.refs_11_.q_ref), channel_id=1, source_target_pairs={{0,48},{16,0},{32,16},{48,32},{1,49},{17,1},{33,17},{49,33},{2,50}... | collective-permute-start | bytes 1032200 | tf_op jit(solution)/shard_map/ppermute | solution.py:318
  28.8 1.3 %collective-permute-start.5 = (bf16[384,384]{1,0:T(8,128)(2,1)S(1)}, bf16[384,384]{1,0:T(8,128)(2,1)S(1)}, u32[]{:S(2)}, u32[]{:S(2)}) collective-permute-start(bf16[384,384]{1,0:T(8,128)(2,1)S(1)} %get-tuple-element.19.refs_2_.refs_3_), channel_id=1, source_target_pairs={{0,64},{64,128},{128,192},{192,0},{1,65},{65,129},{129,193},{193,1... | collective-permute-start | bytes 884744 | tf_op jit(solution)/shard_map/ppermute | solution.py:342
  30.1 1.4 %collective-permute-start.9 = (bf16[384,384]{1,0:T(8,128)(2,1)S(1)}, bf16[384,384]{1,0:T(8,128)(2,1)S(1)}, u32[]{:S(2)}, u32[]{:S(2)}) collective-permute-start(bf16[384,384]{1,0:T(8,128)(2,1)S(1)} %get-tuple-element.20.refs_6_.refs_7_), channel_id=1, source_target_pairs={{0,192},{64,0},{128,64},{192,128},{1,193},{65,1},{129,65},{193,129... | collective-permute-start | bytes 884744 | tf_op jit(solution)/shard_map/ppermute | solution.py:343
  31.5 1.5 %collective-permute-start.6 = (bf16[384,384]{1,0:T(8,128)(2,1)S(1)}, bf16[384,384]{1,0:T(8,128)(2,1)S(1)}, u32[]{:S(2)}, u32[]{:S(2)}) collective-permute-start(bf16[384,384]{1,0:T(8,128)(2,1)S(1)} %get-tuple-element.19.refs_2_.refs_3_), channel_id=1, source_target_pairs={{0,192},{64,0},{128,64},{192,128},{1,193},{65,1},{129,65},{193,129... | collective-permute-start | bytes 884744 | tf_op jit(solution)/shard_map/ppermute | solution.py:342
  33.0 4.5 %collective-permute-done.5.refs_3_.refs_4_ = bf16[384,384]{1,0:T(8,128)(2,1)S(1)} collective-permute-done((bf16[384,384]{1,0:T(8,128)(2,1)S(1)}, bf16[384,384]{1,0:T(8,128)(2,1)S(1)}, u32[]{:S(2)}, u32[]{:S(2)}) %collective-permute-start.5) | collective-permute-done | bytes 294944 | tf_op jit(solution)/shard_map/ppermute | solution.py:342
  37.5 1.3 %collective-permute-start.7 = (bf16[384,384]{1,0:T(8,128)(2,1)S(1)}, bf16[384,384]{1,0:T(8,128)(2,1)S(1)}, u32[]{:S(2)}, u32[]{:S(2)}) collective-permute-start(bf16[384,384]{1,0:T(8,128)(2,1)S(1)} %collective-permute-done.5.refs_3_.refs_4_), channel_id=1, source_target_pairs={{0,64},{64,128},{128,192},{192,0},{1,65},{65,129},{129,193},{193,1... | collective-permute-start | bytes 884744 | tf_op jit(solution)/shard_map/ppermute | solution.py:344
  38.7 3.9 %collective-permute-done.3.refs_1_.refs_15_ = bf16[448,384]{1,0:T(8,128)(2,1)S(1)} collective-permute-done((bf16[448,384]{1,0:T(8,128)(2,1)S(1)}, bf16[448,384]{1,0:T(8,128)(2,1)S(1)}, u32[]{:S(2)}, u32[]{:S(2)}) %collective-permute-start.3) | collective-permute-done | bytes 344096 | tf_op jit(solution)/shard_map/ppermute | solution.py:318
  42.6 2.7 %collective-permute-start.10 = (bf16[384,384]{1,0:T(8,128)(2,1)S(1)}, bf16[384,384]{1,0:T(8,128)(2,1)}, u32[]{:S(2)}, u32[]{:S(2)}) collective-permute-start(bf16[384,384]{1,0:T(8,128)(2,1)S(1)} %collective-permute-done.9.refs_8_.refs_9_), channel_id=1, source_target_pairs={{0,192},{64,0},{128,64},{192,128},{1,193},{65,1},{129,65},{193,129... | collective-permute-start | bytes 884744 | tf_op jit(solution)/shard_map/ppermute | solution.py:345
  45.3 4.3 %collective-permute-done.1.refs_0_.refs_12_ = bf16[448,384]{1,0:T(8,128)(2,1)S(1)} collective-permute-done((bf16[448,384]{1,0:T(8,128)(2,1)S(1)}, bf16[448,384]{1,0:T(8,128)(2,1)S(1)}, u32[]{:S(2)}, u32[]{:S(2)}) %collective-permute-start.1) | collective-permute-done | bytes 344096 | tf_op jit(solution)/shard_map/ppermute | solution.py:318
  49.7 0.7 collective-permute-start.4
  50.4 0.7 slice.12
  51.0 1.7 %collective-permute-start.2 = (bf16[224,384]{1,0:T(8,128)(2,1)}, bf16[224,384]{1,0:T(8,128)(2,1)}, u32[]{:S(2)}, u32[]{:S(2)}) collective-permute-start(bf16[224,384]{1,0:T(8,128)(2,1)} %slice.12), channel_id=1, source_target_pairs={{0,16},{16,32},{32,48},{48,0},{1,17},{17,33},{33,49},{49,1},{2,18}... | collective-permute-start | bytes 516104 | tf_op jit(solution)/shard_map/ppermute | solution.py:321
  52.8 0.6 copy-done
  53.4 6.0 %shard_map.75 = (bf16[400,384]{1,0:T(8,128)(2,1)S(1)}, bf16[400,384]{1,0:T(8,128)(2,1)S(1)}, f32[1,512]{1,0:T(1,128)S(1)}) custom-call(bf16[448,384]{1,0:T(8,128)(2,1)S(1)} %collective-permute-done.1.refs_0_.refs_12_, bf16[448,384]{1,0:T(8,128)(2,1)S(1)} %collective-permute-done.3.refs_1_.refs_15_, bf16[384,384]{1,0:T(8,128)(2,1)S(1)} %get-tuple-element.19.refs_2_.refs_3_, ...), custom_call_target="tpu_custom_call" | custom-call | flops 1811939328 | bytes 2359296 | tf_op jit(solution)/shard_map/pallas_call | solution.py:209
  59.4 2.0 %collective-permute-start.11 = (bf16[400,384]{1,0:T(8,128)(2,1)S(1)}, bf16[400,384]{1,0:T(8,128)(2,1)S(1)}, u32[]{:S(2)}, u32[]{:S(2)}) collective-permute-start(bf16[400,384]{1,0:T(8,128)(2,1)S(1)} %get-tuple-element.21.refs_16_), channel_id=1, source_target_pairs={{0,48},{16,0},{32,16},{48,32},{1,49},{17,1},{33,17},{49,33},{2,50}... | collective-permute-start | bytes 921608 | tf_op jit(solution)/shard_map/ppermute | solution.py:350
  61.3 0.5 collective-permute-start.12
  61.8 6.0 %shard_map.76 = (bf16[400,384]{1,0:T(8,128)(2,1)S(1)}, bf16[400,384]{1,0:T(8,128)(2,1)S(1)}, bf16[2,4,32,384]{3,2,1,0:T(8,128)(2,1)S(1)}) custom-call(bf16[224,384]{1,0:T(8,128)(2,1)} %collective-permute-done.2.refs_0_.refs_13_, bf16[224,384]{1,0:T(8,128)(2,1)S(1)} %collective-permute-done.4.refs_1_.refs_14_, ...), custom_call_target="tpu_custom_call" | custom-call | flops 1811939328 | bytes 2359296 | tf_op jit(solution)/shard_map/pallas_call | solution.py:209
  67.8 4.0 %collective-permute-start.13 = (bf16[400,384]{1,0:T(8,128)(2,1)S(1)}, bf16[400,384]{1,0:T(8,128)(2,1)S(1)}, u32[]{:S(2)}, u32[]{:S(2)}) collective-permute-start(bf16[400,384]{1,0:T(8,128)(2,1)S(1)} %get-tuple-element.24), channel_id=1, source_target_pairs={{0,32},{16,48},{32,0},{48,16},{1,33},{17,49},{33,1},{49,17},{2,34}... | collective-permute-start | bytes 921608 | tf_op jit(solution)/shard_map/ppermute | solution.py:350
  71.9 12.0 %all-gather = bf16[8,4,32,384]{3,2,1,0:T(8,128)(2,1)S(1)} all-gather(bf16[2,4,32,384]{3,2,1,0:T(8,128)(2,1)S(1)} %get-tuple-element.25), channel_id=2, replica_groups=mesh['y'=4,'z_hi'=4,'core'=2,'z_lo'=2,'x'=4] {'y'}, dimensions={0}, use_global_device_ids=true | all-gather | bytes 983040 | tf_op jit(solution)/shard_map/all_gather | solution.py:351
  83.9 6.0 %all-gather.1 = bf16[8,1,4,32,384]{4,3,2,1,0:T(8,128)(2,1)S(1)} all-gather(bf16[4,1,4,32,384]{4,3,2,1,0:T(8,128)(2,1)S(1)} %slice.14), channel_id=3, replica_groups=mesh['y'=4,'z_hi'=4,'core'=2,'z_lo'=2,'x'=4] {'core'}, dimensions={0}, use_global_device_ids=true | all-gather | bytes 1179648 | tf_op jit(solution)/shard_map/all_gather | solution.py:352
  90.0 1.4 %shard_map.77 = (bf16[400,384]{1,0:T(8,128)(2,1)S(1)}, bf16[384,384]{1,0:T(8,128)(2,1)S(1)}) custom-call(s32[1]{0:T(128)} %bitcast.core_ref, bf16[448,384]{1,0:T(8,128)(2,1)S(1)} %get-tuple-element.18.refs_2_.refs_11_.q_ref, bf16[4,2,4,32,384]{4,3,2,1,0:T(8,128)(2,1)S(1)} %bitcast.8, bf16[2,4,4,32,384]{4,3,2,1,0:T(8,128)(2,1)S(1)} %bitcast.10, ...), custom_call_target="tpu_custom_call" | custom-call | flops 452984832 | bytes 1179648 | tf_op jit(solution)/shard_map/pallas_call | solution.py:264
  91.4 0.9 shard_map.78
  92.3 1.3 %collective-permute-start.14 = (bf16[384,384]{1,0:T(8,128)(2,1)S(1)}, bf16[384,384]{1,0:T(8,128)(2,1)S(1)}, u32[]{:S(2)}, u32[]{:S(2)}) collective-permute-start(bf16[384,384]{1,0:T(8,128)(2,1)S(1)} %get-tuple-element.30), channel_id=1, source_target_pairs={{0,8},{1,9},{2,10},{3,11},{4,12},{5,13},{6,14},{7,15},{16,24},{17,... | collective-permute-start | bytes 884744 | tf_op jit(solution)/shard_map/ppermute | solution.py:355
  93.6 2.2 %collective-permute-done.14 = bf16[384,384]{1,0:T(8,128)(2,1)S(1)} collective-permute-done((bf16[384,384]{1,0:T(8,128)(2,1)S(1)}, bf16[384,384]{1,0:T(8,128)(2,1)S(1)}, u32[]{:S(2)}, u32[]{:S(2)}) %collective-permute-start.14) | collective-permute-done | bytes 294944 | tf_op jit(solution)/shard_map/ppermute | solution.py:355
  95.9 11.7 %all_to_all.10.in_ref = bf16[16,24,384]{2,1,0:T(8,128)(2,1)S(1)} all-to-all(bf16[16,24,384]{2,1,0:T(8,128)(2,1)S(1)} %bitcast.12), channel_id=1, replica_groups=mesh['y'=4,'z_hi'=4,'core'=2,'z_lo'=2,'x'=4] {'z_lo','x','core'}, dimensions={0} | all-to-all | bytes 589824 | tf_op jit(solution)/shard_map/all_to_all | solution.py:358
  107.5 0.7 shard_map.79
  (24 shorter events, 0.3 us)
Async XLA Ops:
  2.1 7.3 %copy-start.2 = (bf16[2,16,384]{2,1,0:T(8,128)(2,1)S(1)}, bf16[2,16,384]{2,1,0:T(8,128)(2,1)}, u32[]{:S(2)}) copy-start(bf16[2,16,384]{2,1,0:T(8,128)(2,1)} %param.10) | copy-start | bytes 73732
  2.1 21.3 %all-to-all-start = ((bf16[16,24,1152]{2,1,0:T(8,128)(2,1)}), bf16[16,24,1152]{2,1,0:T(8,128)(2,1)S(1)}, u32[]{:S(2)}, u32[]{:S(2)}) async-start(bf16[16,24,1152]{2,1,0:T(8,128)(2,1)} %shard_map.73), calls=%async_computation | async-start | bytes 1769472 | tf_op jit(solution)/shard_map/all_to_all | solution.py:336
  9.5 0.7 copy-start.3
  10.2 1.2 %collective-permute-start = (bf16[4,16,384]{2,1,0:T(8,128)(2,1)S(1)}, bf16[4,16,384]{2,1,0:T(8,128)(2,1)S(1)}, u32[]{:S(2)}, u32[]{:S(2)}) collective-permute-start(bf16[4,16,384]{2,1,0:T(8,128)(2,1)S(1)} %constant_dynamic-update-slice_fusion.own_ref), channel_id=1, source_target_pairs={{0,8},{8,0},{1,9},{9,1},{2,10},{10,2},{3,11},{11,3},{4,12},{12,4},... | collective-permute-start | bytes 147464 | tf_op jit(solution)/shard_map/ppermute | solution.py:334
  23.6 19.0 %collective-permute-start.3 = (bf16[448,384]{1,0:T(8,128)(2,1)S(1)}, bf16[448,384]{1,0:T(8,128)(2,1)S(1)}, u32[]{:S(2)}, u32[]{:S(2)}) collective-permute-start(bf16[448,384]{1,0:T(8,128)(2,1)S(1)} %get-tuple-element.18.refs_2_.refs_11_.q_ref), channel_id=1, source_target_pairs={{0,48},{16,0},{32,16},{48,32},{1,49},{17,1},{33,17},{49,33},{2,50}... | collective-permute-start | bytes 1032200 | tf_op jit(solution)/shard_map/ppermute | solution.py:318
  28.8 8.7 %collective-permute-start.5 = (bf16[384,384]{1,0:T(8,128)(2,1)S(1)}, bf16[384,384]{1,0:T(8,128)(2,1)S(1)}, u32[]{:S(2)}, u32[]{:S(2)}) collective-permute-start(bf16[384,384]{1,0:T(8,128)(2,1)S(1)} %get-tuple-element.19.refs_2_.refs_3_), channel_id=1, source_target_pairs={{0,64},{64,128},{128,192},{192,0},{1,65},{65,129},{129,193},{193,1... | collective-permute-start | bytes 884744 | tf_op jit(solution)/shard_map/ppermute | solution.py:342
  30.1 7.4 %collective-permute-start.9 = (bf16[384,384]{1,0:T(8,128)(2,1)S(1)}, bf16[384,384]{1,0:T(8,128)(2,1)S(1)}, u32[]{:S(2)}, u32[]{:S(2)}) collective-permute-start(bf16[384,384]{1,0:T(8,128)(2,1)S(1)} %get-tuple-element.20.refs_6_.refs_7_), channel_id=1, source_target_pairs={{0,192},{64,0},{128,64},{192,128},{1,193},{65,1},{129,65},{193,129... | collective-permute-start | bytes 884744 | tf_op jit(solution)/shard_map/ppermute | solution.py:343
  31.5 18.2 %collective-permute-start.1 = (bf16[448,384]{1,0:T(8,128)(2,1)S(1)}, bf16[448,384]{1,0:T(8,128)(2,1)S(1)}, u32[]{:S(2)}, u32[]{:S(2)}) collective-permute-start(bf16[448,384]{1,0:T(8,128)(2,1)S(1)} %get-tuple-element.18.refs_2_.refs_11_.q_ref), channel_id=1, source_target_pairs={{0,16},{16,32},{32,48},{48,0},{1,17},{17,33},{33,49},{49,1},{2,18}... | collective-permute-start | bytes 1032200 | tf_op jit(solution)/shard_map/ppermute | solution.py:318
  31.5 19.5 %collective-permute-start.6 = (bf16[384,384]{1,0:T(8,128)(2,1)S(1)}, bf16[384,384]{1,0:T(8,128)(2,1)S(1)}, u32[]{:S(2)}, u32[]{:S(2)}) collective-permute-start(bf16[384,384]{1,0:T(8,128)(2,1)S(1)} %get-tuple-element.19.refs_2_.refs_3_), channel_id=1, source_target_pairs={{0,192},{64,0},{128,64},{192,128},{1,193},{65,1},{129,65},{193,129... | collective-permute-start | bytes 884744 | tf_op jit(solution)/shard_map/ppermute | solution.py:342
  37.5 15.3 %collective-permute-start.8 = (bf16[384,384]{1,0:T(8,128)(2,1)S(1)}, bf16[384,384]{1,0:T(8,128)(2,1)S(1)}, u32[]{:S(2)}, u32[]{:S(2)}) collective-permute-start(bf16[384,384]{1,0:T(8,128)(2,1)S(1)} %get-tuple-element.20.refs_6_.refs_7_), channel_id=1, source_target_pairs={{0,64},{64,128},{128,192},{192,0},{1,65},{65,129},{129,193},{193,1... | collective-permute-start | bytes 884744 | tf_op jit(solution)/shard_map/ppermute | solution.py:343
  37.5 15.3 %collective-permute-start.7 = (bf16[384,384]{1,0:T(8,128)(2,1)S(1)}, bf16[384,384]{1,0:T(8,128)(2,1)S(1)}, u32[]{:S(2)}, u32[]{:S(2)}) collective-permute-start(bf16[384,384]{1,0:T(8,128)(2,1)S(1)} %collective-permute-done.5.refs_3_.refs_4_), channel_id=1, source_target_pairs={{0,64},{64,128},{128,192},{192,0},{1,65},{65,129},{129,193},{193,1... | collective-permute-start | bytes 884744 | tf_op jit(solution)/shard_map/ppermute | solution.py:344
  42.6 10.2 %collective-permute-start.10 = (bf16[384,384]{1,0:T(8,128)(2,1)S(1)}, bf16[384,384]{1,0:T(8,128)(2,1)}, u32[]{:S(2)}, u32[]{:S(2)}) collective-permute-start(bf16[384,384]{1,0:T(8,128)(2,1)S(1)} %collective-permute-done.9.refs_8_.refs_9_), channel_id=1, source_target_pairs={{0,192},{64,0},{128,64},{192,128},{1,193},{65,1},{129,65},{193,129... | collective-permute-start | bytes 884744 | tf_op jit(solution)/shard_map/ppermute | solution.py:345
  49.7 12.2 %collective-permute-start.4 = (bf16[224,384]{1,0:T(8,128)(2,1)S(1)}, bf16[224,384]{1,0:T(8,128)(2,1)S(1)}, u32[]{:S(2)}, u32[]{:S(2)}) collective-permute-start(bf16[224,384]{1,0:T(8,128)(2,1)S(1)} %slice.13), channel_id=1, source_target_pairs={{0,48},{16,0},{32,16},{48,32},{1,49},{17,1},{33,17},{49,33},{2,50}... | collective-permute-start | bytes 516104 | tf_op jit(solution)/shard_map/ppermute | solution.py:322
  51.0 10.8 %collective-permute-start.2 = (bf16[224,384]{1,0:T(8,128)(2,1)}, bf16[224,384]{1,0:T(8,128)(2,1)}, u32[]{:S(2)}, u32[]{:S(2)}) collective-permute-start(bf16[224,384]{1,0:T(8,128)(2,1)} %slice.12), channel_id=1, source_target_pairs={{0,16},{16,32},{32,48},{48,0},{1,17},{17,33},{33,49},{49,1},{2,18}... | collective-permute-start | bytes 516104 | tf_op jit(solution)/shard_map/ppermute | solution.py:321
  52.7 0.7 copy-start
  52.8 0.7 copy-start.1
  59.4 32.0 %collective-permute-start.11 = (bf16[400,384]{1,0:T(8,128)(2,1)S(1)}, bf16[400,384]{1,0:T(8,128)(2,1)S(1)}, u32[]{:S(2)}, u32[]{:S(2)}) collective-permute-start(bf16[400,384]{1,0:T(8,128)(2,1)S(1)} %get-tuple-element.21.refs_16_), channel_id=1, source_target_pairs={{0,48},{16,0},{32,16},{48,32},{1,49},{17,1},{33,17},{49,33},{2,50}... | collective-permute-start | bytes 921608 | tf_op jit(solution)/shard_map/ppermute | solution.py:350
  61.3 30.1 %collective-permute-start.12 = (bf16[400,384]{1,0:T(8,128)(2,1)S(1)}, bf16[400,384]{1,0:T(8,128)(2,1)S(1)}, u32[]{:S(2)}, u32[]{:S(2)}) collective-permute-start(bf16[400,384]{1,0:T(8,128)(2,1)S(1)} %get-tuple-element.22.refs_17_), channel_id=1, source_target_pairs={{0,16},{16,32},{32,48},{48,0},{1,17},{17,33},{33,49},{49,1},{2,18}... | collective-permute-start | bytes 921608 | tf_op jit(solution)/shard_map/ppermute | solution.py:350
  67.8 23.6 %collective-permute-start.13 = (bf16[400,384]{1,0:T(8,128)(2,1)S(1)}, bf16[400,384]{1,0:T(8,128)(2,1)S(1)}, u32[]{:S(2)}, u32[]{:S(2)}) collective-permute-start(bf16[400,384]{1,0:T(8,128)(2,1)S(1)} %get-tuple-element.24), channel_id=1, source_target_pairs={{0,32},{16,48},{32,0},{48,16},{1,33},{17,49},{33,1},{49,17},{2,34}... | collective-permute-start | bytes 921608 | tf_op jit(solution)/shard_map/ppermute | solution.py:350
  92.3 3.5 %collective-permute-start.14 = (bf16[384,384]{1,0:T(8,128)(2,1)S(1)}, bf16[384,384]{1,0:T(8,128)(2,1)S(1)}, u32[]{:S(2)}, u32[]{:S(2)}) collective-permute-start(bf16[384,384]{1,0:T(8,128)(2,1)S(1)} %get-tuple-element.30), channel_id=1, source_target_pairs={{0,8},{1,9},{2,10},{3,11},{4,12},{5,13},{6,14},{7,15},{16,24},{17,... | collective-permute-start | bytes 884744 | tf_op jit(solution)/shard_map/ppermute | solution.py:355
